TPU v7x, 32 devices: a whole 2x2x4 slice. The times are simulated.
32 devices in a mesh: dp: 4 (over y, x), seq: 8 (over z, core).
Axes of the slice: x: 2, y: 2, z: 4, core: 2. Of those that a mesh axis runs over, the one named last changes fastest.
Arguments:
- x_prompt: bfloat16 [8, 2048, 1024], P('dp', 'seq'), may hold values from -6 to 6
- x_cont: bfloat16 [8, 1024, 1024], P('dp', 'seq'), may hold values from -6 to 6
- dy_prompt: bfloat16 [8, 2048, 1024], P('dp', 'seq'), may hold values from -6 to 6
- dy_cont: bfloat16 [8, 1024, 1024], P('dp', 'seq'), may hold values from -6 to 6
- prompt_pos: int32 [8, 2048], P('dp'), may hold values from 0 to 2047, each once within a row
- weights: bfloat16 [15730944], replicated
- master: float32 [15730944], P(('dp', 'seq')), may hold values from -0.015625 to 0.015625
- moment1: float32 [15730944], P(('dp', 'seq')), may hold values from -6 to 6
- moment2: float32 [15730944], P(('dp', 'seq')), may hold values from 0.1 to 10
Outputs:
- y_prompt: float32 [8, 2048, 1024], P('dp', 'seq')
- y_cont: float32 [8, 1024, 1024], P('dp', 'seq')
- dx_prompt: float32 [8, 2048, 1024], P('dp', 'seq')
- dx_cont: float32 [8, 1024, 1024], P('dp', 'seq')
- grad: float32 [15730944], P(('dp', 'seq'))
- master_new: float32 [15730944], P(('dp', 'seq'))
- moment1_new: float32 [15730944], P(('dp', 'seq'))
- weights_new: bfloat16 [15730944], P('dp')
Inputs may be any that keep to these rules, and one draw needn't show every extreme that they name: `prompt_pos`: each row holds every position 0 to 2047 once.
All inputs are finite; a program needn't handle non-finite values.
Results may differ from a plain program's by a relative error of at most 0.017.
Values may be sent and summed in bfloat16 or wider, within the bound.
No kernel may reach another device: no remote copies, remote signals or barrier semaphores. Data moves between devices by JAX's collectives and lax.ppermute only.
A program may use at most 448 MiB of HBM per device.

v0:
```python
import jax
import jax.numpy as jnp
from jax import lax
from jax.sharding import PartitionSpec as P

D = 1024
FF = 3072
HEADS = 16
KV_HEADS = 8
HEAD_DIM = 128


EPS_NORM = 1e-06
ROPE_BASE = 1000000.0
BETA_ONE = 0.9
BETA_TWO = 0.95
ADAM_EPS = 1e-08
LEARN_RATE = 0.0003
DECAY_RATE = 0.1
CORRECT_ONE = 1.0 - 2.656139888758747e-05
CORRECT_TWO = 1.0 - 0.005920529220333996


def swapped(block, axis, apart):
    count = lax.axis_size(axis)
    route = []
    for low in range(count):
        high = low | 1 << apart
        if high != low and high < count:
            route += [(low, high), (high, low)]
    return lax.ppermute(block, axis, route)


def layout():
    q_width = HEADS * HEAD_DIM
    kv_width = KV_HEADS * HEAD_DIM
    return [
        (D,),
        (D, q_width),
        (D, kv_width),
        (D, kv_width),
        (HEAD_DIM,),
        (HEAD_DIM,),
        (q_width, D),
        (D,),
        (D, FF),
        (D, FF),
        (FF, D),
    ]


def unpack(flat_vec):
    pieces = []
    offset = 0
    for shape in layout():
        count = shape[0] if len(shape) == 1 else shape[0] * shape[1]
        pieces.append(lax.slice(flat_vec, (offset,), (offset + count,)).reshape(shape))
        offset += count
    return pieces


def rms_norm(field, gain_vec):
    return field * lax.rsqrt(jnp.mean(field * field, axis=-1, keepdims=True) + EPS_NORM) * gain_vec


def rotate(field, positions):
    half_dim = field.shape[-1] // 2
    frequency = ROPE_BASE ** (-jnp.arange(half_dim, dtype=jnp.float32) * 2.0 / field.shape[-1])
    angles = positions.astype(jnp.float32)[:, None] * frequency[None, :]
    cosine = jnp.cos(angles)[:, None, :]
    sine_part = jnp.sin(angles)[:, None, :]
    front_half = field[..., :half_dim]
    second = field[..., half_dim:]
    return jnp.concatenate(
        [front_half * cosine - second * sine_part, second * cosine + front_half * sine_part],
        axis=-1,
    )


def plain_dot(left, right):
    return jnp.dot(left, right, preferred_element_type=jnp.float32)


def back_dot(left, right):
    return lax.dot_general(
        left, right, (((1,), (1,)), ((), ())), preferred_element_type=jnp.float32
    )


def weight_grad(left, right):
    return lax.dot_general(
        left, right, (((0,), (0,)), ((), ())), preferred_element_type=jnp.float32
    )


def half_positions(prompt_len, quarter, side):
    first_part = prompt_len + side * quarter + jnp.arange(quarter, dtype=jnp.int32)
    second_part = prompt_len + (3 - side) * quarter + jnp.arange(quarter, dtype=jnp.int32)
    return jnp.concatenate([first_part, second_part])


def shards(x_prompt, x_cont, dy_prompt, dy_cont, prompt_pos, weights, master, moment1, moment2):
    pieces = unpack(weights)
    ln_one, w_query, w_key, w_value, gain_q, gain_k, w_out, ln_two, w_gate, w_up, w_down = pieces
    micro_count = x_prompt.shape[0]
    p_rows = x_prompt.shape[1]
    c_rows = x_cont.shape[1]
    row_count = p_rows + c_rows
    seq_count = lax.axis_size("seq")
    seq_rank = lax.axis_index("seq")
    prompt_len = p_rows * seq_count
    parity = seq_rank % 2
    quarter = c_rows // 2
    own_pos = half_positions(prompt_len, quarter, parity)
    other_pos = half_positions(prompt_len, quarter, 1 - parity)
    group_size = HEADS // KV_HEADS
    score_scale = HEAD_DIM ** (-0.5)
    ln_one_f = ln_one.astype(jnp.float32)
    ln_two_f = ln_two.astype(jnp.float32)
    gain_q_f = gain_q.astype(jnp.float32)
    gain_k_f = gain_k.astype(jnp.float32)

    def micro_step(index, carry):
        grads, y_prompt, y_cont, dx_prompt, dx_cont = carry
        x_rows = jnp.concatenate([x_prompt[index], x_cont[index]], axis=0).astype(jnp.float32)
        dy_rows = jnp.concatenate([dy_prompt[index], dy_cont[index]], axis=0)
        group_pos = prompt_pos[index]
        own_prompt_pos = lax.dynamic_slice_in_dim(group_pos, seq_rank * p_rows, p_rows)
        query_pos = jnp.concatenate([own_prompt_pos, own_pos])
        key_pos = jnp.concatenate([group_pos, own_pos, other_pos])
        allowed = key_pos[None, :] <= query_pos[:, None]
        normed, norm_one_back = jax.vjp(rms_norm, x_rows, ln_one_f)
        normed_b = normed.astype(jnp.bfloat16)
        q_raw = plain_dot(normed_b, w_query)
        k_raw = plain_dot(normed_b, w_key)
        v_raw = plain_dot(normed_b, w_value)
        queries, query_back = jax.vjp(
            lambda raw, gain_vec: rotate(
                rms_norm(raw.reshape(row_count, HEADS, HEAD_DIM), gain_vec), query_pos
            ),
            q_raw,
            gain_q_f,
        )
        keys_rot, key_back = jax.vjp(
            lambda raw, gain_vec: rotate(
                rms_norm(raw.reshape(row_count, KV_HEADS, HEAD_DIM), gain_vec), query_pos
            ),
            k_raw,
            gain_k_f,
        )
        q_heads = (
            queries.astype(jnp.bfloat16)
            .reshape(row_count, KV_HEADS, group_size, HEAD_DIM)
            .transpose(1, 0, 2, 3)
        )
        k_heads = keys_rot.astype(jnp.bfloat16).transpose(1, 0, 2)
        v_heads = (
            v_raw.astype(jnp.bfloat16).reshape(row_count, KV_HEADS, HEAD_DIM).transpose(1, 0, 2)
        )
        prompt_kv = (
            lax.all_gather(k_heads[:, :p_rows], "seq", axis=1, tiled=True),
            lax.all_gather(v_heads[:, :p_rows], "seq", axis=1, tiled=True),
        )
        partner = swapped((k_heads[:, p_rows:], v_heads[:, p_rows:]), "seq", 0)
        all_keys = jnp.concatenate([prompt_kv[0], k_heads[:, p_rows:], partner[0]], axis=1)
        all_values = jnp.concatenate([prompt_kv[1], v_heads[:, p_rows:], partner[1]], axis=1)

        def head_forward(head_args):
            q_head, k_head, v_head = head_args
            scores = (
                jnp.einsum("rgd,kd->grk", q_head, k_head, preferred_element_type=jnp.float32)
                * score_scale
            )
            scores = jnp.where(allowed[None], scores, -1e30)
            highest = jnp.max(scores, axis=-1, keepdims=True)
            exponent = jnp.exp(scores - highest)
            total = jnp.sum(exponent, axis=-1, keepdims=True)
            probability = exponent / total
            attended = jnp.einsum(
                "grk,kd->rgd",
                probability.astype(jnp.bfloat16),
                v_head,
                preferred_element_type=jnp.float32,
            )
            return (attended, highest[..., 0] + jnp.log(total[..., 0]))

        attended, log_total = lax.map(head_forward, (q_heads, all_keys, all_values))
        mixed = (
            attended.transpose(1, 0, 2, 3).reshape(row_count, HEADS * HEAD_DIM).astype(jnp.bfloat16)
        )
        resid = x_rows + plain_dot(mixed, w_out)
        normed_two, norm_two_back = jax.vjp(rms_norm, resid, ln_two_f)
        normed_two_b = normed_two.astype(jnp.bfloat16)
        gate_proj = plain_dot(normed_two_b, w_gate)
        up_proj = plain_dot(normed_two_b, w_up)
        hidden, gated_back = jax.vjp(
            lambda gate_in, up_in: jax.nn.silu(gate_in) * up_in, gate_proj, up_proj
        )
        hidden_b = hidden.astype(jnp.bfloat16)
        output = resid + plain_dot(hidden_b, w_down)
        grad_down = weight_grad(hidden_b, dy_rows)
        d_hidden = back_dot(dy_rows, w_down)
        d_gate, d_up = gated_back(d_hidden)
        d_gate_b = d_gate.astype(jnp.bfloat16)
        d_up_b = d_up.astype(jnp.bfloat16)
        grad_gate = weight_grad(normed_two_b, d_gate_b)
        grad_up = weight_grad(normed_two_b, d_up_b)
        d_normed_two = back_dot(d_gate_b, w_gate) + back_dot(d_up_b, w_up)
        d_resid_part, grad_ln_two = norm_two_back(d_normed_two)
        d_resid = dy_rows.astype(jnp.float32) + d_resid_part
        d_attn_b = d_resid.astype(jnp.bfloat16)
        grad_out = weight_grad(mixed, d_attn_b)
        d_mixed = back_dot(d_attn_b, w_out).astype(jnp.bfloat16)
        d_heads = d_mixed.reshape(row_count, KV_HEADS, group_size, HEAD_DIM).transpose(1, 0, 2, 3)

        def head_backward(head_args):
            q_head, k_head, v_head, d_out, head_total = head_args
            scores = (
                jnp.einsum("rgd,kd->grk", q_head, k_head, preferred_element_type=jnp.float32)
                * score_scale
            )
            scores = jnp.where(allowed[None], scores, -1e30)
            probability = jnp.exp(scores - head_total[..., None])
            grad_prob = jnp.einsum("rgd,kd->grk", d_out, v_head, preferred_element_type=jnp.float32)
            row_dot = jnp.sum(probability * grad_prob, axis=-1, keepdims=True)
            grad_score = (probability * (grad_prob - row_dot)).astype(jnp.bfloat16)
            grad_q = (
                jnp.einsum("grk,kd->rgd", grad_score, k_head, preferred_element_type=jnp.float32)
                * score_scale
            )
            grad_k = (
                jnp.einsum("grk,rgd->kd", grad_score, q_head, preferred_element_type=jnp.float32)
                * score_scale
            )
            grad_v = jnp.einsum(
                "grk,rgd->kd",
                probability.astype(jnp.bfloat16),
                d_out,
                preferred_element_type=jnp.float32,
            )
            return (grad_q, grad_k, grad_v)

        grad_q_heads, grad_k_heads, grad_v_heads = lax.map(
            head_backward, (q_heads, all_keys, all_values, d_heads, log_total)
        )
        split_at = prompt_len + c_rows
        returned = (
            swapped(grad_k_heads[:, split_at:].astype(jnp.bfloat16), "seq", 0).astype(jnp.float32),
            swapped(grad_v_heads[:, split_at:].astype(jnp.bfloat16), "seq", 0).astype(jnp.float32),
        )
        owned = (
            lax.psum_scatter(grad_k_heads[:, :prompt_len], "seq", scatter_dimension=1, tiled=True),
            lax.psum_scatter(grad_v_heads[:, :prompt_len], "seq", scatter_dimension=1, tiled=True),
        )
        d_key = jnp.concatenate(
            [owned[0], grad_k_heads[:, prompt_len:split_at] + returned[0]], axis=1
        ).transpose(1, 0, 2)
        d_value = jnp.concatenate(
            [owned[1], grad_v_heads[:, prompt_len:split_at] + returned[1]], axis=1
        ).transpose(1, 0, 2)
        d_query = grad_q_heads.transpose(1, 0, 2, 3).reshape(row_count, HEADS, HEAD_DIM)
        d_q_raw, grad_gain_q = query_back(d_query)
        d_k_raw, grad_gain_k = key_back(d_key)
        d_q_b = d_q_raw.astype(jnp.bfloat16)
        d_k_b = d_k_raw.astype(jnp.bfloat16)
        d_v_b = d_value.reshape(row_count, KV_HEADS * HEAD_DIM).astype(jnp.bfloat16)
        grad_query = weight_grad(normed_b, d_q_b)
        grad_key = weight_grad(normed_b, d_k_b)
        grad_value = weight_grad(normed_b, d_v_b)
        d_normed = back_dot(d_q_b, w_query) + back_dot(d_k_b, w_key) + back_dot(d_v_b, w_value)
        d_x_part, grad_ln_one = norm_one_back(d_normed)
        d_x = d_resid + d_x_part
        fresh = [
            grad_ln_one,
            grad_query,
            grad_key,
            grad_value,
            grad_gain_q,
            grad_gain_k,
            grad_out,
            grad_ln_two,
            grad_gate,
            grad_up,
            grad_down,
        ]
        grads = tuple((old + new for old, new in zip(grads, fresh)))
        y_prompt = y_prompt.at[index].set(output[:p_rows])
        y_cont = y_cont.at[index].set(output[p_rows:])
        dx_prompt = dx_prompt.at[index].set(d_x[:p_rows])
        dx_cont = dx_cont.at[index].set(d_x[p_rows:])
        return (grads, y_prompt, y_cont, dx_prompt, dx_cont)

    start_grads = tuple((jnp.zeros(shape, jnp.float32) for shape in layout()))
    start = (
        start_grads,
        jnp.zeros(x_prompt.shape, jnp.float32),
        jnp.zeros(x_cont.shape, jnp.float32),
        jnp.zeros(x_prompt.shape, jnp.float32),
        jnp.zeros(x_cont.shape, jnp.float32),
    )
    grads, y_prompt, y_cont, dx_prompt, dx_cont = lax.fori_loop(0, micro_count, micro_step, start)
    flat_grad = jnp.concatenate([piece.reshape(-1) for piece in grads])
    grad_shard = lax.psum_scatter(flat_grad, ("dp", "seq"), scatter_dimension=0, tiled=True)
    moment1_new = BETA_ONE * moment1 + (1.0 - BETA_ONE) * grad_shard
    moment2_new = BETA_TWO * moment2 + (1.0 - BETA_TWO) * grad_shard * grad_shard
    update = moment1_new / CORRECT_ONE / (jnp.sqrt(moment2_new / CORRECT_TWO) + ADAM_EPS)
    master_new = master - LEARN_RATE * (update + DECAY_RATE * master)
    weights_new = lax.all_gather(master_new.astype(jnp.bfloat16), "seq", axis=0, tiled=True)
    return (y_prompt, y_cont, dx_prompt, dx_cont, grad_shard, master_new, moment1_new, weights_new)


def solution(mesh):
    placed = (
        P("dp", "seq", None),
        P("dp", "seq", None),
        P("dp", "seq", None),
        P("dp", "seq", None),
        P("dp", None),
        P(),
        P(("dp", "seq")),
        P(("dp", "seq")),
        P(("dp", "seq")),
    )
    return jax.shard_map(
        shards,
        mesh=mesh,
        in_specs=placed,
        out_specs=(
            P("dp", "seq", None),
            P("dp", "seq", None),
            P("dp", "seq", None),
            P("dp", "seq", None),
            P(("dp", "seq")),
            P(("dp", "seq")),
            P(("dp", "seq")),
            P("dp"),
        ),
        check_vma=False,
    )
```

profile of v0, /device:TPU:0, one launch (start us, length us, event | category | flops | bytes accessed | tf_op | source)
XLA Modules:
  0.0 2915.2 jit_solution(9244670604746523828)
XLA Ops:
  8.0 14.3 fusion.106
  34.1 10.3 reshape.637
  44.4 10.3 reshape.639
  54.7 10.3 reshape.640
  65.0 7.3 reshape.634
  72.3 7.3 reshape.638
  91.5 1246.0 %while.158 = (s32[]{:T(128)}, f32[1024]{0:T(1024)}, f32[1024,2048]{1,0:T(8,128)}, f32[1024,1024]{1,0:T(8,128)}, f32[1024,1024]{1,0:T(8,128)}, /*index=5*/f32[128...) while((s32[]{:T(128)}, f32[1024]{0:T(1024)}, ...), condition=%wide.region_23.24_spmd.clone.clone, body=%wide.region_0.23_spmd.clone.sunk.clone | while | flops 39603556352 | bytes 1338580480 | solution.py:301
  127.7 8.9 fusion.347
  138.9 16.4 all-gather.5.cloned.1.call-done
  167.0 35.4 %all-gather.3.cloned.1.call-done = bf16[8,2048,128]{2,1,0:T(8,128)(2,1)} async-done(((bf16[8,256,128]{2,1,0:T(8,128)(2,1)}), bf16[8,2048,128]{2,1,0:T(8,128)(2,1)}) %all-gather.3.cloned.1.call-update) | async-done | bytes 4194320 | tf_op jit(solution)/shard_map/while/body/eval_jaxpr/all_gather | solution.py:162
  209.0 58.1 %while.156 = (s32[]{:T(128)}, bf16[8,384,2,128]{1,3,2,0:T(8,128)(2,1)S(1)}, f32[8,2,384]{2,1,0:T(2,128)S(1)}, bf16[8,2304,128]{2,1,0:T(8,128)(2,1)}, bf16[8,2304...) while((s32[]{:T(128)}, ...), condition=%wide.region_7.7_spmd.clone, body=%wide.region_4.6_spmd.clone.sunk | while | flops 921009408 | bytes 24810080 | solution.py:187
  277.9 7.4 multiply_convert_fusion.8
  298.0 209.6 %while.157 = (s32[]{:T(128)}, f32[8,384,2,128]{1,3,2,0:T(8,128)}, f32[8,2304,128]{1,2,0:T(8,128)}, f32[8,2304,128]{1,2,0:T(8,128)}, bf16[8,2304,128]{2,1,0:T(8,1...) while((s32[]{:T(128)}, f32[8,384,2,128]{1,3,2,0:T(8,128)}, ...), condition=%wide.region_12.12_spmd.clone, body=%wide.region_10.11_spmd.clone.sunk | while | flops 2282126592 | bytes 119962352 | solution.py:243
  507.6 7.8 slice.510
  515.5 7.8 slice.508
  561.7 9.6 convolution_add_fusion.4
  571.4 7.9 select_add_fusion.30
  579.3 9.0 select_add_fusion.31
  588.4 12.4 select_add_fusion.32
  613.1 81.0 %reduce-scatter.3.cloned.1.call-done = f32[8,256,128]{1,2,0:T(8,128)} async-done(((f32[8,2048,128]{1,2,0:T(8,128)}), f32[8,256,128]{1,2,0:T(8,128)}) %reduce-scatter.3.cloned.1.call-update) | async-done | bytes 1048592 | tf_op jit(solution)/shard_map/while/body/eval_jaxpr/reduce_scatter | solution.py:253
  748.4 9.0 fusion.347
  759.6 12.0 all-gather.5.cloned.1.call-done
  776.6 6.7 copy.255
  783.2 35.3 %all-gather.3.cloned.1.call-done = bf16[8,2048,128]{2,1,0:T(8,128)(2,1)} async-done(((bf16[8,256,128]{2,1,0:T(8,128)(2,1)}), bf16[8,2048,128]{2,1,0:T(8,128)(2,1)}) %all-gather.3.cloned.1.call-update) | async-done | bytes 4194320 | tf_op jit(solution)/shard_map/while/body/eval_jaxpr/all_gather | solution.py:162
  825.1 58.3 %while.156 = (s32[]{:T(128)}, bf16[8,384,2,128]{1,3,2,0:T(8,128)(2,1)S(1)}, f32[8,2,384]{2,1,0:T(2,128)S(1)}, bf16[8,2304,128]{2,1,0:T(8,128)(2,1)}, bf16[8,2304...) while((s32[]{:T(128)}, ...), condition=%wide.region_7.7_spmd.clone, body=%wide.region_4.6_spmd.clone.sunk | while | flops 921009408 | bytes 24810080 | solution.py:187
  894.2 7.4 multiply_convert_fusion.8
  914.1 209.5 %while.157 = (s32[]{:T(128)}, f32[8,384,2,128]{1,3,2,0:T(8,128)}, f32[8,2304,128]{1,2,0:T(8,128)}, f32[8,2304,128]{1,2,0:T(8,128)}, bf16[8,2304,128]{2,1,0:T(8,1...) while((s32[]{:T(128)}, f32[8,384,2,128]{1,3,2,0:T(8,128)}, ...), condition=%wide.region_12.12_spmd.clone, body=%wide.region_10.11_spmd.clone.sunk | while | flops 2282126592 | bytes 119962352 | solution.py:243
  1123.7 7.8 slice.510
  1131.6 7.8 slice.508
  1167.4 9.8 select_add_fusion.26
  1181.1 9.7 convolution_add_fusion.4
  1190.8 8.1 select_add_fusion.30
  1198.9 9.0 select_add_fusion.31
  1208.0 18.3 select_add_fusion.32
  1238.3 72.1 %reduce-scatter.3.cloned.1.call-done = f32[8,256,128]{1,2,0:T(8,128)} async-done(((f32[8,2048,128]{1,2,0:T(8,128)}), f32[8,256,128]{1,2,0:T(8,128)}) %reduce-scatter.3.cloned.1.call-update) | async-done | bytes 1048592 | tf_op jit(solution)/shard_map/while/body/eval_jaxpr/reduce_scatter | solution.py:253
  1338.9 8.8 copy.190
  1359.3 12.1 copy.194
  1371.4 12.3 copy.195
  1383.7 12.3 copy.196
  1410.6 71.8 %dynamic-update-slice.51 = f32[15730944]{0:T(1024)} dynamic-update-slice(f32[15730944]{0:T(1024)} %constant_dynamic-update-slice_fusion.2, f32[2097152]{0:T(1024)} %bitcast.477, s32[]{} %constant.521) | dynamic-update-slice | bytes 16777220
  1483.7 106.8 %dynamic-update-slice.53 = f32[15730944]{0:T(1024)} dynamic-update-slice(f32[15730944]{0:T(1024)} %constant_dynamic-update-slice_fusion.1, f32[3145728]{0:T(1024)} %bitcast.476, s32[]{} %constant.523) | dynamic-update-slice | bytes 25165828
  1590.5 106.8 %dynamic-update-slice.54 = f32[15730944]{0:T(1024)} dynamic-update-slice(f32[15730944]{0:T(1024)} %dynamic-update-slice.53, f32[3145728]{0:T(1024)} %bitcast.475, s32[]{} %constant.524) | dynamic-update-slice | bytes 25165828
  1697.3 106.6 %dynamic-update-slice.55 = f32[15730944]{0:T(1024)} dynamic-update-slice(f32[15730944]{0:T(1024)} %dynamic-update-slice.54, f32[3145728]{0:T(1024)} %bitcast.474, s32[]{} %constant.525) | dynamic-update-slice | bytes 25165828 | tf_op jit(solution)/shard_map/concatenate | solution.py:302
  1805.8 902.9 %all-reduce.11.cloned.1.call-done = f32[15730944]{0:T(1024)} async-done(((f32[15730944]{0:T(1024)}), f32[15730944]{0:T(1024)}) %all-reduce.11.cloned.1.call-update) | async-done | bytes 62923792
  2708.7 7.1 fusion.103
  2719.2 16.1 dynamic-update-slice.44
  2735.4 165.4 %all-reduce.9.cloned.1.call-done = bf16[3932736]{0:T(1024)(128)(2,1)} async-done(((bf16[3932736]{0:T(1024)(128)(2,1)}), bf16[3932736]{0:T(1024)(128)(2,1)}) %all-reduce.9.cloned.1.call-update) | async-done | bytes 7865488
  2900.7 6.8 copy.360
  (1064 shorter events, 871.4 us)
Async XLA Ops:
  92.1 19.9 copy-start.71
  92.1 28.3 copy-start.88
  92.1 35.4 %copy-start.91 = (s32[128]{0:T(128)}, s32[128]{0:T(128)S(1)}, u32[]{:S(2)}) copy-start(s32[128]{0:T(128)S(1)} %get-tuple-element.2333) | copy-start | bytes 1540 | tf_op jit(solution)/shard_map/while
  92.1 199.4 %copy-start.79 = (f32[1024]{0:T(1024)}, f32[1024]{0:T(1024)S(1)}, u32[]{:S(2)}) copy-start(f32[1024]{0:T(1024)S(1)} %get-tuple-element.2341) | copy-start | bytes 12292 | tf_op jit(solution)/shard_map/while
  92.1 63.2 %all-gather.5.cloned.1.call-start = ((), (), s32[]{:S(2)}) async-start(), calls=%async_computation.5 | async-start | bytes 4718592 | tf_op jit(solution)/shard_map/while/body/eval_jaxpr/all_gather | solution.py:161
  93.2 18.7 copy-start.9
  94.4 172.7 %copy-start.21 = (bf16[128,1024]{1,0:T(8,128)(2,1)}, bf16[128,1024]{1,0:T(8,128)(2,1)S(1)}, u32[]{:S(2)}) copy-start(bf16[128,1024]{1,0:T(8,128)(2,1)S(1)} %dynamic-slice_bitcast_fusion.15) | copy-start | bytes 786436 | tf_op jit(solution)/shard_map/while
  104.6 97.8 %all-gather.3.cloned.1.call-start = ((), (), s32[]{:S(2)}) async-start(), calls=%async_computation.4 | async-start | bytes 4718592 | tf_op jit(solution)/shard_map/while/body/eval_jaxpr/all_gather | solution.py:162
  108.3 498.0 %reduce-scatter.5.cloned.1.call-start = ((), (), s32[]{:S(2)}) async-start(), calls=%async_computation.7 | async-start | bytes 9437184 | tf_op jit(solution)/shard_map/while/body/eval_jaxpr/reduce_scatter | solution.py:252
  109.1 29.7 %collective-permute-start.1 = (bf16[8,128,128]{1,2,0:T(8,128)(2,1)}, bf16[8,128,128]{1,2,0:T(8,128)(2,1)}, u32[]{:S(2)}, u32[]{:S(2)}) collective-permute-start(bf16[8,128,128]{1,2,0:T(8,128)(2,1)} %slice.505), channel_id=1, source_target_pairs={{0,1},{1,0},{2,3},{3,2},{4,5},{5,4},{6,7},{7,6},{8,9},{9,8},{10,11... | collective-permute-start | bytes 786440 | tf_op jit(solution)/shard_map/while/body/eval_jaxpr/ppermute | solution.py:31
  110.3 56.7 %collective-permute-start = (bf16[8,128,128]{2,1,0:T(8,128)(2,1)}, bf16[8,128,128]{2,1,0:T(8,128)(2,1)}, u32[]{:S(2)}, u32[]{:S(2)}) collective-permute-start(bf16[8,128,128]{2,1,0:T(8,128)(2,1)} %slice.503), channel_id=1, source_target_pairs={{0,1},{1,0},{2,3},{3,2},{4,5},{5,4},{6,7},{7,6},{8,9},{9,8},{10,11... | collective-permute-start | bytes 786440 | tf_op jit(solution)/shard_map/while/body/eval_jaxpr/ppermute | solution.py:31
  127.6 163.9 %copy-start.44 = (bf16[128,1024]{1,0:T(8,128)(2,1)}, bf16[128,1024]{1,0:T(8,128)(2,1)S(1)}, u32[]{:S(2)}) copy-start(bf16[128,1024]{1,0:T(8,128)(2,1)S(1)} %dynamic-slice_bitcast_fusion.17) | copy-start | bytes 786436 | tf_op jit(solution)/shard_map/while
  127.7 163.9 %copy-start.41 = (bf16[256,1024]{1,0:T(8,128)(2,1)}, bf16[256,1024]{1,0:T(8,128)(2,1)S(1)}, u32[]{:S(2)}) copy-start(bf16[256,1024]{1,0:T(8,128)(2,1)S(1)} %dynamic-slice_bitcast_fusion.18) | copy-start | bytes 1572868 | tf_op jit(solution)/shard_map/while
  209.0 58.2 %copy-start.10 = (bf16[256,1024]{1,0:T(8,128)(2,1)S(1)}, bf16[256,1024]{1,0:T(8,128)(2,1)}, u32[]{:S(2)}) copy-start(bf16[256,1024]{1,0:T(8,128)(2,1)} %copy-done.9) | copy-start | bytes 1572868 | tf_op jit(solution)/shard_map/while
  271.9 19.6 copy-start.30
  515.4 178.7 %reduce-scatter.3.cloned.1.call-start = ((), (), s32[]{:S(2)}) async-start(), calls=%async_computation.6 | async-start | bytes 9437184 | tf_op jit(solution)/shard_map/while/body/eval_jaxpr/reduce_scatter | solution.py:253
  528.2 76.8 %collective-permute-start.3 = (bf16[8,128,128]{1,2,0:T(8,128)(2,1)}, bf16[8,128,128]{1,2,0:T(8,128)(2,1)}, u32[]{:S(2)}, u32[]{:S(2)}) collective-permute-start(bf16[8,128,128]{1,2,0:T(8,128)(2,1)} %slice.509), channel_id=1, source_target_pairs={{0,1},{1,0},{2,3},{3,2},{4,5},{5,4},{6,7},{7,6},{8,9},{9,8},{10,11... | collective-permute-start | bytes 786440 | tf_op jit(solution)/shard_map/while/body/eval_jaxpr/ppermute | solution.py:31
  545.6 58.2 %collective-permute-start.2 = (bf16[8,128,128]{1,2,0:T(8,128)(2,1)}, bf16[8,128,128]{1,2,0:T(8,128)(2,1)}, u32[]{:S(2)}, u32[]{:S(2)}) collective-permute-start(bf16[8,128,128]{1,2,0:T(8,128)(2,1)} %slice.507), channel_id=1, source_target_pairs={{0,1},{1,0},{2,3},{3,2},{4,5},{5,4},{6,7},{7,6},{8,9},{9,8},{10,11... | collective-permute-start | bytes 786440 | tf_op jit(solution)/shard_map/while/body/eval_jaxpr/ppermute | solution.py:31
  613.1 82.6 %copy-start.12 = (bf16[256,1024]{1,0:T(8,128)(2,1)S(1)}, bf16[256,1024]{1,0:T(8,128)(2,1)}, u32[]{:S(2)}) copy-start(bf16[256,1024]{1,0:T(8,128)(2,1)} %copy-done.9) | copy-start | bytes 1572868 | tf_op jit(solution)/shard_map/while
  613.1 82.6 %copy-start.23 = (bf16[128,1024]{1,0:T(8,128)(2,1)S(1)}, bf16[128,1024]{1,0:T(8,128)(2,1)}, u32[]{:S(2)}) copy-start(bf16[128,1024]{1,0:T(8,128)(2,1)} %copy-done.21) | copy-start | bytes 786436 | tf_op jit(solution)/shard_map/while
  613.1 82.6 %copy-start.72 = (f32[1024]{0:T(1024)S(1)}, f32[1024]{0:T(1024)}, u32[]{:S(2)}) copy-start(f32[1024]{0:T(1024)} %copy-done.71) | copy-start | bytes 12292 | tf_op jit(solution)/shard_map/while
  712.7 19.9 copy-start.71
  712.7 28.3 copy-start.88
  712.7 35.5 %copy-start.91 = (s32[128]{0:T(128)}, s32[128]{0:T(128)S(1)}, u32[]{:S(2)}) copy-start(s32[128]{0:T(128)S(1)} %get-tuple-element.2333) | copy-start | bytes 1540 | tf_op jit(solution)/shard_map/while
  712.7 195.1 %copy-start.79 = (f32[1024]{0:T(1024)}, f32[1024]{0:T(1024)S(1)}, u32[]{:S(2)}) copy-start(f32[1024]{0:T(1024)S(1)} %get-tuple-element.2341) | copy-start | bytes 12292 | tf_op jit(solution)/shard_map/while
  712.7 58.9 %all-gather.5.cloned.1.call-start = ((), (), s32[]{:S(2)}) async-start(), calls=%async_computation.5 | async-start | bytes 4718592 | tf_op jit(solution)/shard_map/while/body/eval_jaxpr/all_gather | solution.py:161
  713.9 18.7 copy-start.9
  715.0 168.4 %copy-start.21 = (bf16[128,1024]{1,0:T(8,128)(2,1)}, bf16[128,1024]{1,0:T(8,128)(2,1)S(1)}, u32[]{:S(2)}) copy-start(bf16[128,1024]{1,0:T(8,128)(2,1)S(1)} %dynamic-slice_bitcast_fusion.15) | copy-start | bytes 786436 | tf_op jit(solution)/shard_map/while
  725.3 93.3 %all-gather.3.cloned.1.call-start = ((), (), s32[]{:S(2)}) async-start(), calls=%async_computation.4 | async-start | bytes 4718592 | tf_op jit(solution)/shard_map/while/body/eval_jaxpr/all_gather | solution.py:162
  728.9 502.8 %reduce-scatter.5.cloned.1.call-start = ((), (), s32[]{:S(2)}) async-start(), calls=%async_computation.7 | async-start | bytes 9437184 | tf_op jit(solution)/shard_map/while/body/eval_jaxpr/reduce_scatter | solution.py:252
  729.7 29.9 %collective-permute-start.1 = (bf16[8,128,128]{1,2,0:T(8,128)(2,1)}, bf16[8,128,128]{1,2,0:T(8,128)(2,1)}, u32[]{:S(2)}, u32[]{:S(2)}) collective-permute-start(bf16[8,128,128]{1,2,0:T(8,128)(2,1)} %slice.505), channel_id=1, source_target_pairs={{0,1},{1,0},{2,3},{3,2},{4,5},{5,4},{6,7},{7,6},{8,9},{9,8},{10,11... | collective-permute-start | bytes 786440 | tf_op jit(solution)/shard_map/while/body/eval_jaxpr/ppermute | solution.py:31
  730.5 52.8 %collective-permute-start = (bf16[8,128,128]{2,1,0:T(8,128)(2,1)}, bf16[8,128,128]{2,1,0:T(8,128)(2,1)}, u32[]{:S(2)}, u32[]{:S(2)}) collective-permute-start(bf16[8,128,128]{2,1,0:T(8,128)(2,1)} %slice.503), channel_id=1, source_target_pairs={{0,1},{1,0},{2,3},{3,2},{4,5},{5,4},{6,7},{7,6},{8,9},{9,8},{10,11... | collective-permute-start | bytes 786440 | tf_op jit(solution)/shard_map/while/body/eval_jaxpr/ppermute | solution.py:31
  748.3 159.5 %copy-start.44 = (bf16[128,1024]{1,0:T(8,128)(2,1)}, bf16[128,1024]{1,0:T(8,128)(2,1)S(1)}, u32[]{:S(2)}) copy-start(bf16[128,1024]{1,0:T(8,128)(2,1)S(1)} %dynamic-slice_bitcast_fusion.17) | copy-start | bytes 786436 | tf_op jit(solution)/shard_map/while
  748.3 159.5 %copy-start.41 = (bf16[256,1024]{1,0:T(8,128)(2,1)}, bf16[256,1024]{1,0:T(8,128)(2,1)S(1)}, u32[]{:S(2)}) copy-start(bf16[256,1024]{1,0:T(8,128)(2,1)S(1)} %dynamic-slice_bitcast_fusion.18) | copy-start | bytes 1572868 | tf_op jit(solution)/shard_map/while
  825.1 58.4 %copy-start.10 = (bf16[256,1024]{1,0:T(8,128)(2,1)S(1)}, bf16[256,1024]{1,0:T(8,128)(2,1)}, u32[]{:S(2)}) copy-start(bf16[256,1024]{1,0:T(8,128)(2,1)} %copy-done.9) | copy-start | bytes 1572868 | tf_op jit(solution)/shard_map/while
  888.2 19.6 copy-start.30
  1131.5 178.9 %reduce-scatter.3.cloned.1.call-start = ((), (), s32[]{:S(2)}) async-start(), calls=%async_computation.6 | async-start | bytes 9437184 | tf_op jit(solution)/shard_map/while/body/eval_jaxpr/reduce_scatter | solution.py:253
  1144.3 86.2 %collective-permute-start.3 = (bf16[8,128,128]{1,2,0:T(8,128)(2,1)}, bf16[8,128,128]{1,2,0:T(8,128)(2,1)}, u32[]{:S(2)}, u32[]{:S(2)}) collective-permute-start(bf16[8,128,128]{1,2,0:T(8,128)(2,1)} %slice.509), channel_id=1, source_target_pairs={{0,1},{1,0},{2,3},{3,2},{4,5},{5,4},{6,7},{7,6},{8,9},{9,8},{10,11... | collective-permute-start | bytes 786440 | tf_op jit(solution)/shard_map/while/body/eval_jaxpr/ppermute | solution.py:31
  1161.7 67.5 %collective-permute-start.2 = (bf16[8,128,128]{1,2,0:T(8,128)(2,1)}, bf16[8,128,128]{1,2,0:T(8,128)(2,1)}, u32[]{:S(2)}, u32[]{:S(2)}) collective-permute-start(bf16[8,128,128]{1,2,0:T(8,128)(2,1)} %slice.507), channel_id=1, source_target_pairs={{0,1},{1,0},{2,3},{3,2},{4,5},{5,4},{6,7},{7,6},{8,9},{9,8},{10,11... | collective-permute-start | bytes 786440 | tf_op jit(solution)/shard_map/while/body/eval_jaxpr/ppermute | solution.py:31
  1208.0 18.3 copy-start.8
  1208.0 18.3 copy-start.33
  1238.3 73.6 %copy-start.12 = (bf16[256,1024]{1,0:T(8,128)(2,1)S(1)}, bf16[256,1024]{1,0:T(8,128)(2,1)}, u32[]{:S(2)}) copy-start(bf16[256,1024]{1,0:T(8,128)(2,1)} %copy-done.9) | copy-start | bytes 1572868 | tf_op jit(solution)/shard_map/while
  1238.3 73.6 %copy-start.23 = (bf16[128,1024]{1,0:T(8,128)(2,1)S(1)}, bf16[128,1024]{1,0:T(8,128)(2,1)}, u32[]{:S(2)}) copy-start(bf16[128,1024]{1,0:T(8,128)(2,1)} %copy-done.21) | copy-start | bytes 786436 | tf_op jit(solution)/shard_map/while
  1238.3 73.6 %copy-start.72 = (f32[1024]{0:T(1024)S(1)}, f32[1024]{0:T(1024)}, u32[]{:S(2)}) copy-start(f32[1024]{0:T(1024)} %copy-done.71) | copy-start | bytes 12292 | tf_op jit(solution)/shard_map/while
  1337.6 1371.2 %all-reduce.11.cloned.1.call-start = ((), (), s32[]{:S(2)}) async-start(), calls=%async_computation.3 | async-start | bytes 125853696
  1410.6 71.8 %copy-start.87 = (f32[1024]{0:T(1024)S(1)}, f32[1024]{0:T(1024)}, u32[]{:S(2)}) copy-start(f32[1024]{0:T(1024)} %get-tuple-element.1127) | copy-start | bytes 12292
  1803.9 904.8 %copy-start.76 = (f32[491592]{0:T(1024)S(1)}, f32[491592]{0:T(1024)}, u32[]{:S(2)}) copy-start(f32[491592]{0:T(1024)} %param.29) | copy-start | bytes 5899108
  1804.0 1096.8 %all-reduce.9.cloned.1.call-start = ((), (), s32[]{:S(2)}) async-start(), calls=%async_computation.2 | async-start | bytes 15732736
  (246 other events, 1171.1 us)
Sparse Core Ops, SparseCore 0:
  104.8 50.4 all-gather.4
  157.0 45.3 all-gather.2
  515.6 88.3 reduce-scatter.4
  606.2 87.9 reduce-scatter.2
  725.4 46.1 all-gather.4
  773.1 45.3 all-gather.2
  1131.6 88.3 reduce-scatter.4
  1222.4 87.9 reduce-scatter.2
Sparse Core Ops, SparseCore 1:
  1804.0 904.6 all-reduce.10
  2735.4 165.2 all-reduce.8
where the time goes:
time: 2950 us; the launch traced here: 2920 us
  waiting for transfers between devices  1320 us (45%)
  local copies, waits for them, and re-layouts  758 us (26%)
  matrix products  597 us (20%)
  other arithmetic  206 us (7%)
    unnamed x4, waiting for transfers between devices  1070 us
    unnamed x41, local copies, waits for them, and re-layouts  387 us
    reduce_scatter x2, waiting for transfers between devices, micro_step(): lax.psum_scatter(grad_v_heads[:, :prompt_len], 'seq', scatter_dimension=1...  153 us
    concatenate x1, local copies, waits for them, and re-layouts, shards(): flat_grad = jnp.concatenate([piece.reshape(-1) for piece in grads])  107 us
    dot_general x14, matrix products, weight_grad(): lax.dot_general(left, right, (((0,), (0,)), ((), ())), preferred_element_...  97.9 us
    dot_general x16, matrix products, head_backward(): jnp.einsum('grk,rgd->kd', probability.astype(jnp.bfloat16), d_out, prefer...  88.2 us
    dot_general x14, matrix products, plain_dot(): return jnp.dot(left, right, preferred_element_type=jnp.float32)  73.6 us
    all_gather x2, waiting for transfers between devices, micro_step(): lax.all_gather(v_heads[:, :p_rows], 'seq', axis=1, tiled=True)  70.7 us
  transfers between devices with their start and end apart: 18, of which 8 were waited for; matrix products, arithmetic and copies ran while one was open for 10% of the time, Pallas kernels for 0%

commit v1 on v0

v1 whole, which is shorter than its diff:
```python
import functools

import jax
import jax.numpy as jnp
from jax import lax
from jax.experimental import pallas as pl
from jax.experimental.pallas import tpu as pltpu
from jax.sharding import PartitionSpec as P

D = 1024
FF = 3072
HEADS = 16
KV_HEADS = 8
HEAD_DIM = 128

EPS_NORM = 1e-06
ROPE_BASE = 1000000.0
BETA_ONE = 0.9
BETA_TWO = 0.95
ADAM_EPS = 1e-08
LEARN_RATE = 0.0003
DECAY_RATE = 0.1
CORRECT_ONE = 1.0 - 2.656139888758747e-05
CORRECT_TWO = 1.0 - 0.005920529220333996

CORES = 2
Q_HEADS_C = HEADS // CORES
KV_HEADS_C = KV_HEADS // CORES
QW = Q_HEADS_C * HEAD_DIM
KW = KV_HEADS_C * HEAD_DIM
FW = FF // CORES
GROUP = HEADS // KV_HEADS
LOG2E = 1.4426950408889634
SCORE_FOLD = HEAD_DIM ** (-0.5) * LOG2E
VMEM_LIMIT = 52 * 1024 * 1024
BF = jnp.bfloat16
F32 = jnp.float32


def dot(left, right):
    return jnp.dot(left, right, preferred_element_type=F32)


def dot_t(left, right):
    return lax.dot_general(left, right, (((1,), (1,)), ((), ())), preferred_element_type=F32)


def t_dot(left, right):
    return lax.dot_general(left, right, (((0,), (0,)), ((), ())), preferred_element_type=F32)


def xor_seq(block, mask):
    count = lax.axis_size("seq")
    return lax.ppermute(block, "seq", [(i, i ^ mask) for i in range(count)])


def params(*semantics):
    return pltpu.CompilerParams(vmem_limit_bytes=VMEM_LIMIT)


def whole(shape):
    return pl.BlockSpec(shape, lambda *ids: (0,) * len(shape))


def head_norm_rot(raw, gain, cos, sin):
    r = lax.rsqrt(jnp.mean(raw * raw, axis=-1, keepdims=True) + EPS_NORM)
    n = raw * r * gain
    return n * cos + pltpu.roll(n, HEAD_DIM // 2, 1) * sin


def head_norm_rot_back(raw, gain, cos, sin, grad):
    dn = grad * cos - pltpu.roll(grad, HEAD_DIM // 2, 1) * sin
    r = lax.rsqrt(jnp.mean(raw * raw, axis=-1, keepdims=True) + EPS_NORM)
    xh = raw * r
    gain_rows = dn * xh
    dg = dn * gain
    return r * (dg - xh * jnp.mean(dg * xh, axis=-1, keepdims=True)), gain_rows


def project_kernel(with_q, *refs):
    if with_q:
        (x, g1, cos, sin, wq, wkv, gq, gk, a_out, q_out, qraw_out, k_out, kraw_out, v_out) = refs
    else:
        (x, g1, cos, sin, wkv, gk, a_out, k_out, kraw_out, v_out) = refs
    xv = x[...].astype(F32)
    a = xv * lax.rsqrt(jnp.mean(xv * xv, axis=-1, keepdims=True) + EPS_NORM) * g1[...]
    a = a.astype(BF)
    a_out[...] = a
    cosv, sinv = cos[...], sin[...]
    kv = dot(a, wkv[...])
    for head in range(KV_HEADS_C):
        cols = slice(head * HEAD_DIM, (head + 1) * HEAD_DIM)
        raw = kv[:, cols]
        kraw_out[:, cols] = raw.astype(BF)
        k_out[:, cols] = head_norm_rot(raw, gk[...], cosv, sinv).astype(BF)
    v_out[...] = kv[:, KW:].astype(BF)
    if with_q:
        qv = dot(a, wq[...])
        for head in range(Q_HEADS_C):
            cols = slice(head * HEAD_DIM, (head + 1) * HEAD_DIM)
            raw = qv[:, cols]
            qraw_out[:, cols] = raw.astype(BF)
            rot = head_norm_rot(raw, gq[...], cosv, sinv)
            q_out[:, cols] = (rot * SCORE_FOLD).astype(BF)


def project(x, g1, cos, sin, wq, wkv, gq, gk, with_q):
    rows = x.shape[0]
    bm = 256
    row = lambda width: pl.BlockSpec((bm, width), lambda i: (i, 0))
    ins = [x, g1, cos, sin] + ([wq] if with_q else []) + [wkv] + ([gq] if with_q else []) + [gk]
    specs = [row(D), whole((1, D)), row(HEAD_DIM), row(HEAD_DIM)]
    specs += [whole((D, QW))] if with_q else []
    specs += [whole((D, 2 * KW))]
    specs += [whole((1, HEAD_DIM))] * (2 if with_q else 1)
    widths = [D] + ([QW, QW] if with_q else []) + [KW, KW, KW]
    return pl.pallas_call(
        functools.partial(project_kernel, with_q),
        out_shape=[jax.ShapeDtypeStruct((rows, w), BF) for w in widths],
        grid=(rows // bm,),
        in_specs=specs,
        out_specs=[row(w) for w in widths],
        compiler_params=params(),
        cost_estimate=pl.CostEstimate(
            flops=2 * rows * D * (2 * KW + (QW if with_q else 0)),
            bytes_accessed=2 * rows * sum(widths) + 2 * D * (2 * KW + QW),
            transcendentals=0,
        ),
    )(*ins)


def attend_kernel(own_p, oth, q, k_own, v_own, k_oth, v_oth, qpos, kpos, cqc, ckc, o_out, l_out):
    i = pl.program_id(1)
    bq = q.shape[0]
    is_prompt = i * bq < own_p

    def run(kind):
        for head in range(GROUP):
            cols = slice(head * HEAD_DIM, (head + 1) * HEAD_DIM)
            qh = q[:, cols]
            parts = [(dot_t(qh, k_own[:own_p, :]), v_own[:own_p, :])]
            if oth:
                parts.append((dot_t(qh, k_oth[...]), v_oth[...]))
            if kind == 0:
                at = 0
                masked = []
                for s, v in parts:
                    n = s.shape[1]
                    ok = kpos[:, at : at + n] <= qpos[...]
                    masked.append((jnp.where(ok, s, -1e30), v))
                    at += n
                parts = masked
            else:
                s = dot_t(qh, k_own[own_p:, :])
                code, lowest = cqc[:, 0:1], cqc[:, 1:2]
                ok = (ckc[...] <= code) & (ckc[...] >= lowest)
                parts.append((jnp.where(ok, s, -1e30), v_own[own_p:, :]))
            top = functools.reduce(
                jnp.maximum, [jnp.max(s, axis=-1, keepdims=True) for s, _ in parts]
            )
            total = jnp.zeros((bq, 1), F32)
            acc = jnp.zeros((bq, HEAD_DIM), F32)
            for s, v in parts:
                e = jnp.exp2(s - top)
                total += jnp.sum(e, axis=-1, keepdims=True)
                acc += dot(e.astype(BF), v)
            o_out[:, cols] = (acc / total).astype(BF)
            level = jnp.broadcast_to(top + jnp.log2(total), (bq, HEAD_DIM))
            l_out[0, head : head + 1, :] = level.T[0:1, :]

    @pl.when(is_prompt)
    def _():
        run(0)

    @pl.when(jnp.logical_not(is_prompt))
    def _():
        run(1)


def attend(q, k_own, v_own, k_oth, v_oth, pos, own_p, bq=256):
    rows = q.shape[0]
    oth = k_oth.shape[0]
    keys = own_p + oth
    head_col = lambda n: pl.BlockSpec((n, HEAD_DIM), lambda h, i: (0, h))
    cont_block = lambda h, i: (jnp.maximum(i - own_p // bq, 0), 0)
    return pl.pallas_call(
        functools.partial(attend_kernel, own_p, oth),
        out_shape=[
            jax.ShapeDtypeStruct((rows, QW), BF),
            jax.ShapeDtypeStruct((KV_HEADS_C, GROUP, rows), F32),
        ],
        grid=(KV_HEADS_C, rows // bq),
        in_specs=[
            pl.BlockSpec((bq, GROUP * HEAD_DIM), lambda h, i: (i, h)),
            head_col(rows),
            head_col(rows),
            head_col(oth),
            head_col(oth),
            pl.BlockSpec((bq, 1), lambda h, i: (i, 0)),
            whole((1, keys)),
            pl.BlockSpec((bq, 2), cont_block),
            whole((1, rows - own_p)),
        ],
        out_specs=[
            pl.BlockSpec((bq, GROUP * HEAD_DIM), lambda h, i: (i, h)),
            pl.BlockSpec((1, GROUP, bq), lambda h, i: (h, 0, i)),
        ],
        compiler_params=params(),
        cost_estimate=pl.CostEstimate(
            flops=4 * rows * keys * QW * 2,
            bytes_accessed=4 * rows * QW,
            transcendentals=rows * keys * Q_HEADS_C,
        ),
    )(q, k_own, v_own, k_oth, v_oth, pos["q_col"], pos["k_row"], pos["cq_col"], pos["ck_row"])


def attend_back_kernel(
    own_p, oth, chunk,
    q, qraw, do, o, level, cos_q, sin_q, gq, gk,
    k_own, v_own, kraw_own, cos_o, sin_o, k_oth, v_oth, kraw_oth, cos_t, sin_t,
    qpos, kpos, cqc, ckc,
    dq_out, dk_own_out, dv_own_out, dk_oth_out, dv_oth_out, dgq_out, dgk_out,
    dk_own, dv_own, dk_oth, dv_oth, dq_acc,
):
    h, i = pl.program_id(0), pl.program_id(1)
    bq = q.shape[0]
    is_prompt = i * bq < own_p

    @pl.when(i == 0)
    def _():
        dk_own[...] = jnp.zeros_like(dk_own)
        dv_own[...] = jnp.zeros_like(dv_own)
        dk_oth[...] = jnp.zeros_like(dk_oth)
        dv_oth[...] = jnp.zeros_like(dv_oth)

    @pl.when((i == 0) & (h == 0))
    def _():
        dgq_out[...] = jnp.zeros_like(dgq_out)
        dgk_out[...] = jnp.zeros_like(dgk_out)

    heads = [slice(g * HEAD_DIM, (g + 1) * HEAD_DIM) for g in range(GROUP)]
    q2 = jnp.concatenate([q[:, c] for c in heads], axis=0)
    do2 = jnp.concatenate([do[:, c] for c in heads], axis=0)
    lev = jnp.concatenate([level[0, g : g + 1, :] for g in range(GROUP)], axis=1)
    drows = []
    for c in heads:
        both = jnp.sum(do[:, c].astype(F32) * o[:, c].astype(F32), axis=-1, keepdims=True)
        drows.append(jnp.broadcast_to(both, (bq, HEAD_DIM)).T[0:1, :])
    drow = jnp.concatenate(drows, axis=1)

    def step(k, v, ok, dk, dv, rows):
        s = dot_t(k, q2)
        p = jnp.exp2(s - lev)
        if ok is not None:
            p = jnp.where(ok, p, 0.0)
        dp = dot_t(v, do2)
        ds = (p * (dp - drow)).astype(BF)
        dv[rows, :] += dot(p.astype(BF), do2)
        dk[rows, :] += dot(ds, q2)
        return t_dot(k, ds)

    def twice(row):
        return jnp.concatenate([row] * GROUP, axis=1)

    qrow = twice(qpos[...])
    dq = None
    for at in range(0, own_p, chunk):
        rows = slice(at, at + chunk)
        ok = kpos[rows, :] <= qrow
        part = step(k_own[rows, :], v_own[rows, :], ok, dk_own, dv_own, rows)
        dq = part if dq is None else dq + part
    dq_acc[...] = dq
    if oth // chunk <= 4:
        for at in range(0, oth, chunk):
            rows = slice(at, at + chunk)
            ok = kpos[own_p + at : own_p + at + chunk, :] <= qrow
            dq_acc[...] += step(k_oth[rows, :], v_oth[rows, :], ok, dk_oth, dv_oth, rows)
    else:

        @pl.loop(0, oth // chunk)
        def _(j):
            rows = pl.ds(pl.multiple_of(j * chunk, chunk), chunk)
            ok = kpos[pl.ds(pl.multiple_of(own_p + j * chunk, chunk), chunk), :] <= qrow
            dq_acc[...] += step(k_oth[rows, :], v_oth[rows, :], ok, dk_oth, dv_oth, rows)

    @pl.when(jnp.logical_not(is_prompt))
    def _():
        code, lowest = twice(cqc[0:1, :]), twice(cqc[1:2, :])
        rows = slice(own_p, k_own.shape[0])
        ok = (ckc[...] <= code) & (ckc[...] >= lowest)
        dq_acc[...] += step(k_own[rows, :], v_own[rows, :], ok, dk_own, dv_own, rows)

    scale = HEAD_DIM ** (-0.5)
    gain_sum = jnp.zeros((8, HEAD_DIM), F32)
    for g, c in enumerate(heads):
        grad = dq_acc[:, g * bq : (g + 1) * bq].T * scale
        raw, rows = head_norm_rot_back(
            qraw[:, c].astype(F32), gq[...], cos_q[...], sin_q[...], grad
        )
        dq_out[:, c] = raw.astype(BF)
        gain_sum += jnp.sum(rows.reshape(bq // 8, 8, HEAD_DIM), axis=0)
    dgq_out[...] += gain_sum

    @pl.when(i == pl.num_programs(1) - 1)
    def _():
        for total, raw_in, cos, sin, out in (
            (dk_own, kraw_own, cos_o, sin_o, dk_own_out),
            (dk_oth, kraw_oth, cos_t, sin_t, dk_oth_out),
        ):
            n = total.shape[0]
            part = 256

            def finish(rows, total=total, raw_in=raw_in, cos=cos, sin=sin, out=out):
                raw, gain_rows = head_norm_rot_back(
                    raw_in[rows, :].astype(F32),
                    gk[...],
                    cos[rows, :],
                    sin[rows, :],
                    total[rows, :] * (1.0 / LOG2E),
                )
                out[rows, :] = raw.astype(BF)
                dgk_out[...] += jnp.sum(gain_rows.reshape(part // 8, 8, HEAD_DIM), axis=0)

            @pl.loop(0, n // part)
            def _(j):
                finish(pl.ds(pl.multiple_of(j * part, part), part))

        dv_own_out[...] = dv_own[...].astype(BF)
        dv_oth_out[...] = dv_oth[...].astype(BF)


def attend_back(q, qraw, do, o, level, own, oth, tabs, gq, gk, pos, own_p, bq=256):
    rows = q.shape[0]
    n_oth = oth[0].shape[0]
    keys = own_p + n_oth
    chunk = min(512, own_p)
    wide = pl.BlockSpec((bq, GROUP * HEAD_DIM), lambda h, i: (i, h))
    tab = pl.BlockSpec((bq, HEAD_DIM), lambda h, i: (i, 0))
    head_col = lambda n: pl.BlockSpec((n, HEAD_DIM), lambda h, i: (0, h))
    cont_block = lambda h, i: (0, jnp.maximum(i - own_p // bq, 0))
    one = whole((1, HEAD_DIM))
    full = lambda n: whole((n, HEAD_DIM))
    cos_own, sin_own, cos_oth, sin_oth = tabs
    return pl.pallas_call(
        functools.partial(attend_back_kernel, own_p, n_oth, chunk),
        out_shape=[
            jax.ShapeDtypeStruct((rows, QW), BF),
            jax.ShapeDtypeStruct((rows, KW), BF),
            jax.ShapeDtypeStruct((rows, KW), BF),
            jax.ShapeDtypeStruct((n_oth, KW), BF),
            jax.ShapeDtypeStruct((n_oth, KW), BF),
            jax.ShapeDtypeStruct((8, HEAD_DIM), F32),
            jax.ShapeDtypeStruct((8, HEAD_DIM), F32),
        ],
        grid=(KV_HEADS_C, rows // bq),
        in_specs=[
            wide, wide, wide, wide,
            pl.BlockSpec((1, GROUP, bq), lambda h, i: (h, 0, i)),
            tab, tab, one, one,
            head_col(rows), head_col(rows), head_col(rows), full(rows), full(rows),
            head_col(n_oth), head_col(n_oth), head_col(n_oth), full(n_oth), full(n_oth),
            pl.BlockSpec((1, bq), lambda h, i: (0, i)),
            whole((keys, 1)),
            pl.BlockSpec((2, bq), cont_block),
            whole((rows - own_p, 1)),
        ],
        out_specs=[
            wide, head_col(rows), head_col(rows), head_col(n_oth), head_col(n_oth),
            whole((8, HEAD_DIM)), whole((8, HEAD_DIM)),
        ],
        scratch_shapes=[
            pltpu.VMEM((rows, HEAD_DIM), F32),
            pltpu.VMEM((rows, HEAD_DIM), F32),
            pltpu.VMEM((n_oth, HEAD_DIM), F32),
            pltpu.VMEM((n_oth, HEAD_DIM), F32),
            pltpu.VMEM((HEAD_DIM, GROUP * bq), F32),
        ],
        compiler_params=params(),
        cost_estimate=pl.CostEstimate(
            flops=10 * rows * keys * QW * 2,
            bytes_accessed=12 * rows * QW,
            transcendentals=rows * keys * Q_HEADS_C,
        ),
    )(
        q, qraw, do, o, level, cos_own, sin_own, gq, gk,
        own[0], own[1], own[2], cos_own, sin_own,
        oth[0], oth[1], oth[2], cos_oth, sin_oth,
        pos["q_row"], pos["k_col"], pos["cq_row"], pos["ck_col"],
    )


def feed_kernel(h1, dy, g2, wg, wu, wd, b_out, hid_out, dg_out, du_out, y_out, db_out):
    hv = h1[...]
    b = hv * lax.rsqrt(jnp.mean(hv * hv, axis=-1, keepdims=True) + EPS_NORM) * g2[...]
    b = b.astype(BF)
    b_out[...] = b
    dyv = dy[...]
    step = 512
    y = db = None
    for at in range(0, FW, step):
        cols = slice(at, at + step)
        gate = dot(b, wg[:, cols])
        up = dot(b, wu[:, cols])
        dhid = dot_t(dyv, wd[cols, :])
        sig = 1.0 / (1.0 + jnp.exp(-gate))
        act = gate * sig
        hid = (act * up).astype(BF)
        dgate = (dhid * up * (sig * (1.0 + gate * (1.0 - sig)))).astype(BF)
        dup = (dhid * act).astype(BF)
        hid_out[:, cols] = hid
        dg_out[:, cols] = dgate
        du_out[:, cols] = dup
        y_part = dot(hid, wd[cols, :])
        db_part = dot_t(dgate, wg[:, cols]) + dot_t(dup, wu[:, cols])
        y = y_part if y is None else y + y_part
        db = db_part if db is None else db + db_part
    y_out[...] = y
    db_out[...] = db


def feed(h1, dy, g2, wg, wu, wd):
    rows = h1.shape[0]
    bm = 256
    row = lambda width: pl.BlockSpec((bm, width), lambda i: (i, 0))
    return pl.pallas_call(
        feed_kernel,
        out_shape=[
            jax.ShapeDtypeStruct((rows, D), BF),
            jax.ShapeDtypeStruct((rows, FW), BF),
            jax.ShapeDtypeStruct((rows, FW), BF),
            jax.ShapeDtypeStruct((rows, FW), BF),
            jax.ShapeDtypeStruct((rows, D), F32),
            jax.ShapeDtypeStruct((rows, D), F32),
        ],
        grid=(rows // bm,),
        in_specs=[
            row(D), row(D), whole((1, D)), whole((D, FW)), whole((D, FW)), whole((FW, D)),
        ],
        out_specs=[row(D), row(FW), row(FW), row(FW), row(D), row(D)],
        compiler_params=params(),
        cost_estimate=pl.CostEstimate(
            flops=12 * rows * D * FW,
            bytes_accessed=rows * (16 * D + 6 * FW) + 6 * D * FW,
            transcendentals=rows * FW,
        ),
    )(h1, dy, g2, wg, wu, wd)


def layout():
    q_width = HEADS * HEAD_DIM
    kv_width = KV_HEADS * HEAD_DIM
    return [
        (D,),
        (D, q_width),
        (D, kv_width),
        (D, kv_width),
        (HEAD_DIM,),
        (HEAD_DIM,),
        (q_width, D),
        (D,),
        (D, FF),
        (D, FF),
        (FF, D),
    ]


def unpack(flat_vec, core):
    lanes = flat_vec.reshape(-1, 128)
    split = {1: 1, 2: 1, 3: 1, 6: 0, 8: 1, 9: 1, 10: 0}
    pieces = []
    offset = 0
    for number, shape in enumerate(layout()):
        count = shape[0] if len(shape) == 1 else shape[0] * shape[1]
        if number not in split:
            pieces.append(lax.slice(flat_vec, (offset,), (offset + count,)))
        else:
            rows, cols = shape
            block = lanes[offset // 128 : (offset + count) // 128]
            block = block.reshape(rows, cols // 128, 128)
            axis = split[number]
            width = block.shape[axis] // CORES
            block = lax.dynamic_slice_in_dim(block, core * width, width, axis)
            pieces.append(block.reshape(block.shape[0], -1))
        offset += count
    return pieces


def plain_grads(
    pick, a, a_far, b, o, hid, dgate, dup, dy, da_out, dq, dk, dv, dg1, dgq, dgk, dg2
):
    a_all = jnp.concatenate([a, a_far])
    grads = [
        dg1,
        t_dot(a, dq),
        t_dot(a_all, jnp.concatenate(dk)),
        t_dot(a_all, jnp.concatenate(dv)),
        jnp.sum(dgq, axis=0),
        jnp.sum(dgk, axis=0),
        t_dot(o, da_out),
        0.5 * dg2,
        t_dot(b, dgate),
        t_dot(b, dup),
        t_dot(hid, dy),
    ]
    flat = []
    for number, (grad, shape) in enumerate(zip(grads, layout())):
        if len(shape) == 2:
            axis = 0 if number in (6, 10) else 1
            blank = jnp.zeros_like(grad)
            grad = jnp.concatenate([pick(grad, blank), pick(blank, grad)], axis=axis)
        flat.append(grad.reshape(-1).astype(F32))
    return lax.psum_scatter(
        jnp.concatenate(flat), ("dp", "seq"), scatter_dimension=0, tiled=True
    )


LANES = 128
SHARD = 491592
FLAT_AT = {"g1": 0, "wq": 8, "wk": 16392, "wv": 24584, "gqk": 32776, "wo": 32778,
           "g2": 49162, "wg": 49170, "wu": 73746, "wd": 98322}
PER_ROW = {"wq": 16, "wk": 8, "wv": 8, "wo": 8, "wg": 24, "wu": 24, "wd": 8}
X_FIRST = ("wq", "wo", "wd")
FEED_PARTS = {
    (1, 0): [("wo", 0, 704)],
    (1, 1): [("wo", 704, 1664)],
    (1, 2): [("wo", 1664, 2048), ("wg", 0, 192)],
    (1, 3): [("wg", 192, 512)],
    (2, 0): [("wg", 512, 832)],
    (2, 1): [("wg", 832, 1024), ("wu", 0, 128)],
    (2, 2): [("wu", 128, 448)],
    (2, 3): [("wu", 448, 768)],
    (3, 0): [("wu", 768, 1024), ("wd", 0, 192)],
    (3, 1): [("wd", 192, 1152)],
    (3, 2): [("wd", 1152, 2112)],
    (3, 3): [("wd", 2112, 3072)],
}
HEAD_PARTS = {0: ("wq", 0, 512), 1: ("wq", 512, 1024), 2: ("wk", 0, 1024), 3: ("wv", 0, 1024)}
TAIL = 288


def plane_pairs(distance, wanted=lambda dp, seq: True):
    pairs = []
    for dp in range(4):
        for seq in range(8):
            to = dp ^ distance
            if wanted(to, seq):
                pairs.append((dp * 8 + seq, to * 8 + seq))
    return pairs


def swap_dp(block, distance):
    return lax.ppermute(block, "dp", [(i, i ^ distance) for i in range(4)])


def cut(block, index, axis=1):
    width = block.shape[axis] // 2
    return lax.dynamic_slice_in_dim(block, index * width, width, axis)


def plane_sum(grad, x_first):
    dp = lax.axis_index("dp")
    order = ((dp % 2, 1), (dp // 2, 2)) if x_first else ((dp // 2, 2), (dp % 2, 1))
    for mine, distance in order:
        got = swap_dp(cut(grad, 1 - mine), distance)
        grad = (cut(grad, mine).astype(F32) + got.astype(F32)).astype(BF)
    return grad


def line_sum(parts):
    line = lax.axis_index("seq") // 2
    low, high = line % 2, line // 2
    parts = parts.reshape((2, 2) + parts.shape[1:])
    for mine, mask, axis in ((low, 2, 1), (high, 4, 0)):
        keep = lax.dynamic_index_in_dim(parts, mine, axis, keepdims=False)
        send = lax.dynamic_index_in_dim(parts, 1 - mine, axis, keepdims=False)
        parts = (keep.astype(F32) + xor_seq(send, mask).astype(F32)).astype(BF)
    return parts


def stack_rows(grad, low, high):
    return [grad[low:high, at : at + LANES] for at in range(0, grad.shape[1], LANES)]


def flat_rows(cores, name, low, high, dp):
    rows = high - low
    per = PER_ROW[name] // 8
    blocks = []
    for core in range(2):
        for place in range(4):
            chip = (place % 2) * 2 + place // 2 if name in X_FIRST else place
            part = cores[core][chip ^ dp]
            blocks += [part[at * rows : (at + 1) * rows] for at in range(per)]
    return jnp.stack(blocks, axis=1).reshape(rows * 8 * per, LANES)


def fast_grads(
    core, pick, a, a_far, b, o, hid, dgate, dup, dy, da_out, dq, dk, dv, dg1, dgq, dgk, dg2
):
    dp = lax.axis_index("dp")
    line = lax.axis_index("seq") // 2

    def both(mine):
        got = xor_seq(mine, 1)
        return jnp.concatenate([pick(mine, got), pick(got, mine)], axis=1)

    def my_columns(rows):
        return cut(rows, core)

    def grad_of(left, right, name):
        return plane_sum(t_dot(left, right).astype(BF), name in X_FIRST)

    sums = {}
    sums["wg"] = grad_of(b, dgate, "wg")
    sums["wu"] = grad_of(b, dup, "wu")
    sums["wd"] = grad_of(both(hid), my_columns(dy), "wd")
    sums["wo"] = grad_of(both(o), my_columns(da_out), "wo")
    spare = jnp.zeros((256, LANES), BF)
    per_line = []
    for z in range(4):
        blocks = [spare] if z == 0 else []
        for d in (1, 2, 3):
            for name, low, high in FEED_PARTS[d, z]:
                blocks += stack_rows(sums[name], low, high)
        per_line.append(jnp.concatenate(blocks))
    feed_part = line_sum(jnp.stack(per_line)).reshape(3, 960, LANES)

    def for_chip(d):
        return lax.dynamic_index_in_dim(feed_part, jnp.maximum(d - 1, 0), 0, keepdims=False)

    got = [for_chip(dp)]
    for distance in (1, 2, 3):
        pairs = plane_pairs(distance, lambda d, s: d > 0)
        got.append(lax.ppermute(for_chip(dp ^ distance), ("dp", "seq"), pairs))
    got = jnp.stack(got)
    far = xor_seq(got, 1)
    feed_cores = (pick(got, far), pick(far, got))

    def feed_branch(d, z):
        def build(cores):
            if d == 0:
                return jnp.zeros((7680, LANES), BF)
            at = 256 if z == 0 and d == 1 else 0
            rows = [jnp.zeros((2048, LANES), BF)] if at else []
            for name, low, high in FEED_PARTS[d, z]:
                size = (high - low) * PER_ROW[name] // 8
                part = [[cores[c][k][at : at + size] for k in range(4)] for c in range(2)]
                rows.append(flat_rows(part, name, low, high, d))
                at += size
            return jnp.concatenate(rows)

        return build

    place = dp * 4 + line
    feed_flat = lax.switch(
        place, [feed_branch(d, z) for d in range(4) for z in range(4)], feed_cores
    )
    chain = [(8 * d + s, 8 * d + s + 2) for d in range(4) for s in range(8) if 8 * d + s < 30]
    before = lax.ppermute(feed_flat[-16:], ("dp", "seq"), chain)

    a_all = jnp.concatenate([a, a_far])
    head_q = grad_of(a, dq, "wq")
    pair = [t_dot(a_all, jnp.concatenate(part)).astype(BF) for part in (dk, dv)]
    head_kv = plane_sum(jnp.concatenate(pair), False)
    head_part = line_sum(
        jnp.stack(
            [
                jnp.concatenate(stack_rows(head_q, 0, 512)),
                jnp.concatenate(stack_rows(head_q, 512, 1024)),
                head_kv[:1024],
                head_kv[1024:],
            ]
        )
    )
    tail = jnp.where(
        line < 2,
        jnp.concatenate([head_part[512 - TAIL // 2 : 512], head_part[1024 - TAIL // 2 :]]),
        head_part[1024 - TAIL :],
    )
    ring = [(8 * d + s, 8 * d + (s + 2) % 8) for d in range(4) for s in range(8)]
    head_all = jnp.concatenate([head_part, lax.ppermute(tail, ("dp", "seq"), ring)])
    got = [head_all]
    for distance in (1, 2, 3):
        pairs = plane_pairs(distance, lambda d, s: d == 0 or (d == 1 and s < 2))
        got.append(lax.ppermute(head_all, ("dp", "seq"), pairs))
    got = jnp.stack(got)
    far = xor_seq(got, 1)
    head_cores = (pick(got, far), pick(far, got))

    gains = jnp.concatenate([dg1, jnp.sum(dgq, 0), jnp.sum(dgk, 0), 0.5 * dg2])
    gains = lax.psum(gains, ("dp", "seq")).reshape(-1, LANES)

    def shard_branch(d, z, c):
        first = (8 * d + 2 * z + c) * SHARD // LANES
        last = min(first + 3842, 122898)

        def build(cores, flat, before, gains):
            parts = []
            part_at = lambda low, high: [[cores[k][j][low:high] for j in range(4)] for k in (0, 1)]
            if d == 0 or (d == 1 and z == 0):
                if d == 0 and z == 0:
                    parts.append((FLAT_AT["g1"], gains[:8]))
                else:
                    name, low, high = HEAD_PARTS[(z - 1) % 4]
                    low = high - TAIL * 8 // PER_ROW[name]
                    rows = flat_rows(part_at(1024, 1024 + TAIL), name, low, high, d)
                    parts.append((FLAT_AT[name] + low * PER_ROW[name], rows.astype(F32)))
            if d == 0:
                name, low, high = HEAD_PARTS[z]
                rows = flat_rows(part_at(0, 1024), name, low, high, d)
                parts.append((FLAT_AT[name] + low * PER_ROW[name], rows.astype(F32)))
            elif d == 1 and z == 0:
                parts.append((FLAT_AT["gqk"], gains[8:10]))
                parts.append((FLAT_AT["wo"], flat[2048:].astype(F32)))
            else:
                name, low, high = FEED_PARTS[d, z][0]
                at = FLAT_AT[name] + low * PER_ROW[name]
                parts.append((at - 16, before.astype(F32)))
                used = 0
                for name, low, high in FEED_PARTS[d, z]:
                    size = (high - low) * PER_ROW[name]
                    if used and name == "wg":
                        parts.append((FLAT_AT["g2"], gains[10:18]))
                    at = FLAT_AT[name] + low * PER_ROW[name]
                    parts.append((at, flat[used : used + size].astype(F32)))
                    used += size
            kept = []
            reached = first
            for at, rows in parts:
                low = max(first, at)
                high = min(last, at + rows.shape[0])
                if high > low:
                    assert low == reached
                    kept.append(rows[low - at : high - at])
                    reached = high
            assert reached == last
            kept.append(jnp.zeros((3856 - (last - first), LANES), F32))
            return jnp.concatenate(kept)

        return build

    branches = [shard_branch(d, z, c) for d in range(4) for z in range(4) for c in range(2)]
    rows = lax.switch(place * 2 + core, branches, head_cores, feed_flat, before, gains)
    skip = ((place * 2 + core) * (SHARD % LANES)) % LANES
    return shift_rows(rows, LANES - skip, 3848).reshape(-1)[:SHARD]


def shift_kernel(lanes, rows_in, out):
    count = out.shape[0]
    col = lax.broadcasted_iota(jnp.int32, (count, LANES), 1)
    shift = lanes[0]
    turn = lax.rem(shift, LANES)
    now = pltpu.roll(rows_in[0:count, :], turn, 1)
    after = pltpu.roll(rows_in[pl.ds(1, count), :], turn, 1)
    out[...] = jnp.where(col < shift, now, after)


def shift_rows(rows, shift, count):
    shift = jnp.asarray(shift, jnp.int32).reshape(1)
    return pl.pallas_call(
        shift_kernel,
        out_shape=jax.ShapeDtypeStruct((count, LANES), F32),
        in_specs=[pl.BlockSpec(memory_space=pltpu.SMEM), pl.BlockSpec(memory_space=pltpu.VMEM)],
        out_specs=pl.BlockSpec(memory_space=pltpu.VMEM),
        compiler_params=params(),
    )(shift, rows)


def gather_weights(master_new):
    rank = lax.axis_index("seq")
    flat = jnp.concatenate([master_new, jnp.zeros((3848 * LANES - SHARD,), F32)])
    rows = flat.reshape(3848, LANES)
    moved = rank * 72
    ahead = moved // LANES
    blank = jnp.zeros((8, LANES), F32)
    rows = jnp.concatenate([blank, rows, blank])
    rows = lax.dynamic_slice_in_dim(rows, 7 - ahead, 3856 + 1, 0)
    rows = jnp.concatenate([rows, jnp.zeros((7, LANES), F32)])
    block = shift_rows(rows, moved % LANES, 3848 + 8)[:3848].astype(BF)
    blocks = lax.all_gather(block, "seq", axis=0)
    body, ends = blocks[:, :3840], blocks[:, 3840:]
    heads = body[1:, :8] + ends[:-1]
    heads = jnp.concatenate([body[:1, :8], heads])
    rows = jnp.concatenate([heads, body[:, 8:]], axis=1).reshape(-1, LANES)
    rows = jnp.concatenate([rows, ends[-1]])
    return rows.reshape(-1)[: 8 * SHARD]


def norm_back(x, gain, grad):
    r = lax.rsqrt(jnp.mean(x * x, axis=-1, keepdims=True) + EPS_NORM)
    xh = x * r
    dg = grad * gain
    return r * (dg - xh * jnp.mean(dg * xh, axis=-1, keepdims=True)), jnp.sum(grad * xh, axis=0)


def tables(positions):
    half_dim = HEAD_DIM // 2
    frequency = ROPE_BASE ** (-jnp.arange(half_dim, dtype=F32) * 2.0 / HEAD_DIM)
    angles = positions.astype(F32)[:, None] * frequency[None, :]
    cosine, sine = jnp.cos(angles), jnp.sin(angles)
    return jnp.concatenate([cosine, cosine], 1), jnp.concatenate([-sine, sine], 1)


def shards(x_prompt, x_cont, dy_prompt, dy_cont, prompt_pos, weights, master, moment1, moment2):
    count = lax.axis_size("seq")
    rank = lax.axis_index("seq")
    half = count // 2
    side = rank // half
    core = rank % CORES
    chips = half // CORES
    p = x_prompt.shape[1]
    c = x_cont.shape[1]
    prompt_len = p * count
    own_p = 4 * p
    first = core == 0

    def pick(lo, hi):
        return jnp.where(first, lo, hi)

    def share(mine, got):
        return pick(mine, got), pick(got, mine)

    def chip_rows(prompt, cont):
        both = jnp.concatenate([prompt, cont], axis=1)
        own = lax.dynamic_index_in_dim(both, side, 0, keepdims=False)
        other = lax.dynamic_index_in_dim(both, 1 - side, 0, keepdims=False)
        mine = jnp.stack([own, xor_seq(other, half)])
        return mine, xor_seq(mine, 1)

    def join(mine, got):
        lo, hi = share(mine, got)
        rows_p = jnp.concatenate([lo[:, :p], hi[:, :p]], axis=0).reshape(4 * p, D)
        rows_c = jnp.concatenate([lo[:, p:], hi[:, p:]], axis=0).reshape(4 * c, D)
        return jnp.concatenate([rows_p, rows_c], axis=0)

    x_mine, x_got = chip_rows(x_prompt, x_cont)
    x = join(x_mine, x_got)
    far = x_mine[:, :p].reshape(1, 2 * p, D)
    mask = 2
    while mask < half:
        far = jnp.concatenate([far, xor_seq(far, mask)], axis=0)
        mask *= 2
    far = far[1:]
    lo, hi = share(far, xor_seq(far, 1))
    x_far = jnp.stack([lo, hi], axis=1).reshape(-1, D)
    dy = join(*chip_rows(dy_prompt, dy_cont))

    (g1, w_q, w_k, w_v, gq, gk, w_o, g2, w_g, w_u, w_d) = unpack(weights, core)
    g1, g2, gq, gk = [gain.astype(F32).reshape(1, -1) for gain in (g1, g2, gq, gk)]
    w_kv = jnp.concatenate([w_k, w_v], axis=1)

    chip_ids = (rank - core) ^ (CORES * jnp.arange(chips)[:, None, None])
    ids = (chip_ids + jnp.arange(CORES)[None, :, None]) ^ (half * jnp.arange(2)[None, None, :])
    own_group = lax.dynamic_index_in_dim(prompt_pos, side, 0, keepdims=False)
    key_pos = jnp.take(own_group.reshape(count, p), ids.reshape(-1), axis=0).reshape(-1)
    quarter = c // 2
    steps = jnp.arange(quarter, dtype=jnp.int32)
    own_half = [
        prompt_len + jnp.concatenate([k * quarter + steps, (3 - k) * quarter + steps])
        for k in range(CORES)
    ]
    cont_pos = jnp.concatenate([own_half[0], own_half[0], own_half[1], own_half[1]])
    seg = jnp.tile(jnp.repeat(jnp.arange(2, dtype=jnp.int32), c), CORES)
    big = 2 * prompt_len + 4 * c
    cont_code = seg * big + cont_pos
    query_pos = jnp.concatenate([key_pos[:own_p], cont_pos])
    cont_q = jnp.stack([cont_code, seg * big])
    pos = {
        "q_col": query_pos[:, None], "q_row": query_pos[None, :],
        "k_col": key_pos[:, None], "k_row": key_pos[None, :],
        "cq_col": cont_q.T, "cq_row": cont_q,
        "ck_col": cont_code[:, None], "ck_row": cont_code[None, :],
    }
    cos_own, sin_own = tables(query_pos)
    cos_far, sin_far = tables(key_pos[own_p:])

    a, q, qraw, k_own, kraw_own, v_own = project(x, g1, cos_own, sin_own, w_q, w_kv, gq, gk, True)
    a_far, k_far, kraw_far, v_far = project(x_far, g1, cos_far, sin_far, w_q, w_kv, gq, gk, False)
    o, level = attend(q, k_own, v_own, k_far, v_far, pos, own_p)

    h1_part = dot(o, w_o)
    h1 = x.astype(F32) + h1_part + xor_seq(h1_part.astype(BF), 1).astype(F32)
    b, hid, dgate, dup, y_part, db_part = feed(h1, dy, g2, w_g, w_u, w_d)

    def core_rows(rows, which):
        return jnp.concatenate(
            [
                lax.dynamic_slice_in_dim(rows, which * 2 * p, 2 * p),
                lax.dynamic_slice_in_dim(rows, own_p + which * 2 * c, 2 * c),
            ]
        )

    def core_sum(rows):
        sent = core_rows(rows, 1 - core).astype(BF)
        return core_rows(rows, core).astype(F32) + xor_seq(sent, 1).astype(F32)

    def send_home(rows):
        rows_p, rows_c = rows[: 2 * p], rows[2 * p :]
        own = jnp.concatenate([rows_p[:p], rows_c[:c]])
        away = jnp.concatenate([rows_p[p:], rows_c[c:]]).astype(BF)
        back = xor_seq(away, half).astype(F32)
        zero = side == 0
        out = jnp.stack([jnp.where(zero, own, back), jnp.where(zero, back, own)])
        return out[:, :p], out[:, p:]

    y_prompt, y_cont = send_home(core_rows(h1, core) + core_sum(y_part))

    db = db_part + xor_seq(db_part.astype(BF), 1).astype(F32)
    dh1_back, dg2 = norm_back(h1, g2, db)
    dh1 = dy.astype(F32) + dh1_back
    da_out = dh1.astype(BF)
    d_o = dot_t(da_out, w_o).astype(BF)

    (dq, dk_own, dv_own, dk_far, dv_far, dgq, dgk) = attend_back(
        q, qraw, d_o, o, level,
        (k_own, v_own, kraw_own), (k_far, v_far, kraw_far),
        (cos_own, sin_own, cos_far, sin_far), gq, gk, pos, own_p,
    )

    dkv_own = jnp.concatenate([dk_own, dv_own], axis=1)
    dkv_far = jnp.concatenate([dk_far, dv_far], axis=1)
    da_far = dot_t(dkv_far, w_kv).astype(BF).reshape(chips - 1, CORES, 2 * p, D)
    da_own = dot_t(dq, w_q) + dot_t(dkv_own, w_kv)
    far_keep = lax.dynamic_index_in_dim(da_far, core, 1, keepdims=False)
    far_send = lax.dynamic_index_in_dim(da_far, 1 - core, 1, keepdims=False)
    far_sum = far_keep.astype(F32) + xor_seq(far_send, 1).astype(F32)
    mine = core_sum(da_own)
    blocks = jnp.concatenate([mine[None, : 2 * p], far_sum])
    mask = half // 2
    while mask > 1:
        near, away = blocks[: mask // 2], blocks[mask // 2 :]
        blocks = near + xor_seq(away.astype(BF), mask).astype(F32)
        mask //= 2
    da = jnp.concatenate([blocks[0], mine[2 * p :]])
    x_core = core_rows(x, core).astype(F32)
    dx_back, dg1 = norm_back(x_core, g1, da)
    dx_prompt, dx_cont = send_home(core_rows(dh1, core) + dx_back)

    fast = count == 8 and lax.axis_size("dp") == 4
    if fast:
        grad_shard = fast_grads(
            core, pick, a, a_far, b, o, hid, dgate, dup, dy, da_out, dq,
            (dk_own, dk_far), (dv_own, dv_far), dg1, dgq, dgk, dg2,
        )
    else:
        grad_shard = plain_grads(
            pick, a, a_far, b, o, hid, dgate, dup, dy, da_out, dq,
            (dk_own, dk_far), (dv_own, dv_far), dg1, dgq, dgk, dg2,
        )
    moment1_new = BETA_ONE * moment1 + (1.0 - BETA_ONE) * grad_shard
    moment2_new = BETA_TWO * moment2 + (1.0 - BETA_TWO) * grad_shard * grad_shard
    update = moment1_new / CORRECT_ONE / (jnp.sqrt(moment2_new / CORRECT_TWO) + ADAM_EPS)
    master_new = master - LEARN_RATE * (update + DECAY_RATE * master)
    if fast:
        weights_new = gather_weights(master_new)
    else:
        weights_new = lax.all_gather(master_new.astype(BF), "seq", axis=0, tiled=True)
    return (y_prompt, y_cont, dx_prompt, dx_cont, grad_shard, master_new, moment1_new, weights_new)


def solution(mesh):
    placed = (
        P("dp", "seq", None),
        P("dp", "seq", None),
        P("dp", "seq", None),
        P("dp", "seq", None),
        P("dp", None),
        P(),
        P(("dp", "seq")),
        P(("dp", "seq")),
        P(("dp", "seq")),
    )
    return jax.shard_map(
        shards,
        mesh=mesh,
        in_specs=placed,
        out_specs=(
            P("dp", "seq", None),
            P("dp", "seq", None),
            P("dp", "seq", None),
            P("dp", "seq", None),
            P(("dp", "seq")),
            P(("dp", "seq")),
            P(("dp", "seq")),
            P("dp"),
        ),
        check_vma=False,
    )
```

time: 2950 us -> 1060 us (0.36)
  waiting for transfers between devices: 1320 us -> 369 us
  local copies, waits for them, and re-layouts: 758 us -> 127 us
  matrix products: 597 us -> 71.4 us
  Pallas kernels: 0 us -> 222 us
  other arithmetic: 206 us -> 113 us
  starting transfers between devices: 2.61 us -> 55.3 us
  blocking collectives: 0 us -> 49.4 us
    unnamed x4 -> x1, waiting for transfers between devices: 1070 us -> 0.02 us
    dot_general x154 -> x12, matrix products: 597 us -> 71.4 us  [the longest x7 38.2 us: t_dot(): lax.dot_general(left, right, (((0,), (0,)), ((), ())), preferred_element_...]
    ppermute x8 -> x42, waiting for transfers between devices: 0.02 us -> 369 us  [the longest x22 217 us: xor_seq(): return lax.ppermute(block, 'seq', [(i, i ^ mask) for i in range(count)])]
    unnamed x41 -> x199, local copies, waits for them, and re-layouts: 387 us -> 25.8 us
    pallas_call x0 -> x7, Pallas kernels: none -> 222 us  [the longest x1 105 us: attend_back(): pl.pallas_call(functools.partial(attend_back_kernel, own_p, n_oth, chunk)...]
    reduce_scatter x4 -> x0, waiting for transfers between devices: 153 us -> none  [the longest x2 153 us: micro_step(): lax.psum_scatter(grad_v_heads[:, :prompt_len], 'seq', scatter_dimension=1...]
    concatenate x3 -> x9, local copies, waits for them, and re-layouts: 107 us -> 6.15 us  [the longest x1 4.19 us: build(): return jnp.concatenate(kept)]
    all_gather x4 -> x1, waiting for transfers between devices: 99.1 us -> 0.01 us  [gather_weights(): blocks = lax.all_gather(block, 'seq', axis=0)]
  transfers between devices with their start and end apart: 18 -> 43, of which waited for: 8 -> 20; matrix products, arithmetic and copies ran while one was open for 10% -> 26% of each run, Pallas kernels for 0% -> 21%
where the time goes in v1:
time: 1060 us; the launch traced here: 1050 us
  waiting for transfers between devices  369 us (35%)
  Pallas kernels  222 us (21%)
  local copies, waits for them, and re-layouts  127 us (12%)
  other arithmetic  113 us (11%)
  matrix products  71.4 us (7%)
  starting transfers between devices  55.3 us (5%)
  blocking collectives  49.4 us (5%)
  loops' own time  25.7 us (2%)
  between operations  16.3 us (2%)
    ppermute x22, waiting for transfers between devices, xor_seq(): return lax.ppermute(block, 'seq', [(i, i ^ mask) for i in range(count)])  217 us
    ppermute x12, waiting for transfers between devices, swap_dp(): return lax.ppermute(block, 'dp', [(i, i ^ distance) for i in range(4)])  128 us
    pallas_call x1, Pallas kernels, attend_back(): pl.pallas_call(functools.partial(attend_back_kernel, own_p, n_oth, chunk)...  105 us
    pallas_call x1, Pallas kernels, attend(): pl.pallas_call(functools.partial(attend_kernel, own_p, oth), out_shape=[j...  53.3 us
    psum x1, blocking collectives, fast_grads(): gains = lax.psum(gains, ('dp', 'seq')).reshape(-1, LANES)  49.4 us
    pallas_call x1, Pallas kernels, feed(): pl.pallas_call(feed_kernel, out_shape=[jax.ShapeDtypeStruct((rows, D), BF...  38.7 us
    dot_general x7, matrix products, t_dot(): lax.dot_general(left, right, (((0,), (0,)), ((), ())), preferred_element_...  38.2 us
    dynamic_slice x7, local copies, waits for them, and re-layouts, unpack(): block = lax.dynamic_slice_in_dim(block, core * width, width, axis)  32.7 us
  transfers between devices with their start and end apart: 43, of which 20 were waited for; matrix products, arithmetic and copies ran while one was open for 26% of the time, Pallas kernels for 21%

profile of v1, /device:TPU:0, one launch (start us, length us, event | category | flops | bytes accessed | tf_op | source)
XLA Modules:
  0.0 1048.7 jit_solution(18309555549149335521)
XLA Ops:
  16.0 4.5 slice_bitcast_fusion.251
  20.5 6.0 slice_bitcast_fusion.249
  42.3 40.1 %collective-permute-done = bf16[384,1024]{1,0:T(8,128)(2,1)} collective-permute-done((bf16[384,1024]{1,0:T(8,128)(2,1)}, bf16[384,1024]{1,0:T(8,128)(2,1)}, u32[]{:S(2)}, u32[]{:S(2)}) %collective-permute-start) | collective-permute-done | bytes 786464 | tf_op jit(solution)/shard_map/ppermute | solution.py:54
  89.5 23.9 %collective-permute-done.2 = bf16[1,512,1024]{2,1,0:T(8,128)(2,1)} collective-permute-done((bf16[1,512,1024]{2,1,0:T(8,128)(2,1)S(1)}, bf16[1,512,1024]{2,1,0:T(8,128)(2,1)}, u32[]{:S(2)}, u32[]{:S(2)}) %collective-permute-start.2) | collective-permute-done | bytes 1048608 | tf_op jit(solution)/shard_map/ppermute | solution.py:54
  117.7 14.4 %shard_map.152 = (bf16[1536,1024]{1,0:T(8,128)(2,1)}, bf16[1536,1024]{1,0:T(8,128)(2,1)}, bf16[1536,1024]{1,0:T(8,128)(2,1)}, bf16[1536,512]{1,0:T(8,128)(2,1)},...) custom-call(bf16[1536,1024]{1,0:T(8,128)(2,1)} %pad_maximum_fusion.4.refs_0_, f32[1,1024]{1,0:T(1,128)S(1)} %bitcast.1526, ...), custom_call_target="tpu_custom_call" | custom-call | flops 6442450944 | bytes 18350080 | tf_op jit(solution)/shard_map/pallas_call | solution.py:117
  135.3 6.8 shard_map.153
  142.1 53.3 %shard_map.154 = (bf16[1536,1024]{1,0:T(8,128)(2,1)}, f32[4,2,1536]{2,1,0:T(2,128)S(1)}) custom-call(bf16[1536,1024]{1,0:T(8,128)(2,1)} %get-tuple-element.299.q, bf16[1536,512]{1,0:T(8,128)(2,1)} %get-tuple-element.300.k_own, bf16[1536,512]{1,0:T(8,128)(2,1)} %get-tuple-element.301.v_own, bf16[1024,512]{1,0:T(8,128)(2,1)} %get-tuple-element.302.k_oth, ...), custom_call_target="tpu_custom_call" | custom-call | flops 25769803776 | bytes 6291456 | tf_op jit(solution)/shard_map/pallas_call | solution.py:186
  195.4 7.8 fusion.246
  207.6 14.6 %slice_bitcast_fusion.248 = (bf16[3072,8,128]{2,1,0:T(8,128)(2,1)}, bf16[3145728]{0:T(1024)(128)(2,1)}, bf16[3145728]{0:T(1024)(128)(2,1)}) fusion(bf16[15730944]{0:T(1024)(128)(2,1)} %param.62), kind=kLoop, calls=%fused_computation.746 | loop fusion | bytes 37748736 | tf_op jit(solution)/shard_map/reshape | solution.py:479
  222.2 11.9 %constant_dynamic-slice_fusion.19 = (bf16[1024,12,128]{2,1,0:T(8,128)(2,1)}, bf16[1024,12,128]{2,1,0:T(8,128)(2,1)}) fusion(bf16[1024,24,128]{2,1,0:T(8,128)(2,1)} %bitcast.1558, s32[]{:T(128)S(6)} %select_n.370, bf16[1024,24,128]{2,1,0:T(8,128)(2,1)} %bitcast.1557), kind=kLoop, calls=%fused_computation.995 | loop fusion | bytes 12582916 | tf_op jit(solution)/shard_map/dynamic_slice | solution.py:482
  234.0 6.4 copy.194
  240.5 4.6 copy.196.wg
  245.1 6.4 copy.195
  251.5 4.6 copy.197.wu
  267.6 4.8 multiply_reduce_fusion.2
  272.4 38.7 %shard_map.155 = (bf16[1536,1024]{1,0:T(8,128)(2,1)}, bf16[1536,1536]{1,0:T(8,128)(2,1)}, bf16[1536,1536]{1,0:T(8,128)(2,1)}, bf16[1536,1536]{1,0:T(8,128)(2,1)}...) custom-call(f32[1536,1024]{1,0:T(8,128)} %get-tuple-element.516.h1, bf16[1536,1024]{1,0:T(8,128)(2,1)} %pad_maximum_fusion.5.dy, ...), custom_call_target="tpu_custom_call" | custom-call | flops 28991029248 | bytes 48758784 | tf_op jit(solution)/shard_map/pallas_call | solution.py:425
  311.1 8.3 convolution_convert_fusion.1
  321.2 5.7 convolution_convert_fusion
  338.2 18.8 %collective-permute-done.28 = bf16[1024,768]{1,0:T(8,128)(2,1)} collective-permute-done((bf16[1024,768]{1,0:T(8,128)(2,1)S(1)}, bf16[1024,768]{1,0:T(8,128)(2,1)}, u32[]{:S(2)}, u32[]{:S(2)}) %collective-permute-start.28) | collective-permute-done | bytes 1572896 | tf_op jit(solution)/shard_map/ppermute | solution.py:552
  361.4 27.6 %collective-permute-done.30 = bf16[1024,768]{1,0:T(8,128)(2,1)} collective-permute-done((bf16[1024,768]{1,0:T(8,128)(2,1)}, bf16[1024,768]{1,0:T(8,128)(2,1)}, u32[]{:S(2)}, u32[]{:S(2)}) %collective-permute-start.30) | collective-permute-done | bytes 1572896 | tf_op jit(solution)/shard_map/ppermute | solution.py:552
  393.5 5.9 broadcast_select_fusion.27
  400.5 9.5 collective-permute-done.31
  414.3 5.3 fusion.241
  419.6 7.7 convolution_convert_fusion.2.do
  427.3 104.5 %shard_map.156 = (bf16[1536,1024]{1,0:T(8,128)(2,1)}, bf16[1536,512]{1,0:T(8,128)(2,1)}, bf16[1536,512]{1,0:T(8,128)(2,1)}, bf16[1024,512]{1,0:T(8,128)(2,1)}, b...) custom-call(bf16[1536,1024]{1,0:T(8,128)(2,1)} %get-tuple-element.299.q, ...), custom_call_target="tpu_custom_call" | custom-call | flops 64424509440 | bytes 18874368 | tf_op jit(solution)/shard_map/pallas_call | solution.py:344
  531.9 7.6 fusion.238
  543.3 4.4 fusion.167
  554.9 7.7 convolution_add_fusion
  562.7 5.5 fusion.209
  575.9 17.0 %collective-permute-done.14 = bf16[1024,512]{1,0:T(8,128)(2,1)S(1)} collective-permute-done((bf16[1024,512]{1,0:T(8,128)(2,1)S(1)}, bf16[1024,512]{1,0:T(8,128)(2,1)S(1)}, u32[]{:S(2)}, u32[]{:S(2)}) %collective-permute-start.14) | collective-permute-done | bytes 1048608 | tf_op jit(solution)/shard_map/ppermute | solution.py:552
  599.4 9.1 collective-permute-done.27
  610.0 6.8 broadcast_select_fusion.25
  616.8 7.7 fusion.152
  629.3 29.6 %collective-permute-done.33 = bf16[3072,256]{1,0:T(8,128)(2,1)S(1)} collective-permute-done((bf16[3072,256]{1,0:T(8,128)(2,1)S(1)}, bf16[3072,256]{1,0:T(8,128)(2,1)S(1)}, u32[]{:S(2)}, u32[]{:S(2)}) %collective-permute-start.33) | collective-permute-done | bytes 1572896 | tf_op jit(solution)/shard_map/ppermute | solution.py:552
  662.1 13.8 %collective-permute-done.34 = bf16[3072,128]{1,0:T(8,128)(2,1)S(1)} collective-permute-done((bf16[3072,128]{1,0:T(8,128)(2,1)S(1)}, bf16[3072,128]{1,0:T(8,128)(2,1)S(1)}, u32[]{:S(2)}, u32[]{:S(2)}) %collective-permute-start.34) | collective-permute-done | bytes 786464 | tf_op jit(solution)/shard_map/ppermute | solution.py:552
  684.3 27.4 %collective-permute-done.19 = bf16[1024,128]{1,0:T(8,128)(2,1)S(1)} collective-permute-done((bf16[1024,128]{1,0:T(8,128)(2,1)S(1)}, bf16[1024,128]{1,0:T(8,128)(2,1)S(1)}, u32[]{:S(2)}, u32[]{:S(2)}) %collective-permute-start.19) | collective-permute-done | bytes 262176 | tf_op jit(solution)/shard_map/ppermute | solution.py:54
  720.9 17.2 %collective-permute-done.20 = bf16[288,128]{1,0:T(8,128)(2,1)S(1)} collective-permute-done((bf16[288,128]{1,0:T(8,128)(2,1)S(1)}, bf16[288,128]{1,0:T(8,128)(2,1)S(1)}, u32[]{:S(2)}, u32[]{:S(2)}) %collective-permute-start.20) | collective-permute-done | bytes 73760 | tf_op jit(solution)/shard_map/ppermute | solution.py:680
  741.4 6.3 collective-permute-done.36
  751.4 6.6 collective-permute-start.38
  776.7 49.4 %psum.7 = f32[18,128]{1,0:T(8,128)S(1)} all-reduce(f32[18,128]{1,0:T(8,128)S(1)} %maximum_bitcast_fusion.3), channel_id=1, replica_groups=mesh['dp'=4,'seq'=8] {'dp','seq'}, use_global_device_ids=true, to_apply=%region_8.9 | all-reduce | flops 2304 | bytes 18432 | tf_op jit(solution)/shard_map/psum | solution.py:690
  826.2 10.2 conditional.2
  840.0 23.1 %conditional.3 = (f32[3856,128]{1,0:T(8,128)S(1)}) conditional(s32[]{:T(128)} %clamp.6, (f32[18,128]{1,0:T(8,128)S(1)}, bf16[4,1312,128]{2,1,0:T(8,128)(2,1)S(1)}, bf16[4,1312,128]{2,1,0:T(8,128)(2,1)S(1)}) %tuple.152, (bf16[4,1312,128]{2,1,0:T(8,128)(2,1)S(1)}, bf16[4,1312,128]{2,1,0:T(8,128)(2,1)S(1)}) %tuple.153, ...), branch_computations={%region_25.26_spmd, %region_26.27_spmd, %region_27.28_spmd, %regio... | conditional | flops 493568 | bytes 17654284 | solution.py:742
  865.3 4.9 multiply_subtract_fusion
  884.3 4.4 fusion.242
  889.7 5.0 collective-permute-start.8
  902.4 89.7 %collective-permute-done.8 = bf16[384,1024]{1,0:T(8,128)(2,1)} collective-permute-done((bf16[384,1024]{1,0:T(8,128)(2,1)}, bf16[384,1024]{1,0:T(8,128)(2,1)}, u32[]{:S(2)}, u32[]{:S(2)}) %collective-permute-start.8) | collective-permute-done | bytes 786464 | tf_op jit(solution)/shard_map/ppermute | solution.py:54
  997.5 28.6 %collective-permute-done.13 = bf16[384,1024]{1,0:T(8,128)(2,1)} collective-permute-done((bf16[384,1024]{1,0:T(8,128)(2,1)}, bf16[384,1024]{1,0:T(8,128)(2,1)}, u32[]{:S(2)}, u32[]{:S(2)}) %collective-permute-start.13) | collective-permute-done | bytes 786464 | tf_op jit(solution)/shard_map/ppermute | solution.py:54
  1036.0 5.7 maximum_bitcast_fusion
  (480 shorter events, 209.9 us)
Async XLA Ops:
  7.2 1023.1 %all-gather.3.cloned.1.call-start = ((), (), s32[]{:S(2)}) async-start(), calls=%async_computation | async-start | bytes 8865792 | tf_op jit(solution)/shard_map/all_gather | solution.py:779
  10.0 193.8 %collective-permute-start.5 = (bf16[384,1024]{1,0:T(8,128)(2,1)}, bf16[384,1024]{1,0:T(8,128)(2,1)}, u32[]{:S(2)}, u32[]{:S(2)}) collective-permute-start(bf16[384,1024]{1,0:T(8,128)(2,1)} %get-tuple-element.577), channel_id=1, source_target_pairs={{0,4},{1,5},{2,6},{3,7},{4,0},{5,1},{6,2},{7,3},{8,12},{9,13},{10,... | collective-permute-start | bytes 2359304 | tf_op jit(solution)/shard_map/ppermute | solution.py:54
  15.1 67.3 %collective-permute-start = (bf16[384,1024]{1,0:T(8,128)(2,1)}, bf16[384,1024]{1,0:T(8,128)(2,1)}, u32[]{:S(2)}, u32[]{:S(2)}) collective-permute-start(bf16[384,1024]{1,0:T(8,128)(2,1)} %get-tuple-element.579), channel_id=1, source_target_pairs={{0,4},{1,5},{2,6},{3,7},{4,0},{5,1},{6,2},{7,3},{8,12},{9,13},{10,... | collective-permute-start | bytes 2359304 | tf_op jit(solution)/shard_map/ppermute | solution.py:54
  38.8 156.5 %copy-start.42 = (bf16[1024,8,128]{2,1,0:T(8,128)(2,1)}, bf16[1024,8,128]{2,1,0:T(8,128)(2,1)S(1)}, u32[]{:S(2)}) copy-start(bf16[1024,8,128]{2,1,0:T(8,128)(2,1)S(1)} %constant_dynamic-slice_fusion.24) | copy-start | bytes 6291460
  41.6 76.1 %copy-start.8 = (f32[1,128]{1,0:T(1,128)}, f32[1,128]{1,0:T(1,128)S(1)}, u32[]{:S(2)}) copy-start(f32[1,128]{1,0:T(1,128)S(1)} %get-tuple-element.555.refs_6_.gq) | copy-start | bytes 1540
  41.6 93.7 %copy-start.6 = (f32[1,128]{1,0:T(1,128)}, f32[1,128]{1,0:T(1,128)S(1)}, u32[]{:S(2)}) copy-start(f32[1,128]{1,0:T(1,128)S(1)} %get-tuple-element.554.refs_7_.refs_5_.gk) | copy-start | bytes 1540
  42.3 93.0 %copy-start.4 = (f32[1024]{0:T(1024)}, f32[1024]{0:T(1024)S(1)}, u32[]{:S(2)}) copy-start(f32[1024]{0:T(1024)S(1)} %get-tuple-element.551) | copy-start | bytes 12292
  83.7 29.8 %collective-permute-start.1 = (bf16[2,384,1024]{2,1,0:T(8,128)(2,1)S(1)}, bf16[2,384,1024]{2,1,0:T(8,128)(2,1)S(1)}, u32[]{:S(2)}, u32[]{:S(2)}) collective-permute-start(bf16[2,384,1024]{2,1,0:T(8,128)(2,1)S(1)} %pad_maximum_fusion.11), channel_id=1, source_target_pairs={{0,1},{1,0},{2,3},{3,2},{4,5},{5,4},{6,7},{7,6},{8,9},{9,8},{10,11... | collective-permute-start | bytes 4718600 | tf_op jit(solution)/shard_map/ppermute | solution.py:54
  87.7 25.7 %collective-permute-start.2 = (bf16[1,512,1024]{2,1,0:T(8,128)(2,1)S(1)}, bf16[1,512,1024]{2,1,0:T(8,128)(2,1)}, u32[]{:S(2)}, u32[]{:S(2)}) collective-permute-start(bf16[1,512,1024]{2,1,0:T(8,128)(2,1)S(1)} %bitcast.1620), channel_id=1, source_target_pairs={{0,2},{1,3},{2,0},{3,1},{4,6},{5,7},{6,4},{7,5},{8,10},{9,11},{10,... | collective-permute-start | bytes 3145736 | tf_op jit(solution)/shard_map/ppermute | solution.py:54
  113.5 18.6 %collective-permute-start.3 = (bf16[1,512,1024]{2,1,0:T(8,128)(2,1)}, bf16[1,512,1024]{2,1,0:T(8,128)(2,1)}, u32[]{:S(2)}, u32[]{:S(2)}) collective-permute-start(bf16[1,512,1024]{2,1,0:T(8,128)(2,1)} %collective-permute-done.2), channel_id=1, source_target_pairs={{0,1},{1,0},{2,3},{3,2},{4,5},{5,4},{6,7},{7,6},{8,9},{9,8},{10,11... | collective-permute-start | bytes 3145736 | tf_op jit(solution)/shard_map/ppermute | solution.py:54
  203.2 62.2 %collective-permute-start.4 = (bf16[1536,1024]{1,0:T(8,128)(2,1)}, bf16[1536,1024]{1,0:T(8,128)(2,1)}, u32[]{:S(2)}, u32[]{:S(2)}) collective-permute-start(bf16[1536,1024]{1,0:T(8,128)(2,1)} %get-tuple-element.625), channel_id=1, source_target_pairs={{0,1},{1,0},{2,3},{3,2},{4,5},{5,4},{6,7},{7,6},{8,9},{9,8},{10,11... | collective-permute-start | bytes 9437192 | tf_op jit(solution)/shard_map/ppermute | solution.py:54
  206.1 54.8 %collective-permute-start.6 = (bf16[2,384,1024]{2,1,0:T(8,128)(2,1)}, bf16[2,384,1024]{2,1,0:T(8,128)(2,1)}, u32[]{:S(2)}, u32[]{:S(2)}) collective-permute-start(bf16[2,384,1024]{2,1,0:T(8,128)(2,1)} %pad_maximum_fusion.12), channel_id=1, source_target_pairs={{0,1},{1,0},{2,3},{3,2},{4,5},{5,4},{6,7},{7,6},{8,9},{9,8},{10,11... | collective-permute-start | bytes 4718600 | tf_op jit(solution)/shard_map/ppermute | solution.py:54
  265.5 128.0 %collective-permute-start.25 = (bf16[1536,1024]{1,0:T(8,128)(2,1)}, bf16[1536,1024]{1,0:T(8,128)(2,1)}, u32[]{:S(2)}, u32[]{:S(2)}) collective-permute-start(bf16[1536,1024]{1,0:T(8,128)(2,1)} %get-tuple-element.304.o), channel_id=1, source_target_pairs={{0,1},{1,0},{2,3},{3,2},{4,5},{5,4},{6,7},{7,6},{8,9},{9,8},{10,11... | collective-permute-start | bytes 9437192 | tf_op jit(solution)/shard_map/ppermute | solution.py:54
  319.5 37.5 %collective-permute-start.28 = (bf16[1024,768]{1,0:T(8,128)(2,1)S(1)}, bf16[1024,768]{1,0:T(8,128)(2,1)}, u32[]{:S(2)}, u32[]{:S(2)}) collective-permute-start(bf16[1024,768]{1,0:T(8,128)(2,1)S(1)} %constant_dynamic-slice_fusion.6), channel_id=1, source_target_pairs={{0,16},{8,24},{16,0},{24,8},{1,17},{9,25},{17,1},{25,9},{2,18},{10... | collective-permute-start | bytes 4718600 | tf_op jit(solution)/shard_map/ppermute | solution.py:552
  328.2 60.8 %collective-permute-start.30 = (bf16[1024,768]{1,0:T(8,128)(2,1)}, bf16[1024,768]{1,0:T(8,128)(2,1)}, u32[]{:S(2)}, u32[]{:S(2)}) collective-permute-start(bf16[1024,768]{1,0:T(8,128)(2,1)} %constant_dynamic-slice_fusion.4), channel_id=1, source_target_pairs={{0,16},{8,24},{16,0},{24,8},{1,17},{9,25},{17,1},{25,9},{2,18},{10... | collective-permute-start | bytes 4718600 | tf_op jit(solution)/shard_map/ppermute | solution.py:552
  335.2 75.9 %collective-permute-start.9 = (bf16[1536,1024]{1,0:T(8,128)(2,1)}, bf16[1536,1024]{1,0:T(8,128)(2,1)S(1)}, u32[]{:S(2)}, u32[]{:S(2)}) collective-permute-start(bf16[1536,1024]{1,0:T(8,128)(2,1)} %convert_element_type.371), channel_id=1, source_target_pairs={{0,1},{1,0},{2,3},{3,2},{4,5},{5,4},{6,7},{7,6},{8,9},{9,8},{10,11... | collective-permute-start | bytes 9437192 | tf_op jit(solution)/shard_map/ppermute | solution.py:54
  337.7 272.3 %collective-permute-start.32 = (bf16[1536,1536]{1,0:T(8,128)(2,1)}, bf16[1536,1536]{1,0:T(8,128)(2,1)}, u32[]{:S(2)}, u32[]{:S(2)}) collective-permute-start(bf16[1536,1536]{1,0:T(8,128)(2,1)} %get-tuple-element.323), channel_id=1, source_target_pairs={{0,1},{1,0},{2,3},{3,2},{4,5},{5,4},{6,7},{7,6},{8,9},{9,8},{10,11... | collective-permute-start | bytes 14155784 | tf_op jit(solution)/shard_map/ppermute | solution.py:54
  359.8 39.6 %collective-permute-start.29 = (bf16[1024,384]{1,0:T(8,128)(2,1)}, bf16[1024,384]{1,0:T(8,128)(2,1)S(1)}, u32[]{:S(2)}, u32[]{:S(2)}) collective-permute-start(bf16[1024,384]{1,0:T(8,128)(2,1)} %constant_dynamic-slice_fusion.5), channel_id=1, source_target_pairs={{0,8},{8,0},{16,24},{24,16},{1,9},{9,1},{17,25},{25,17},{2,10},{10... | collective-permute-start | bytes 2359304 | tf_op jit(solution)/shard_map/ppermute | solution.py:552
  391.9 18.1 %collective-permute-start.31 = (bf16[1024,384]{1,0:T(8,128)(2,1)}, bf16[1024,384]{1,0:T(8,128)(2,1)S(1)}, u32[]{:S(2)}, u32[]{:S(2)}) collective-permute-start(bf16[1024,384]{1,0:T(8,128)(2,1)} %constant_dynamic-slice_fusion.3), channel_id=1, source_target_pairs={{0,8},{8,0},{16,24},{24,16},{1,9},{9,1},{17,25},{25,17},{2,10},{10... | collective-permute-start | bytes 2359304 | tf_op jit(solution)/shard_map/ppermute | solution.py:552
  427.3 104.6 %copy-start.21 = (bf16[1024,8,128]{2,1,0:T(8,128)(2,1)S(1)}, bf16[1024,8,128]{2,1,0:T(8,128)(2,1)}, u32[]{:S(2)}) copy-start(bf16[1024,8,128]{2,1,0:T(8,128)(2,1)} %constant_dynamic-slice_fusion.27) | copy-start | bytes 6291460
  547.8 26.2 %collective-permute-start.26 = (bf16[2048,256]{1,0:T(8,128)(2,1)S(1)}, bf16[2048,256]{1,0:T(8,128)(2,1)S(1)}, u32[]{:S(2)}, u32[]{:S(2)}) collective-permute-start(bf16[2048,256]{1,0:T(8,128)(2,1)S(1)} %constant_dynamic-slice_fusion.8), channel_id=1, source_target_pairs={{0,8},{8,0},{16,24},{24,16},{1,9},{9,1},{17,25},{25,17},{2,10},{10... | collective-permute-start | bytes 3145736 | tf_op jit(solution)/shard_map/ppermute | solution.py:552
  552.8 165.4 %collective-permute-start.11 = (bf16[1,512,1024]{2,1,0:T(8,128)(2,1)}, bf16[1,512,1024]{2,1,0:T(8,128)(2,1)}, u32[]{:S(2)}, u32[]{:S(2)}) collective-permute-start(bf16[1,512,1024]{2,1,0:T(8,128)(2,1)} %dynamic-slice_bitcast_fusion.1), channel_id=1, source_target_pairs={{0,1},{1,0},{2,3},{3,2},{4,5},{5,4},{6,7},{7,6},{8,9},{9,8},{10,11... | collective-permute-start | bytes 3145736 | tf_op jit(solution)/shard_map/ppermute | solution.py:54
  553.4 39.5 %collective-permute-start.14 = (bf16[1024,512]{1,0:T(8,128)(2,1)S(1)}, bf16[1024,512]{1,0:T(8,128)(2,1)S(1)}, u32[]{:S(2)}, u32[]{:S(2)}) collective-permute-start(bf16[1024,512]{1,0:T(8,128)(2,1)S(1)} %constant_dynamic-slice_fusion.11), channel_id=1, source_target_pairs={{0,8},{8,0},{16,24},{24,16},{1,9},{9,1},{17,25},{25,17},{2,10},{10... | collective-permute-start | bytes 3145736 | tf_op jit(solution)/shard_map/ppermute | solution.py:552
  571.1 26.1 %collective-permute-start.16 = (bf16[2048,256]{1,0:T(8,128)(2,1)S(1)}, bf16[2048,256]{1,0:T(8,128)(2,1)S(1)}, u32[]{:S(2)}, u32[]{:S(2)}) collective-permute-start(bf16[2048,256]{1,0:T(8,128)(2,1)S(1)} %fusion.217), channel_id=1, source_target_pairs={{0,16},{8,24},{16,0},{24,8},{1,17},{9,25},{17,1},{25,9},{2,18},{10... | collective-permute-start | bytes 3145736 | tf_op jit(solution)/shard_map/ppermute | solution.py:552
  574.4 34.1 %collective-permute-start.27 = (bf16[2048,128]{1,0:T(8,128)(2,1)S(1)}, bf16[2048,128]{1,0:T(8,128)(2,1)S(1)}, u32[]{:S(2)}, u32[]{:S(2)}) collective-permute-start(bf16[2048,128]{1,0:T(8,128)(2,1)S(1)} %constant_dynamic-slice_fusion.7), channel_id=1, source_target_pairs={{0,16},{8,24},{16,0},{24,8},{1,17},{9,25},{17,1},{25,9},{2,18},{10... | collective-permute-start | bytes 1572872 | tf_op jit(solution)/shard_map/ppermute | solution.py:552
  594.2 31.9 %collective-permute-start.15 = (bf16[1024,256]{1,0:T(8,128)(2,1)}, bf16[1024,256]{1,0:T(8,128)(2,1)}, u32[]{:S(2)}, u32[]{:S(2)}) collective-permute-start(bf16[1024,256]{1,0:T(8,128)(2,1)} %constant_dynamic-slice_fusion.10), channel_id=1, source_target_pairs={{0,16},{8,24},{16,0},{24,8},{1,17},{9,25},{17,1},{25,9},{2,18},{10... | collective-permute-start | bytes 1572872 | tf_op jit(solution)/shard_map/ppermute | solution.py:552
  598.5 29.2 %collective-permute-start.17 = (bf16[2048,128]{1,0:T(8,128)(2,1)}, bf16[2048,128]{1,0:T(8,128)(2,1)}, u32[]{:S(2)}, u32[]{:S(2)}) collective-permute-start(bf16[2048,128]{1,0:T(8,128)(2,1)} %constant_dynamic-slice_fusion.9), channel_id=1, source_target_pairs={{0,8},{8,0},{16,24},{24,16},{1,9},{9,1},{17,25},{25,17},{2,10},{10... | collective-permute-start | bytes 1572872 | tf_op jit(solution)/shard_map/ppermute | solution.py:552
  624.6 34.3 %collective-permute-start.33 = (bf16[3072,256]{1,0:T(8,128)(2,1)S(1)}, bf16[3072,256]{1,0:T(8,128)(2,1)S(1)}, u32[]{:S(2)}, u32[]{:S(2)}) collective-permute-start(bf16[3072,256]{1,0:T(8,128)(2,1)S(1)} %constant_dynamic-slice_fusion.2), channel_id=1, source_target_pairs={{0,8},{8,0},{16,24},{24,16},{1,9},{9,1},{17,25},{25,17},{2,10},{10... | collective-permute-start | bytes 4718600 | tf_op jit(solution)/shard_map/ppermute | solution.py:552
  659.5 16.5 %collective-permute-start.34 = (bf16[3072,128]{1,0:T(8,128)(2,1)S(1)}, bf16[3072,128]{1,0:T(8,128)(2,1)S(1)}, u32[]{:S(2)}, u32[]{:S(2)}) collective-permute-start(bf16[3072,128]{1,0:T(8,128)(2,1)S(1)} %constant_dynamic-slice_fusion.1), channel_id=1, source_target_pairs={{0,16},{8,24},{16,0},{24,8},{1,17},{9,25},{17,1},{25,9},{2,18},{10... | collective-permute-start | bytes 2359304 | tf_op jit(solution)/shard_map/ppermute | solution.py:552
  661.3 19.2 %collective-permute-start.18 = (bf16[2,1024,128]{2,1,0:T(8,128)(2,1)S(1)}, bf16[2,1024,128]{2,1,0:T(8,128)(2,1)S(1)}, u32[]{:S(2)}, u32[]{:S(2)}) collective-permute-start(bf16[2,1024,128]{2,1,0:T(8,128)(2,1)S(1)} %dynamic-slice_bitcast_fusion.5), channel_id=1, source_target_pairs={{0,2},{1,3},{2,0},{3,1},{4,6},{5,7},{6,4},{7,5},{8,10},{9,11},{10,... | collective-permute-start | bytes 1572872 | tf_op jit(solution)/shard_map/ppermute | solution.py:54
  676.8 36.0 %collective-permute-start.35 = (bf16[2,2880,128]{2,1,0:T(8,128)(2,1)S(1)}, bf16[2,2880,128]{2,1,0:T(8,128)(2,1)S(1)}, u32[]{:S(2)}, u32[]{:S(2)}) collective-permute-start(bf16[2,2880,128]{2,1,0:T(8,128)(2,1)S(1)} %dynamic-slice_bitcast_fusion), channel_id=1, source_target_pairs={{0,2},{1,3},{2,0},{3,1},{4,6},{5,7},{6,4},{7,5},{8,10},{9,11},{10,... | collective-permute-start | bytes 4423688 | tf_op jit(solution)/shard_map/ppermute | solution.py:54
  680.6 31.1 %collective-permute-start.19 = (bf16[1024,128]{1,0:T(8,128)(2,1)S(1)}, bf16[1024,128]{1,0:T(8,128)(2,1)S(1)}, u32[]{:S(2)}, u32[]{:S(2)}) collective-permute-start(bf16[1024,128]{1,0:T(8,128)(2,1)S(1)} %dynamic-slice_bitcast_fusion.6), channel_id=1, source_target_pairs={{0,4},{1,5},{2,6},{3,7},{4,0},{5,1},{6,2},{7,3},{8,12},{9,13},{10,... | collective-permute-start | bytes 786440 | tf_op jit(solution)/shard_map/ppermute | solution.py:54
  684.3 85.9 %collective-permute-start.10 = (bf16[768,1024]{1,0:T(8,128)(2,1)}, bf16[768,1024]{1,0:T(8,128)(2,1)}, u32[]{:S(2)}, u32[]{:S(2)}) collective-permute-start(bf16[768,1024]{1,0:T(8,128)(2,1)} %pad_maximum_fusion.16), channel_id=1, source_target_pairs={{0,1},{1,0},{2,3},{3,2},{4,5},{5,4},{6,7},{7,6},{8,9},{9,8},{10,11... | collective-permute-start | bytes 4718600 | tf_op jit(solution)/shard_map/ppermute | solution.py:54
  713.3 34.5 %collective-permute-start.36 = (bf16[2880,128]{1,0:T(8,128)(2,1)S(1)}, bf16[2880,128]{1,0:T(8,128)(2,1)S(1)}, u32[]{:S(2)}, u32[]{:S(2)}) collective-permute-start(bf16[2880,128]{1,0:T(8,128)(2,1)S(1)} %dynamic-slice_bitcast_fusion.4), channel_id=1, source_target_pairs={{0,4},{1,5},{2,6},{3,7},{4,0},{5,1},{6,2},{7,3},{8,12},{9,13},{10,... | collective-permute-start | bytes 2211848 | tf_op jit(solution)/shard_map/ppermute | solution.py:54
  715.9 22.3 %collective-permute-start.20 = (bf16[288,128]{1,0:T(8,128)(2,1)S(1)}, bf16[288,128]{1,0:T(8,128)(2,1)S(1)}, u32[]{:S(2)}, u32[]{:S(2)}) collective-permute-start(bf16[288,128]{1,0:T(8,128)(2,1)S(1)} %slice_select_fusion), channel_id=1, source_target_pairs={{0,2},{1,3},{2,4},{3,5},{4,6},{5,7},{6,0},{7,1},{8,10},{9,11},{10,... | collective-permute-start | bytes 221192 | tf_op jit(solution)/shard_map/ppermute | solution.py:680
  720.9 52.1 %collective-permute-start.12 = (bf16[1,512,1024]{2,1,0:T(8,128)(2,1)}, bf16[1,512,1024]{2,1,0:T(8,128)(2,1)}, u32[]{:S(2)}, u32[]{:S(2)}) collective-permute-start(bf16[1,512,1024]{2,1,0:T(8,128)(2,1)} %fusion.190), channel_id=1, source_target_pairs={{0,2},{1,3},{2,0},{3,1},{4,6},{5,7},{6,4},{7,5},{8,10},{9,11},{10,... | collective-permute-start | bytes 3145736 | tf_op jit(solution)/shard_map/ppermute | solution.py:54
  738.2 11.8 %collective-permute-start.21 = (bf16[1312,128]{1,0:T(8,128)(2,1)S(1)}, bf16[1312,128]{1,0:T(8,128)(2,1)S(1)}, u32[]{:S(2)}, u32[]{:S(2)}) collective-permute-start(bf16[1312,128]{1,0:T(8,128)(2,1)S(1)} %get-tuple-element.612), channel_id=1, source_target_pairs={{0,8},{1,9},{8,0},{9,1},{10,2},{11,3},{12,4},{13,5},{14,6},{15,7}} | collective-permute-start | bytes 1007624 | tf_op jit(solution)/shard_map/ppermute | solution.py:684
  740.1 11.2 %collective-permute-start.22 = (bf16[1312,128]{1,0:T(8,128)(2,1)S(1)}, bf16[1312,128]{1,0:T(8,128)(2,1)S(1)}, u32[]{:S(2)}, u32[]{:S(2)}) collective-permute-start(bf16[1312,128]{1,0:T(8,128)(2,1)S(1)} %get-tuple-element.612), channel_id=1, source_target_pairs={{16,0},{17,1},{18,2},{19,3},{20,4},{21,5},{22,6},{23,7},{24,8},{25... | collective-permute-start | bytes 1007624 | tf_op jit(solution)/shard_map/ppermute | solution.py:684
  747.8 13.5 %collective-permute-start.23 = (bf16[1312,128]{1,0:T(8,128)(2,1)S(1)}, bf16[1312,128]{1,0:T(8,128)(2,1)S(1)}, u32[]{:S(2)}, u32[]{:S(2)}) collective-permute-start(bf16[1312,128]{1,0:T(8,128)(2,1)S(1)} %get-tuple-element.612), channel_id=1, source_target_pairs={{16,8},{17,9},{24,0},{25,1},{26,2},{27,3},{28,4},{29,5},{30,6},{31... | collective-permute-start | bytes 1007624 | tf_op jit(solution)/shard_map/ppermute | solution.py:684
  750.0 14.9 %collective-permute-start.37 = (bf16[960,128]{1,0:T(8,128)(2,1)S(1)}, bf16[960,128]{1,0:T(8,128)(2,1)S(1)}, u32[]{:S(2)}, u32[]{:S(2)}) collective-permute-start(bf16[960,128]{1,0:T(8,128)(2,1)S(1)} %get-tuple-element.604), channel_id=1, source_target_pairs={{0,8},{1,9},{2,10},{3,11},{4,12},{5,13},{6,14},{7,15},{16,24},{17,... | collective-permute-start | bytes 737288 | tf_op jit(solution)/shard_map/ppermute | solution.py:633
  751.4 16.6 %collective-permute-start.38 = (bf16[960,128]{1,0:T(8,128)(2,1)S(1)}, bf16[960,128]{1,0:T(8,128)(2,1)S(1)}, u32[]{:S(2)}, u32[]{:S(2)}) collective-permute-start(bf16[960,128]{1,0:T(8,128)(2,1)S(1)} %get-tuple-element.603), channel_id=1, source_target_pairs={{0,16},{1,17},{2,18},{3,19},{4,20},{5,21},{6,22},{7,23},{8,24},{9,... | collective-permute-start | bytes 737288 | tf_op jit(solution)/shard_map/ppermute | solution.py:633
  761.3 6.7 collective-permute-start.39
  764.9 73.2 %collective-permute-start.24 = (bf16[4,1312,128]{2,1,0:T(8,128)(2,1)}, bf16[4,1312,128]{2,1,0:T(8,128)(2,1)}, u32[]{:S(2)}, u32[]{:S(2)}) collective-permute-start(bf16[4,1312,128]{2,1,0:T(8,128)(2,1)} %pad_maximum_fusion.18), channel_id=1, source_target_pairs={{0,1},{1,0},{2,3},{3,2},{4,5},{5,4},{6,7},{7,6},{8,9},{9,8},{10,11... | collective-permute-start | bytes 4030472 | tf_op jit(solution)/shard_map/ppermute | solution.py:54
  770.2 56.0 %collective-permute-start.40 = (bf16[4,960,128]{2,1,0:T(8,128)(2,1)S(1)}, bf16[4,960,128]{2,1,0:T(8,128)(2,1)S(1)}, u32[]{:S(2)}, u32[]{:S(2)}) collective-permute-start(bf16[4,960,128]{2,1,0:T(8,128)(2,1)S(1)} %pad_maximum_fusion.24), channel_id=1, source_target_pairs={{0,1},{1,0},{2,3},{3,2},{4,5},{5,4},{6,7},{7,6},{8,9},{9,8},{10,11... | collective-permute-start | bytes 2949128 | tf_op jit(solution)/shard_map/ppermute | solution.py:54
  836.3 3.7 collective-permute-start.41
  880.7 3.6 collective-permute-start.7
  889.7 102.3 %collective-permute-start.8 = (bf16[384,1024]{1,0:T(8,128)(2,1)}, bf16[384,1024]{1,0:T(8,128)(2,1)}, u32[]{:S(2)}, u32[]{:S(2)}) collective-permute-start(bf16[384,1024]{1,0:T(8,128)(2,1)} %pad_maximum_fusion.27), channel_id=1, source_target_pairs={{0,4},{1,5},{2,6},{3,7},{4,0},{5,1},{6,2},{7,3},{8,12},{9,13},{10,... | collective-permute-start | bytes 2359304 | tf_op jit(solution)/shard_map/ppermute | solution.py:54
  901.0 125.1 %collective-permute-start.13 = (bf16[384,1024]{1,0:T(8,128)(2,1)}, bf16[384,1024]{1,0:T(8,128)(2,1)}, u32[]{:S(2)}, u32[]{:S(2)}) collective-permute-start(bf16[384,1024]{1,0:T(8,128)(2,1)} %pad_maximum_fusion.28), channel_id=1, source_target_pairs={{0,4},{1,5},{2,6},{3,7},{4,0},{5,1},{6,2},{7,3},{8,12},{9,13},{10,... | collective-permute-start | bytes 2359304 | tf_op jit(solution)/shard_map/ppermute | solution.py:54
  (78 other events, 517.7 us)
Sparse Core Ops, SparseCore 0:
  877.4 148.1 all-gather.2

commit v2 on v1

v2 whole, which is shorter than its diff:
```python
import functools

import jax
import jax.numpy as jnp
from jax import lax
from jax.experimental import pallas as pl
from jax.experimental.pallas import tpu as pltpu
from jax.sharding import PartitionSpec as P

D = 1024
FF = 3072
HEADS = 16
KV_HEADS = 8
HEAD_DIM = 128

EPS_NORM = 1e-06
ROPE_BASE = 1000000.0
BETA_ONE = 0.9
BETA_TWO = 0.95
ADAM_EPS = 1e-08
LEARN_RATE = 0.0003
DECAY_RATE = 0.1
CORRECT_ONE = 1.0 - 2.656139888758747e-05
CORRECT_TWO = 1.0 - 0.005920529220333996

CORES = 2
Q_HEADS_C = HEADS // CORES
KV_HEADS_C = KV_HEADS // CORES
QW = Q_HEADS_C * HEAD_DIM
KW = KV_HEADS_C * HEAD_DIM
FW = FF // CORES
GROUP = HEADS // KV_HEADS
LOG2E = 1.4426950408889634
SCORE_FOLD = HEAD_DIM ** (-0.5) * LOG2E
VMEM_LIMIT = 52 * 1024 * 1024
SMALL = pl.CostEstimate(flops=1000, bytes_accessed=1000, transcendentals=0)
BF = jnp.bfloat16
F32 = jnp.float32


def dot(left, right):
    return jnp.dot(left, right, preferred_element_type=F32)


def dot_t(left, right):
    return lax.dot_general(left, right, (((1,), (1,)), ((), ())), preferred_element_type=F32)


def t_dot(left, right):
    return lax.dot_general(left, right, (((0,), (0,)), ((), ())), preferred_element_type=F32)


def xor_seq(block, mask):
    count = lax.axis_size("seq")
    return lax.ppermute(block, "seq", [(i, i ^ mask) for i in range(count)])


def after(values, *earlier):
    return lax.optimization_barrier((values, earlier))[0]


def home_start(rows, half, p, c):
    rows_p, rows_c = rows[: 2 * p], rows[2 * p :]
    own = jnp.concatenate([rows_p[:p], rows_c[:c]])
    away = jnp.concatenate([rows_p[p:], rows_c[c:]]).astype(BF)
    return own, xor_seq(away, half)


def home_end(both, side, p):
    own, back = both[0], both[1].astype(F32)
    zero = side == 0
    out = jnp.stack([jnp.where(zero, own, back), jnp.where(zero, back, own)])
    return out[:, :p], out[:, p:]


def params(*semantics):
    return pltpu.CompilerParams(vmem_limit_bytes=VMEM_LIMIT)


def whole(shape):
    return pl.BlockSpec(shape, lambda *ids: (0,) * len(shape))


def head_norm_rot(raw, gain, cos, sin):
    r = lax.rsqrt(jnp.mean(raw * raw, axis=-1, keepdims=True) + EPS_NORM)
    n = raw * r * gain
    return n * cos + pltpu.roll(n, HEAD_DIM // 2, 1) * sin


def head_norm_rot_back(raw, gain, cos, sin, grad):
    dn = grad * cos - pltpu.roll(grad, HEAD_DIM // 2, 1) * sin
    r = lax.rsqrt(jnp.mean(raw * raw, axis=-1, keepdims=True) + EPS_NORM)
    xh = raw * r
    gain_rows = dn * xh
    dg = dn * gain
    return r * (dg - xh * jnp.mean(dg * xh, axis=-1, keepdims=True)), gain_rows


def project_kernel(with_q, *refs):
    if with_q:
        (x, g1, cos, sin, wq, wk, wv, gq, gk, a_out, q_out, qraw_out, k_out, kraw_out, v_out) = refs
    else:
        (x, g1, cos, sin, wk, wv, gk, a_out, k_out, kraw_out, v_out) = refs
    xv = x[...].astype(F32)
    a = xv * lax.rsqrt(jnp.mean(xv * xv, axis=-1, keepdims=True) + EPS_NORM) * g1[...]
    a = a.astype(BF)
    a_out[...] = a
    cosv, sinv = cos[...], sin[...]
    kv = dot(a, wk[...])
    for head in range(KV_HEADS_C):
        cols = slice(head * HEAD_DIM, (head + 1) * HEAD_DIM)
        raw = kv[:, cols]
        kraw_out[:, cols] = raw.astype(BF)
        k_out[:, cols] = head_norm_rot(raw, gk[...], cosv, sinv).astype(BF)
    v_out[...] = dot(a, wv[...]).astype(BF)
    if with_q:
        qv = dot(a, wq[...])
        for head in range(Q_HEADS_C):
            cols = slice(head * HEAD_DIM, (head + 1) * HEAD_DIM)
            raw = qv[:, cols]
            qraw_out[:, cols] = raw.astype(BF)
            rot = head_norm_rot(raw, gq[...], cosv, sinv)
            q_out[:, cols] = (rot * SCORE_FOLD).astype(BF)


def project(x, g1, cos, sin, wq, wk, wv, gq, gk, with_q):
    rows = x.shape[0]
    bm = 256
    row = lambda width: pl.BlockSpec((bm, width), lambda i: (i, 0))
    ins = [x, g1, cos, sin] + ([wq] if with_q else []) + [wk, wv] + ([gq] if with_q else []) + [gk]
    specs = [row(D), whole((1, D)), row(HEAD_DIM), row(HEAD_DIM)]
    specs += [whole((D, QW))] if with_q else []
    specs += [whole((D, KW))] * 2
    specs += [whole((1, HEAD_DIM))] * (2 if with_q else 1)
    widths = [D] + ([QW, QW] if with_q else []) + [KW, KW, KW]
    return pl.pallas_call(
        functools.partial(project_kernel, with_q),
        out_shape=[jax.ShapeDtypeStruct((rows, w), BF) for w in widths],
        grid=(rows // bm,),
        in_specs=specs,
        out_specs=[row(w) for w in widths],
        compiler_params=params(),
        cost_estimate=SMALL,
    )(*ins)


def attend_kernel(own_p, oth, cont, q, k_own, v_own, k_oth, v_oth, qpos, kpos, cqc, ckc, o_out, l_out):
    bq = q.shape[0]

    def run(kind):
        for head in range(GROUP):
            cols = slice(head * HEAD_DIM, (head + 1) * HEAD_DIM)
            qh = q[:, cols]
            parts = [(dot_t(qh, k_own[:own_p, :]), v_own[:own_p, :])]
            if oth:
                parts.append((dot_t(qh, k_oth[...]), v_oth[...]))
            if kind == 0:
                at = 0
                masked = []
                for s, v in parts:
                    n = s.shape[1]
                    ok = kpos[:, at : at + n] <= qpos[...]
                    masked.append((jnp.where(ok, s, -1e30), v))
                    at += n
                parts = masked
            else:
                s = dot_t(qh, k_own[own_p:, :])
                code, lowest = cqc[:, 0:1], cqc[:, 1:2]
                ok = (ckc[...] <= code) & (ckc[...] >= lowest)
                parts.append((jnp.where(ok, s, -1e30), v_own[own_p:, :]))
            top = functools.reduce(
                jnp.maximum, [jnp.max(s, axis=-1, keepdims=True) for s, _ in parts]
            )
            total = jnp.zeros((bq, 1), F32)
            acc = jnp.zeros((bq, HEAD_DIM), F32)
            for s, v in parts:
                e = jnp.exp2(s - top)
                total += jnp.sum(e, axis=-1, keepdims=True)
                acc += dot(e.astype(BF), v)
            o_out[:, cols] = (acc / total).astype(BF)
            level = jnp.broadcast_to(top + jnp.log2(total), (bq, HEAD_DIM))
            l_out[0, head : head + 1, :] = level.T[0:1, :]

    run(1 if cont else 0)


def attend(q, k_own, v_own, k_oth, v_oth, pos, own_p, cont, bq=256):
    rows = q.shape[0]
    oth = k_oth.shape[0]
    keys = own_p + oth
    base = own_p // bq if cont else 0
    here = rows - own_p if cont else own_p
    head_col = lambda n: pl.BlockSpec((n, HEAD_DIM), lambda h, i: (0, h))
    cont_block = lambda h, i: (i if cont else 0, 0)
    return pl.pallas_call(
        functools.partial(attend_kernel, own_p, oth, cont),
        out_shape=[
            jax.ShapeDtypeStruct((here, QW), BF),
            jax.ShapeDtypeStruct((KV_HEADS_C, GROUP, here), F32),
        ],
        grid=(KV_HEADS_C, here // bq),
        in_specs=[
            pl.BlockSpec((bq, GROUP * HEAD_DIM), lambda h, i: (base + i, h)),
            head_col(rows),
            head_col(rows),
            head_col(oth),
            head_col(oth),
            pl.BlockSpec((bq, 1), lambda h, i: (base + i, 0)),
            whole((1, keys)),
            pl.BlockSpec((bq, 2), cont_block),
            whole((1, rows - own_p)),
        ],
        out_specs=[
            pl.BlockSpec((bq, GROUP * HEAD_DIM), lambda h, i: (i, h)),
            pl.BlockSpec((1, GROUP, bq), lambda h, i: (h, 0, i)),
        ],
        compiler_params=params(),
        cost_estimate=SMALL,
    )(q, k_own, v_own, k_oth, v_oth, pos["q_col"], pos["k_row"], pos["cq_col"], pos["ck_row"])


def attend_back_kernel(
    own_p, oth, chunk,
    q, qraw, do, o, level, cos_q, sin_q, gq, gk,
    k_own, v_own, kraw_own, cos_o, sin_o, k_oth, v_oth, kraw_oth, cos_t, sin_t,
    qpos, kpos, cqc, ckc, *rest,
):
    (dq_out, dk_own_out, dv_own_out, dk_oth_out, dv_oth_out, dgq_out, dgk_out,
     dk_own, dv_own, dk_oth, dv_oth, dq_acc) = rest[-12:]
    i = pl.program_id(0)
    bq = q.shape[0]
    is_prompt = i * bq < own_p

    @pl.when(i == 0)
    def _():
        dk_own[...] = jnp.zeros_like(dk_own)
        dv_own[...] = jnp.zeros_like(dv_own)
        dk_oth[...] = jnp.zeros_like(dk_oth)
        dv_oth[...] = jnp.zeros_like(dv_oth)

    @pl.when(i == 0)
    def _():
        dgq_out[...] = jnp.zeros_like(dgq_out)
        dgk_out[...] = jnp.zeros_like(dgk_out)

    heads = [slice(g * HEAD_DIM, (g + 1) * HEAD_DIM) for g in range(GROUP)]
    q2 = jnp.concatenate([q[:, c] for c in heads], axis=0)
    do2 = jnp.concatenate([do[:, c] for c in heads], axis=0)
    lev = jnp.concatenate([level[0, g : g + 1, :] for g in range(GROUP)], axis=1)
    drows = []
    for c in heads:
        both = jnp.sum(do[:, c].astype(F32) * o[:, c].astype(F32), axis=-1, keepdims=True)
        drows.append(jnp.broadcast_to(both, (bq, HEAD_DIM)).T[0:1, :])
    drow = jnp.concatenate(drows, axis=1)

    def step(k, v, ok, dk, dv, rows):
        s = dot_t(k, q2)
        p = jnp.exp2(s - lev)
        if ok is not None:
            p = jnp.where(ok, p, 0.0)
        dp = dot_t(v, do2)
        ds = (p * (dp - drow)).astype(BF)
        dv[rows, :] += dot(p.astype(BF), do2)
        dk[rows, :] += dot(ds, q2)
        return t_dot(k, ds)

    def twice(row):
        return jnp.concatenate([row] * GROUP, axis=1)

    qrow = twice(qpos[...])
    dq = None
    for at in range(0, own_p, chunk):
        rows = slice(at, at + chunk)
        ok = kpos[rows, :] <= qrow
        part = step(k_own[rows, :], v_own[rows, :], ok, dk_own, dv_own, rows)
        dq = part if dq is None else dq + part
    dq_acc[...] = dq
    if oth // chunk <= 4:
        for at in range(0, oth, chunk):
            rows = slice(at, at + chunk)
            ok = kpos[own_p + at : own_p + at + chunk, :] <= qrow
            dq_acc[...] += step(k_oth[rows, :], v_oth[rows, :], ok, dk_oth, dv_oth, rows)
    else:

        @pl.loop(0, oth // chunk)
        def _(j):
            rows = pl.ds(pl.multiple_of(j * chunk, chunk), chunk)
            ok = kpos[pl.ds(pl.multiple_of(own_p + j * chunk, chunk), chunk), :] <= qrow
            dq_acc[...] += step(k_oth[rows, :], v_oth[rows, :], ok, dk_oth, dv_oth, rows)

    @pl.when(jnp.logical_not(is_prompt))
    def _():
        code, lowest = twice(cqc[0:1, :]), twice(cqc[1:2, :])
        rows = slice(own_p, k_own.shape[0])
        ok = (ckc[...] <= code) & (ckc[...] >= lowest)
        dq_acc[...] += step(k_own[rows, :], v_own[rows, :], ok, dk_own, dv_own, rows)

    scale = HEAD_DIM ** (-0.5)
    gain_sum = jnp.zeros((8, HEAD_DIM), F32)
    for g, c in enumerate(heads):
        grad = dq_acc[:, g * bq : (g + 1) * bq].T * scale
        raw, rows = head_norm_rot_back(
            qraw[:, c].astype(F32), gq[...], cos_q[...], sin_q[...], grad
        )
        dq_out[:, c] = raw.astype(BF)
        gain_sum += jnp.sum(rows.reshape(bq // 8, 8, HEAD_DIM), axis=0)
    dgq_out[...] += gain_sum

    @pl.when(i == pl.num_programs(0) - 1)
    def _():
        for total, raw_in, cos, sin, out in (
            (dk_own, kraw_own, cos_o, sin_o, dk_own_out),
            (dk_oth, kraw_oth, cos_t, sin_t, dk_oth_out),
        ):
            n = total.shape[0]
            part = 256

            def finish(rows, total=total, raw_in=raw_in, cos=cos, sin=sin, out=out):
                raw, gain_rows = head_norm_rot_back(
                    raw_in[rows, :].astype(F32),
                    gk[...],
                    cos[rows, :],
                    sin[rows, :],
                    total[rows, :] * (1.0 / LOG2E),
                )
                out[rows, :] = raw.astype(BF)
                dgk_out[...] += jnp.sum(gain_rows.reshape(part // 8, 8, HEAD_DIM), axis=0)

            @pl.loop(0, n // part)
            def _(j):
                finish(pl.ds(pl.multiple_of(j * part, part), part))

        dv_own_out[...] = dv_own[...].astype(BF)
        dv_oth_out[...] = dv_oth[...].astype(BF)


def attend_back(
    head, filled, waits, q, qraw, do, o, level, own, oth, tabs, gq, gk, pos, own_p, bq=256
):
    rows = q.shape[0]
    n_oth = oth[0].shape[0]
    keys = own_p + n_oth
    chunk = min(512, own_p)
    wide = pl.BlockSpec((bq, GROUP * HEAD_DIM), lambda i: (i, head))
    tab = pl.BlockSpec((bq, HEAD_DIM), lambda i: (i, 0))
    head_col = lambda n: pl.BlockSpec((n, HEAD_DIM), lambda i: (0, head))
    cont_block = lambda i: (0, jnp.maximum(i - own_p // bq, 0))
    one = whole((1, HEAD_DIM))
    full = lambda n: whole((n, HEAD_DIM))
    cos_own, sin_own, cos_oth, sin_oth = tabs
    ins = [
        q, qraw, do, o, level, cos_own, sin_own, gq, gk,
        own[0], own[1], own[2], cos_own, sin_own,
        oth[0], oth[1], oth[2], cos_oth, sin_oth,
        pos["q_row"], pos["k_col"], pos["cq_row"], pos["ck_col"],
    ]
    specs = [
        wide, wide, wide, wide,
        pl.BlockSpec((1, GROUP, bq), lambda i: (head, 0, i)),
        tab, tab, one, one,
        head_col(rows), head_col(rows), head_col(rows), full(rows), full(rows),
        head_col(n_oth), head_col(n_oth), head_col(n_oth), full(n_oth), full(n_oth),
        pl.BlockSpec((1, bq), lambda i: (0, i)),
        whole((keys, 1)),
        pl.BlockSpec((2, bq), cont_block),
        whole((rows - own_p, 1)),
    ]
    anywhere = pl.BlockSpec(memory_space=pl.ANY)
    aliases = {len(ins) + n: n for n in range(len(filled))}
    extra = list(filled) + list(waits)
    return pl.pallas_call(
        functools.partial(attend_back_kernel, own_p, n_oth, chunk),
        out_shape=[
            jax.ShapeDtypeStruct((rows, QW), BF),
            jax.ShapeDtypeStruct((rows, KW), BF),
            jax.ShapeDtypeStruct((rows, KW), BF),
            jax.ShapeDtypeStruct((n_oth, KW), BF),
            jax.ShapeDtypeStruct((n_oth, KW), BF),
            jax.ShapeDtypeStruct((8, HEAD_DIM), F32),
            jax.ShapeDtypeStruct((8, HEAD_DIM), F32),
        ],
        grid=(rows // bq,),
        in_specs=specs + [anywhere] * len(extra),
        out_specs=[
            wide, head_col(rows), head_col(rows), head_col(n_oth), head_col(n_oth),
            whole((8, HEAD_DIM)), whole((8, HEAD_DIM)),
        ],
        scratch_shapes=[
            pltpu.VMEM((rows, HEAD_DIM), F32),
            pltpu.VMEM((rows, HEAD_DIM), F32),
            pltpu.VMEM((n_oth, HEAD_DIM), F32),
            pltpu.VMEM((n_oth, HEAD_DIM), F32),
            pltpu.VMEM((HEAD_DIM, GROUP * bq), F32),
        ],
        input_output_aliases=aliases,
        compiler_params=params(),
        cost_estimate=SMALL,
    )(*ins, *extra)


def feed_kernel(x, part, got, dy, g2, wg, wu, wd, *rest):
    h1_out, b_out, hid_out, dg_out, du_out, y_out, db_out = rest[-7:]
    hv = x[...].astype(F32) + (part[...].astype(F32) + got[...].astype(F32))
    h1_out[...] = hv
    b = hv * lax.rsqrt(jnp.mean(hv * hv, axis=-1, keepdims=True) + EPS_NORM) * g2[...]
    b = b.astype(BF)
    b_out[...] = b
    dyv = dy[...]
    step = 512
    y = db = None
    for at in range(0, FW, step):
        cols = slice(at, at + step)
        gate = dot(b, wg[:, cols])
        up = dot(b, wu[:, cols])
        dhid = dot_t(dyv, wd[cols, :])
        sig = 1.0 / (1.0 + jnp.exp(-gate))
        act = gate * sig
        hid = (act * up).astype(BF)
        dgate = (dhid * up * (sig * (1.0 + gate * (1.0 - sig)))).astype(BF)
        dup = (dhid * act).astype(BF)
        hid_out[:, cols] = hid
        dg_out[:, cols] = dgate
        du_out[:, cols] = dup
        y_part = dot(hid, wd[cols, :])
        db_part = dot_t(dgate, wg[:, cols]) + dot_t(dup, wu[:, cols])
        y = y_part if y is None else y + y_part
        db = db_part if db is None else db + db_part
    y_out[...] = y.astype(BF)
    db_out[...] = db.astype(BF)


def feed(filled, base, total, x, part, got, dy, g2, wg, wu, wd):
    rows = part.shape[0]
    bm = 256
    base //= bm
    row = lambda width: pl.BlockSpec((bm, width), lambda i: (i, 0))
    later = lambda width: pl.BlockSpec((bm, width), lambda i: (base + i, 0))
    anywhere = pl.BlockSpec(memory_space=pl.ANY)
    return pl.pallas_call(
        feed_kernel,
        out_shape=[
            jax.ShapeDtypeStruct((total, D), F32),
            jax.ShapeDtypeStruct((total, D), BF),
            jax.ShapeDtypeStruct((total, FW), BF),
            jax.ShapeDtypeStruct((total, FW), BF),
            jax.ShapeDtypeStruct((total, FW), BF),
            jax.ShapeDtypeStruct((rows, D), BF),
            jax.ShapeDtypeStruct((rows, D), BF),
        ],
        grid=(rows // bm,),
        in_specs=[
            later(D), row(D), row(D), later(D), whole((1, D)), whole((D, FW)), whole((D, FW)), whole((FW, D)),
        ]
        + [anywhere] * len(filled),
        out_specs=[later(D), later(D), later(FW), later(FW), later(FW), row(D), row(D)],
        input_output_aliases={8 + n: n for n in range(len(filled))},
        compiler_params=params(),
        cost_estimate=SMALL,
    )(x, part, got, dy, g2, wg, wu, wd, *filled)


def back_kernel(h1, dy, mine, got, g2, wo, *rest):
    dh_out, da_out, do_out, dg_out = rest[-4:]
    hv = h1[...]
    db = mine[...].astype(F32) + got[...].astype(F32)
    r = lax.rsqrt(jnp.mean(hv * hv, axis=-1, keepdims=True) + EPS_NORM)
    xh = hv * r
    dg = db * g2[...]
    dh = dy[...].astype(F32) + r * (dg - xh * jnp.mean(dg * xh, axis=-1, keepdims=True))
    dh_out[...] = dh
    da = dh.astype(BF)
    da_out[...] = da
    do_out[...] = dot_t(da, wo[...]).astype(BF)
    gain = jnp.sum((db * xh).reshape(hv.shape[0] // 8, 8, D), axis=0)

    @pl.when(pl.program_id(0) == 0)
    def _():
        dg_out[...] = jnp.zeros_like(dg_out)

    dg_out[...] += gain


def back_norm(filled, base, h1, dy, mine, got, g2, wo):
    rows, total = mine.shape[0], h1.shape[0]
    bm = 256
    base //= bm
    row = lambda width: pl.BlockSpec((bm, width), lambda i: (i, 0))
    later = lambda width: pl.BlockSpec((bm, width), lambda i: (base + i, 0))
    anywhere = pl.BlockSpec(memory_space=pl.ANY)
    return pl.pallas_call(
        back_kernel,
        out_shape=[
            jax.ShapeDtypeStruct((total, D), F32),
            jax.ShapeDtypeStruct((total, D), BF),
            jax.ShapeDtypeStruct((total, QW), BF),
            jax.ShapeDtypeStruct((8, D), F32),
        ],
        grid=(rows // bm,),
        in_specs=[later(D), later(D), row(D), row(D), whole((1, D)), whole((QW, D))]
        + [anywhere] * len(filled),
        out_specs=[later(D), later(D), later(QW), whole((8, D))],
        input_output_aliases={6 + n: n for n in range(len(filled))},
        compiler_params=params(),
        cost_estimate=SMALL,
    )(h1, dy, mine, got, g2, wo, *filled)


def layout():
    q_width = HEADS * HEAD_DIM
    kv_width = KV_HEADS * HEAD_DIM
    return [
        (D,),
        (D, q_width),
        (D, kv_width),
        (D, kv_width),
        (HEAD_DIM,),
        (HEAD_DIM,),
        (q_width, D),
        (D,),
        (D, FF),
        (D, FF),
        (FF, D),
    ]


LANES = 128
SHARD = 491592
FLAT_AT = {"g1": 0, "wq": 8, "wk": 16392, "wv": 24584, "gqk": 32776, "wo": 32778,
           "g2": 49162, "wg": 49170, "wu": 73746, "wd": 98322}
PER_ROW = {"wq": 16, "wk": 8, "wv": 8, "wo": 8, "wg": 24, "wu": 24, "wd": 8}


def matrix_kernel(per, split, place, main, extra, out, wide):
    count = main.shape[0]
    wide[:count, :] = main[...].astype(F32)
    wide[count:, :] = extra[...].astype(F32)
    rows = out.shape[0]
    first = place[1]
    if split:
        first = first + place[0] * (out.shape[1] // LANES)
    for at in range(out.shape[1] // LANES):
        cols = slice(at * LANES, (at + 1) * LANES)
        out[:, cols] = wide[pl.ds(first + at, rows, stride=per), :].astype(BF)


def matrix(lanes, name, split, rows, step, core):
    per = PER_ROW[name]
    count = step * per
    at = FLAT_AT[name]
    base = at // count
    width = per * LANES // (CORES if split else 1)
    blocks = (rows if split else rows // CORES) // step
    place = jnp.stack([core, jnp.full_like(core, at - base * count)]).astype(jnp.int32)

    def block(i, place):
        return base + i + (0 if split else place[0] * blocks)

    return pl.pallas_call(
        functools.partial(matrix_kernel, per, split),
        out_shape=jax.ShapeDtypeStruct((blocks * step, width), BF),
        grid_spec=pltpu.PrefetchScalarGridSpec(
            num_scalar_prefetch=1,
            grid=(blocks,),
            in_specs=[
                pl.BlockSpec((count, LANES), lambda i, place: (block(i, place), 0)),
                pl.BlockSpec(
                    (32, LANES), lambda i, place: ((block(i, place) + 1) * (count // 32), 0)
                ),
            ],
            out_specs=pl.BlockSpec((step, width), lambda i, place: (i, 0)),
            scratch_shapes=[pltpu.VMEM((count + 32, LANES), F32)],
        ),
        compiler_params=params(),
        cost_estimate=SMALL,
    )(place, lanes, lanes)


def gain_vectors(flat_vec):
    take = lambda name, skip, size: lax.slice(
        flat_vec, (FLAT_AT[name] * LANES + skip,), (FLAT_AT[name] * LANES + skip + size,)
    )
    gains = take("g1", 0, D), take("g2", 0, D), take("gqk", 0, LANES), take("gqk", LANES, LANES)
    return [gain.astype(F32).reshape(1, -1) for gain in gains]


def plain_grads(
    pick, a, a_far, b, o, hid, dgate, dup, dy, da_out, dq, dk, dv, dg1, dgq, dgk, dg2
):
    a_all = jnp.concatenate([a, a_far])
    grads = [
        dg1,
        t_dot(a, dq),
        t_dot(a_all, jnp.concatenate(dk)),
        t_dot(a_all, jnp.concatenate(dv)),
        jnp.sum(dgq, axis=0),
        jnp.sum(dgk, axis=0),
        t_dot(o, da_out),
        0.5 * dg2,
        t_dot(b, dgate),
        t_dot(b, dup),
        t_dot(hid, dy),
    ]
    flat = []
    for number, (grad, shape) in enumerate(zip(grads, layout())):
        if len(shape) == 2:
            axis = 0 if number in (6, 10) else 1
            blank = jnp.zeros_like(grad)
            grad = jnp.concatenate([pick(grad, blank), pick(blank, grad)], axis=axis)
        flat.append(grad.reshape(-1).astype(F32))
    return lax.psum_scatter(
        jnp.concatenate(flat), ("dp", "seq"), scatter_dimension=0, tiled=True
    )


X_FIRST = ("wq", "wg", "wd")
FEED_PARTS = {
    (1, 0): [("wo", 0, 704)],
    (1, 1): [("wo", 704, 1664)],
    (1, 2): [("wo", 1664, 2048), ("wg", 0, 192)],
    (1, 3): [("wg", 192, 512)],
    (2, 0): [("wg", 512, 832)],
    (2, 1): [("wg", 832, 1024), ("wu", 0, 128)],
    (2, 2): [("wu", 128, 448)],
    (2, 3): [("wu", 448, 768)],
    (3, 0): [("wu", 768, 1024), ("wd", 0, 192)],
    (3, 1): [("wd", 192, 1152)],
    (3, 2): [("wd", 1152, 2112)],
    (3, 3): [("wd", 2112, 3072)],
}
HEAD_PARTS = {0: ("wq", 0, 512), 1: ("wq", 512, 1024), 2: ("wk", 0, 1024), 3: ("wv", 0, 1024)}
TAIL = 288


def plane_pairs(distance, wanted=lambda dp, seq: True):
    pairs = []
    for dp in range(4):
        for seq in range(8):
            to = dp ^ distance
            if wanted(to, seq):
                pairs.append((dp * 8 + seq, to * 8 + seq))
    return pairs


def swap_dp(block, distance):
    return lax.ppermute(block, "dp", [(i, i ^ distance) for i in range(4)])


def cut(block, index, axis=1):
    width = block.shape[axis] // 2
    return lax.dynamic_slice_in_dim(block, index * width, width, axis)


def plane_order(name):
    dp = lax.axis_index("dp")
    order = ((dp % 2, 1), (dp // 2, 2))
    return order if name in X_FIRST else order[::-1]


def plane_step(grad, name, step):
    mine, distance = plane_order(name)[step]
    return cut(grad, mine), swap_dp(cut(grad, 1 - mine), distance)


def kept(*stages):
    return [stage[0] for stage in stages]


def added(stage):
    return (stage[0].astype(F32) + stage[1].astype(F32)).astype(BF)


def line_start(parts):
    low = lax.axis_index("seq") // 2 % 2
    parts = parts.reshape((2, 2) + parts.shape[1:])
    keep = lax.dynamic_index_in_dim(parts, low, 1, keepdims=False)
    send = lax.dynamic_index_in_dim(parts, 1 - low, 1, keepdims=False)
    return keep, xor_seq(send, 2)


def line_next(stage):
    high = lax.axis_index("seq") // 4
    parts = added(stage)
    keep = lax.dynamic_index_in_dim(parts, high, 0, keepdims=False)
    send = lax.dynamic_index_in_dim(parts, 1 - high, 0, keepdims=False)
    return keep, xor_seq(send, 4)


def stack_rows(grad, low, high):
    return [grad[low:high, at : at + LANES] for at in range(0, grad.shape[1], LANES)]


def feed_line(sums):
    spare = jnp.zeros((256, LANES), BF)
    per_line = []
    for z in range(4):
        blocks = [spare] if z == 0 else []
        for d in (1, 2, 3):
            for name, low, high in FEED_PARTS[d, z]:
                blocks += stack_rows(sums[name], low, high)
        per_line.append(jnp.concatenate(blocks))
    return line_start(jnp.stack(per_line))


ROWS = 3872
PART = 176
BEFORE = TAIL * 8


def spread(who, other, core, dp, name, at, rows, into, to):
    per = PER_ROW[name] // 8
    for source, side in ((who, core), (other, 1 - core)):
        for place in range(4):
            chip = (place % 2) * 2 + place // 2 if name in X_FIRST else place
            for col in range(per):
                first = to + side * (4 * per) + place * per + col
                block = source[chip ^ dp, at + col * rows : at + (col + 1) * rows, :]
                into[pl.ds(first, rows, stride=8 * per), :] = block.astype(F32)


def feed_flat_kernel(info, who, other, out):
    core, spot = info[0], info[1]

    @pl.when((spot < 4) | (spot == 4))
    def _():
        out[...] = jnp.zeros_like(out)

    for (d, z), blocks in FEED_PARTS.items():

        @pl.when(spot == d * 4 + z)
        def _(d=d, z=z, blocks=blocks):
            at, to = (256, 2048) if (d, z) == (1, 0) else (0, 0)
            for name, low, high in blocks:
                rows = high - low
                spread(who, other, core, 0, name, at, rows, out, to)
                at += rows * PER_ROW[name] // 8
                to += rows * PER_ROW[name]


def main_row(d, z):
    if (d, z) == (1, 0):
        return FLAT_AT["gqk"]
    name, low, _ = HEAD_PARTS[z] if d == 0 else FEED_PARTS[d, z][0]
    return FLAT_AT[name] + low * PER_ROW[name]


STARTS = [
    (8 * d + 2 * z + c) * SHARD // LANES - (main_row(d, z) - BEFORE)
    for d in range(4)
    for z in range(4)
    for c in range(2)
]
WIDE = max(BEFORE + 8192, (max(STARTS) + ROWS + 16) // 8 * 8)


def adam(grad, master, moment1, moment2):
    moment1_new = BETA_ONE * moment1 + (1.0 - BETA_ONE) * grad
    moment2_new = BETA_TWO * moment2 + (1.0 - BETA_TWO) * grad * grad
    update = moment1_new / CORRECT_ONE / (jnp.sqrt(moment2_new / CORRECT_TWO) + ADAM_EPS)
    return moment1_new, master - LEARN_RATE * (update + DECAY_RATE * master)


def finish_kernel(
    info, who, other, flat, before, gains, master, moment1, moment2,
    grad_out, moment1_out, master_out, block_out, wide, work,
):
    core, spot, start, skip, ahead, rest = [info[i] for i in range(6)]

    def put_before(name, dp):
        spread(who, other, core, dp, name, 1024, TAIL * 8 // PER_ROW[name], wide, 0)

    @pl.when(spot == 0)
    def _():
        wide[BEFORE - 8 : BEFORE, :] = gains[0:8, :]

    @pl.when((spot == 1) | (spot == 2))
    def _():
        put_before("wq", 0)

    @pl.when(spot == 3)
    def _():
        put_before("wk", 0)

    @pl.when(spot == 4)
    def _():
        put_before("wv", 1)
        wide[BEFORE : BEFORE + 2, :] = gains[8:10, :]
        wide[BEFORE + 2 : BEFORE + 2 + 5632, :] = flat[2048:, :]

    @pl.when(spot < 2)
    def _():
        spread(who, other, core, 0, "wq", 0, 512, wide, BEFORE)

    @pl.when((spot == 2) | (spot == 3))
    def _():
        spread(who, other, core, 0, "wk", 0, 1024, wide, BEFORE)

    @pl.when(spot > 4)
    def _():
        wide[BEFORE - 16 : BEFORE, :] = before[...]

    @pl.when(spot == 6)
    def _():
        wide[BEFORE : BEFORE + 3072, :] = flat[:3072, :]
        wide[BEFORE + 3072 : BEFORE + 3080, :] = gains[10:18, :]
        wide[BEFORE + 3080 : BEFORE + 7688, :] = flat[3072:, :]

    @pl.when((spot == 5) | (spot > 6))
    def _():
        wide[BEFORE : BEFORE + 7680, :] = flat[...]

    col = lax.broadcasted_iota(jnp.int32, (PART, LANES), 1)
    row = lax.broadcasted_iota(jnp.int32, (PART, LANES), 0)
    work[0:8, :] = jnp.zeros((8, LANES), F32)
    work[ROWS + 8 :, :] = jnp.zeros((8, LANES), F32)
    turn = lax.rem(LANES - skip, LANES)

    @pl.loop(0, ROWS // PART)
    def _(j):
        at = pl.multiple_of(j * PART, 8)
        here = pl.ds(at, PART)
        now = pltpu.roll(wide[pl.ds(start + at, PART), :], turn, 1)
        after_it = pltpu.roll(wide[pl.ds(start + at + 1, PART), :], turn, 1)
        grad = jnp.where(col < LANES - skip, now, after_it)
        moment1_new, master_new = adam(grad, master[here, :], moment1[here, :], moment2[here, :])
        grad_out[here, :] = grad
        moment1_out[here, :] = moment1_new
        master_out[here, :] = master_new
        inside = (at + row) * LANES + col < SHARD
        work[pl.ds(at + 8, PART), :] = jnp.where(inside, master_new, 0.0)

    @pl.loop(0, ROWS // PART)
    def _(j):
        at = pl.multiple_of(j * PART, 16)
        now = pltpu.roll(work[pl.ds(7 - ahead + at, PART), :], rest, 1)
        after_it = pltpu.roll(work[pl.ds(8 - ahead + at, PART), :], rest, 1)
        block_out[pl.ds(at, PART), :] = jnp.where(col < rest, now, after_it).astype(BF)


def local(kernel, shapes, scratch, info, *arrays):
    vmem = pl.BlockSpec(memory_space=pltpu.VMEM)
    return pl.pallas_call(
        kernel,
        out_shape=shapes,
        in_specs=[pl.BlockSpec(memory_space=pltpu.SMEM)] + [vmem] * len(arrays),
        out_specs=jax.tree.map(lambda _: vmem, shapes),
        scratch_shapes=scratch,
        compiler_params=params(),
        cost_estimate=SMALL,
    )(jnp.stack(info).astype(jnp.int32), *arrays)


def fast_grads(core, feed_stage, head_q, head_kv, gains, states, da, to_home):
    dp = lax.axis_index("dp")
    rank = lax.axis_index("seq")
    line = rank // 2
    spot = dp * 4 + line
    gains = jnp.concatenate(gains).reshape(1, -1, LANES)
    gains = jnp.broadcast_to(gains, (32,) + gains.shape[1:])
    gains = lax.all_to_all(gains, ("dp", "seq"), 0, 0, tiled=True)
    head_q, head_kv = added(head_q), added(head_kv)
    head_stage = line_start(
        jnp.stack(
            [
                jnp.concatenate(stack_rows(head_q, 0, 512)),
                jnp.concatenate(stack_rows(head_q, 512, 1024)),
                head_kv[:1024],
                head_kv[1024:],
            ]
        )
    )
    feed_part = added(feed_stage).reshape(3, 960, LANES)
    feed_part = after(feed_part, head_stage[0])
    feed_got = jnp.concatenate([feed_part[:1], feed_part])
    feed_got = lax.all_to_all(feed_got, "dp", 0, 0, tiled=True)
    head_stage, da, gains = after((head_stage, da, gains))
    head_stage = line_next(head_stage)
    feed_got = after(feed_got, head_stage[0])
    feed_far = xor_seq(feed_got, 1)
    dx_rows = to_home(after(da, head_stage[0]))
    head_part = added(head_stage)
    tail = jnp.where(
        line < 2,
        jnp.concatenate([head_part[512 - TAIL // 2 : 512], head_part[1024 - TAIL // 2 :]]),
        head_part[1024 - TAIL :],
    )
    ring = [(8 * d + s, 8 * d + (s + 2) % 8) for d in range(4) for s in range(8)]
    head_all = jnp.concatenate([head_part, lax.ppermute(tail, ("dp", "seq"), ring)])
    head_got = [head_all]
    for distance in (1, 2, 3):
        pairs = plane_pairs(distance, lambda d, s: d == 0 or (d == 1 and s < 2))
        head_got.append(lax.ppermute(head_all, ("dp", "seq"), pairs))
    feed_flat = local(
        feed_flat_kernel,
        jax.ShapeDtypeStruct((7680, LANES), F32),
        [],
        (core, spot),
        feed_got,
        after(feed_far, head_all),
    )
    chain = [(8 * d + s, 8 * d + s + 2) for d in range(4) for s in range(8) if 8 * d + s < 30]
    before = lax.ppermute(feed_flat[-16:], ("dp", "seq"), chain)
    gains = jnp.sum(gains, axis=0)
    head_got, dx_rows, before = after((head_got, dx_rows, before))
    head_got = jnp.stack(head_got)
    head_far = xor_seq(head_got, 1)

    index = spot * 2 + core
    start = jnp.asarray(STARTS, jnp.int32)[index]
    info = (core, spot, start, index * (SHARD % LANES) % LANES, rank * 72 // LANES, rank * 72 % LANES)
    rows = jax.ShapeDtypeStruct((ROWS, LANES), F32)
    results = local(
        finish_kernel,
        [rows, rows, rows, jax.ShapeDtypeStruct((ROWS, LANES), BF)],
        [pltpu.VMEM((WIDE, LANES), F32), pltpu.VMEM((ROWS + 16, LANES), F32)],
        info, head_got, head_far, feed_flat, before, gains, *states,
    )
    return *results, dx_rows


def gather_weights(block):
    blocks = lax.all_gather(block, "seq", axis=0)
    body, ends = blocks[:, :3840], blocks[:, 3840:3848]
    heads = body[1:, :8] + ends[:-1]
    heads = jnp.concatenate([body[:1, :8], heads])
    rows = jnp.concatenate([heads, body[:, 8:]], axis=1).reshape(-1, LANES)
    rows = jnp.concatenate([rows, ends[-1]])
    return rows.reshape(-1)[: 8 * SHARD]


def norm_back(x, gain, grad):
    r = lax.rsqrt(jnp.mean(x * x, axis=-1, keepdims=True) + EPS_NORM)
    xh = x * r
    dg = grad * gain
    return r * (dg - xh * jnp.mean(dg * xh, axis=-1, keepdims=True))


def gain_sum(x, grad):
    x = x.astype(F32)
    r = lax.rsqrt(jnp.mean(x * x, axis=-1, keepdims=True) + EPS_NORM)
    return jnp.sum(grad.astype(F32) * x * r, axis=0)


def tables(positions):
    half_dim = HEAD_DIM // 2
    frequency = ROPE_BASE ** (-jnp.arange(half_dim, dtype=F32) * 2.0 / HEAD_DIM)
    angles = positions.astype(F32)[:, None] * frequency[None, :]
    cosine, sine = jnp.cos(angles), jnp.sin(angles)
    return jnp.concatenate([cosine, cosine], 1), jnp.concatenate([-sine, sine], 1)


def shards(x_prompt, x_cont, dy_prompt, dy_cont, prompt_pos, weights, master, moment1, moment2):
    count = lax.axis_size("seq")
    rank = lax.axis_index("seq")
    half = count // 2
    side = rank // half
    core = rank % CORES
    chips = half // CORES
    p = x_prompt.shape[1]
    c = x_cont.shape[1]
    prompt_len = p * count
    own_p = 4 * p
    first = core == 0

    def pick(lo, hi):
        return jnp.where(first, lo, hi)

    def share(mine, got):
        return pick(mine, got), pick(got, mine)

    def far_rows(block):
        rows = block[None]
        mask = 2
        while mask < half:
            rows = jnp.concatenate([rows, xor_seq(rows, mask)])
            mask *= 2
        return rows[1:]

    def sides(prompt, cont):
        rows = jnp.concatenate([prompt, cont], axis=1)
        own = lax.dynamic_index_in_dim(rows, side, 0, keepdims=False)
        other = lax.dynamic_index_in_dim(rows, 1 - side, 0, keepdims=False)
        return own, other

    def join(own, recv, own_got, recv_got):
        lo, hi = share(own, own_got)
        lo2, hi2 = share(recv, recv_got)
        rows_p = [lo[:p], lo2[:p], hi[:p], hi2[:p]]
        rows_c = [lo[p:], lo2[p:], hi[p:], hi2[p:]]
        return jnp.concatenate(rows_p + rows_c, axis=0)

    x_own, x_other = sides(x_prompt, x_cont)
    x_recv = xor_seq(x_other, half)
    far_one = far_rows(x_own[:p])
    x_own_got = xor_seq(x_own, 1)

    lanes = weights.reshape(-1, LANES)
    g1, g2, gq, gk = gain_vectors(weights)
    w_q = matrix(lanes, "wq", True, D, 128, core)
    w_k = matrix(lanes, "wk", True, D, 256, core)
    w_v = matrix(lanes, "wv", True, D, 256, core)
    x_recv = after(x_recv, w_q, w_k, w_v)
    far_two = far_rows(x_recv[:p])
    x_recv_got = xor_seq(x_recv, 1)
    far_one = after(far_one, x_recv)
    far_one_got = xor_seq(far_one, 1)
    lanes = after(lanes, x_recv)
    w_g = matrix(lanes, "wg", True, D, 128, core)
    w_u = matrix(lanes, "wu", True, D, 128, core)
    x_recv_got = after(x_recv_got, w_g, w_u)
    x = join(x_own, x_recv, x_own_got, x_recv_got)

    chip_ids = (rank - core) ^ (CORES * jnp.arange(chips)[:, None, None])
    ids = (chip_ids + jnp.arange(CORES)[None, :, None]) ^ (half * jnp.arange(2)[None, None, :])
    own_group = lax.dynamic_index_in_dim(prompt_pos, side, 0, keepdims=False)
    key_pos = jnp.take(own_group.reshape(count, p), ids.reshape(-1), axis=0).reshape(-1)
    quarter = c // 2
    steps = jnp.arange(quarter, dtype=jnp.int32)
    own_half = [
        prompt_len + jnp.concatenate([k * quarter + steps, (3 - k) * quarter + steps])
        for k in range(CORES)
    ]
    cont_pos = jnp.concatenate([own_half[0], own_half[0], own_half[1], own_half[1]])
    seg = jnp.tile(jnp.repeat(jnp.arange(2, dtype=jnp.int32), c), CORES)
    big = 2 * prompt_len + 4 * c
    cont_code = seg * big + cont_pos
    query_pos = jnp.concatenate([key_pos[:own_p], cont_pos])
    cont_q = jnp.stack([cont_code, seg * big])
    pos = {
        "q_col": query_pos[:, None], "q_row": query_pos[None, :],
        "k_col": key_pos[:, None], "k_row": key_pos[None, :],
        "cq_col": cont_q.T, "cq_row": cont_q,
        "ck_col": cont_code[:, None], "ck_row": cont_code[None, :],
    }
    cos_own, sin_own = tables(query_pos)
    cos_far, sin_far = tables(key_pos[own_p:])

    a, q, qraw, k_own, kraw_own, v_own = project(x, g1, cos_own, sin_own, w_q, w_k, w_v, gq, gk, True)
    far_two = after(far_two, a)
    far_two_got = xor_seq(far_two, 1)
    lanes = after(lanes, a)
    w_d = matrix(lanes, "wd", False, FF, 384, core)
    w_o = matrix(lanes, "wo", False, HEADS * HEAD_DIM, 256, core)
    far_two_got = after(far_two_got, w_d, w_o)
    dy_own, dy_other = after(sides(dy_prompt, dy_cont), far_two)
    dy_recv = xor_seq(dy_other, half)
    dy_own_got = xor_seq(dy_own, 1)
    lo, hi = share(far_one, far_one_got)
    lo2, hi2 = share(far_two, far_two_got)
    x_far = jnp.stack([lo, lo2, hi, hi2], axis=1).reshape(-1, D)
    a_far, k_far, kraw_far, v_far = project(x_far, g1, cos_far, sin_far, w_q, w_k, w_v, gq, gk, False)
    rows = x.shape[0]
    o_p, level_p = attend(q, k_own, v_own, k_far, v_far, pos, own_p, False)
    part_p = dot(o_p, w_o).astype(BF)
    part_p_got = xor_seq(part_p, 1)
    q, part_p, dy_recv = after((q, part_p, dy_recv))
    dy_recv_got = xor_seq(dy_recv, 1)
    o_c, level_c = attend(q, k_own, v_own, k_far, v_far, pos, own_p, True)
    o_c, dy_recv_got = after((o_c, dy_recv_got))
    part_c = dot(o_c, w_o).astype(BF)
    part_c_got = xor_seq(part_c, 1)
    part_p_got = after(part_p_got, part_c)
    dy = join(dy_own, dy_recv, dy_own_got, dy_recv_got)
    *filled, y_p, db_p = feed((), 0, rows, x, part_p, part_p_got, dy, g2, w_g, w_u, w_d)
    db_p_got = xor_seq(db_p, 1)
    o = jnp.concatenate([o_p, o_c])
    o_got = xor_seq(o, 1)
    part_c_got, o_got = after((part_c_got, o_got), db_p)
    *filled, y_c, db_c = feed(filled, own_p, rows, x, part_c, part_c_got, dy, g2, w_g, w_u, w_d)
    h1, b, hid, dgate, dup = filled
    db_c_got = xor_seq(db_c, 1)
    hid_got = xor_seq(hid, 1)
    level = jnp.concatenate([level_p, level_c], axis=2)
    y_part = jnp.concatenate([y_p, y_c])
    fast = count == 8 and lax.axis_size("dp") == 4
    def core_rows(rows, which):
        return jnp.concatenate(
            [
                lax.dynamic_slice_in_dim(rows, which * 2 * p, 2 * p),
                lax.dynamic_slice_in_dim(rows, own_p + which * 2 * c, 2 * c),
            ]
        )

    y_got = xor_seq(core_rows(y_part, 1 - core), 1)
    if fast:
        flow = {"wg": plane_step(t_dot(b, dgate).astype(BF), "wg", 0)}
        flow["wu"] = plane_step(t_dot(b, dup).astype(BF), "wu", 0)
        dy_cols = cut(dy, core)
        grad_d = t_dot(hid, dy_cols).astype(BF)
        hid_got, y_got = after((hid_got, y_got), kept(flow["wg"], flow["wu"]))
        grad_d = share(grad_d, t_dot(hid_got, dy_cols).astype(BF))
        flow["wd"] = plane_step(jnp.concatenate(grad_d), "wd", 0)
        db_p_got, db_c_got = after((db_p_got, db_c_got), kept(flow["wd"]))
    y_core = core_rows(h1, core) + core_rows(y_part, core).astype(F32) + y_got.astype(F32)
    *filled, dg2_p = back_norm((), 0, h1, dy, db_p, db_p_got, g2, w_o)
    *filled, dg2_c = back_norm(filled, own_p, h1, dy, db_c, db_c_got, g2, w_o)
    dh1, da_out, d_o = filled
    dg2 = jnp.sum(dg2_p + dg2_c, axis=0)

    filled, waits = (), [y_core]
    back = []
    if fast:
        cols = cut(da_out, core)
        grad_o = share(t_dot(o, cols).astype(BF), t_dot(o_got, cols).astype(BF))
        flow["wo"] = plane_step(jnp.concatenate(grad_o), "wo", 0)
        flow["wg"], flow["wu"] = after((flow["wg"], flow["wu"]), flow["wo"][0])
        for name in ("wg", "wu"):
            flow[name] = plane_step(added(flow[name]), name, 1)
        waits += kept(*flow.values())
    for head in range(KV_HEADS_C):
        *filled, dgq, dgk = attend_back(
            head, filled, waits, q, qraw, d_o, o, level,
            (k_own, v_own, kraw_own), (k_far, v_far, kraw_far),
            (cos_own, sin_own, cos_far, sin_far), gq, gk, pos, own_p,
        )
        waits = []
        back.append((dgq, dgk))
        if head == 2:
            y_rows = after(y_rows, dgq)
            waits = [y_rows[1]]
        if fast and head == 1:
            flow = after(flow, dgq)
            flow["wg"], flow["wu"] = added(flow["wg"]), added(flow["wu"])
            for name in ("wd", "wo"):
                flow[name] = plane_step(added(flow[name]), name, 1)
            waits += [flow["wg"], flow["wu"]] + kept(flow["wd"], flow["wo"])
        if head == 1:
            y_rows = home_start(after(y_core, dgq, waits), half, p, c)
            waits.append(y_rows[0])
        if fast and head == 2:
            flow = after(flow, dgq)
            flow["wd"], flow["wo"] = added(flow["wd"]), added(flow["wo"])
            feed_stage = feed_line(flow)
            waits += kept(feed_stage)
    dq, dk_own, dv_own, dk_far, dv_far = filled
    dgq, dgk = [sum(parts) for parts in zip(*back)]
    y_prompt, y_cont = home_end(y_rows, side, p)

    if fast:
        dq, feed_stage = after((dq, feed_stage))
        head_q = plane_step(t_dot(a, dq).astype(BF), "wq", 0)
        a_all = jnp.concatenate([a, a_far])
        pair = [(dk_own, dk_far), (dv_own, dv_far)]
        pair = [t_dot(a_all, jnp.concatenate(part)).astype(BF) for part in pair]
        head_kv = plane_step(jnp.concatenate(pair), "wk", 0)
        feed_stage = line_next(feed_stage)
        dk_own, dk_far = after((dk_own, dk_far), kept(feed_stage, head_q, head_kv))

    da_far = (dot_t(dk_far, w_k) + dot_t(dv_far, w_v)).astype(BF)
    da_far = da_far.reshape(chips - 1, CORES, 2 * p, D)
    da_own = (dot_t(dq, w_q) + dot_t(dk_own, w_k) + dot_t(dv_own, w_v)).astype(BF)
    far_keep = lax.dynamic_index_in_dim(da_far, core, 1, keepdims=False)
    far_send = lax.dynamic_index_in_dim(da_far, 1 - core, 1, keepdims=False)
    sent = jnp.concatenate([core_rows(da_own, 1 - core), far_send.reshape(-1, D)])
    got = xor_seq(sent, 1)
    dg1 = gain_sum(x, da_own) + gain_sum(x_far, da_far.reshape(-1, D))
    if fast:
        head_q, head_kv, feed_stage = after((head_q, head_kv, feed_stage))
        head_q = plane_step(added(head_q), "wq", 1)
        head_kv = plane_step(added(head_kv), "wk", 1)
        got = after(got, kept(head_q, head_kv))
    mine = core_rows(da_own, core).astype(F32) + got[: rows // 2].astype(F32)
    far_sum = far_keep.astype(F32) + got[rows // 2 :].reshape(far_keep.shape).astype(F32)
    blocks = jnp.concatenate([mine[None, : 2 * p], far_sum])
    mask = half // 2
    while mask > 1:
        near, away = blocks[: mask // 2], blocks[mask // 2 :]
        blocks = near + xor_seq(away.astype(BF), mask).astype(F32)
        mask //= 2
    da = jnp.concatenate([blocks[0], mine[2 * p :]])

    def to_dx(da):
        return core_rows(dh1, core) + norm_back(core_rows(x, core).astype(F32), g1, da)

    if fast:
        gains = [dg1, jnp.sum(dgq, 0), jnp.sum(dgk, 0), 0.5 * dg2]
        states = [
            jnp.concatenate([state, jnp.zeros((ROWS * LANES - SHARD,), F32)]).reshape(ROWS, LANES)
            for state in (master, moment1, moment2)
        ]
        states = after(states, x)
        *results, block, dx_rows = fast_grads(
            core, feed_stage, head_q, head_kv, gains, states, da, lambda da: home_start(to_dx(da), half, p, c)
        )
        weights_new = gather_weights(block)
        grad_shard, moment1_new, master_new = [one.reshape(-1)[:SHARD] for one in results]
    else:
        grad_shard = plain_grads(
            pick, a, a_far, b, o, hid, dgate, dup, dy, da_out, dq,
            (dk_own, dk_far), (dv_own, dv_far), dg1, dgq, dgk, dg2,
        )
        dx_rows = home_start(to_dx(da), half, p, c)
        moment1_new, master_new = adam(grad_shard, master, moment1, moment2)
        weights_new = lax.all_gather(master_new.astype(BF), "seq", axis=0, tiled=True)
    dx_prompt, dx_cont = home_end(dx_rows, side, p)
    return (y_prompt, y_cont, dx_prompt, dx_cont, grad_shard, master_new, moment1_new, weights_new)


def solution(mesh):
    placed = (
        P("dp", "seq", None),
        P("dp", "seq", None),
        P("dp", "seq", None),
        P("dp", "seq", None),
        P("dp", None),
        P(),
        P(("dp", "seq")),
        P(("dp", "seq")),
        P(("dp", "seq")),
    )
    return jax.shard_map(
        shards,
        mesh=mesh,
        in_specs=placed,
        out_specs=(
            P("dp", "seq", None),
            P("dp", "seq", None),
            P("dp", "seq", None),
            P("dp", "seq", None),
            P(("dp", "seq")),
            P(("dp", "seq")),
            P(("dp", "seq")),
            P("dp"),
        ),
        check_vma=False,
    )
```

time: 1060 us -> 790 us (0.75)
  waiting for transfers between devices: 369 us -> 132 us
  Pallas kernels: 222 us -> 317 us
  blocking collectives: 49.4 us -> 0 us
  local copies, waits for them, and re-layouts: 127 us -> 85.3 us
  loops' own time: 25.7 us -> 0 us
  other arithmetic: 113 us -> 96.1 us
    ppermute x22 -> x27, waiting for transfers between devices: 217 us -> 30.3 us  [xor_seq(): return lax.ppermute(block, 'seq', [(i, i ^ mask) for i in range(count)])]
    ppermute x12, waiting for transfers between devices: 128 us -> 11.5 us  [swap_dp(): return lax.ppermute(block, 'dp', [(i, i ^ distance) for i in range(4)])]
    pallas_call x4 -> x15, Pallas kernels: 95.8 us -> 180 us  [the longest x2 55.4 us: attend(): pl.pallas_call(functools.partial(attend_kernel, own_p, oth, cont), out_sh...]
    all_gather x1, waiting for transfers between devices: 0.01 us -> 69 us  [gather_weights(): blocks = lax.all_gather(block, 'seq', axis=0)]
    psum x1 -> x0, blocking collectives: 49.4 us -> none  [fast_grads(): gains = lax.psum(gains, ('dp', 'seq')).reshape(-1, LANES)]
    dynamic_slice x10 -> x1, local copies, waits for them, and re-layouts: 35.8 us -> 0.58 us  [fast_grads(): start = jnp.asarray(STARTS, jnp.int32)[index]]
    reshape x6 -> x3, local copies, waits for them, and re-layouts: 34.5 us -> 3.96 us  [the longest x2 3.89 us: shards(): jnp.concatenate([state, jnp.zeros((ROWS * LANES - SHARD,), F32)])]
    another operation x2 -> x0, loops' own time: 25.7 us -> none  [the longest x1 15.8 us: fast_grads(): lax.switch(place * 2 + core, branches, head_cores, feed_flat, before, gains)]
  transfers between devices with their start and end apart: 43 -> 47, of which waited for: 20 -> 11; matrix products, arithmetic and copies ran while one was open for 26% -> 26% of each run, Pallas kernels for 21% -> 36%
where the time goes in v2:
time: 790 us; the launch traced here: 779 us
  Pallas kernels  317 us (40%)
  waiting for transfers between devices  132 us (17%)
  other arithmetic  96.1 us (12%)
  local copies, waits for them, and re-layouts  85.3 us (11%)
  matrix products  66.7 us (8%)
  starting transfers between devices  65.1 us (8%)
  between operations  16.3 us (2%)
    pallas_call x4, Pallas kernels, attend_back(): pl.pallas_call(functools.partial(attend_back_kernel, own_p, n_oth, chunk)...  116 us
    all_gather x1, waiting for transfers between devices, gather_weights(): blocks = lax.all_gather(block, 'seq', axis=0)  69 us
    pallas_call x2, Pallas kernels, attend(): pl.pallas_call(functools.partial(attend_kernel, own_p, oth, cont), out_sh...  55.4 us
    pallas_call x2, Pallas kernels, feed(): pl.pallas_call(feed_kernel, out_shape=[jax.ShapeDtypeStruct((total, D), F...  46.2 us
    pallas_call x7, Pallas kernels, matrix(): pl.pallas_call(functools.partial(matrix_kernel, per, split), out_shape=ja...  41.4 us
    dot_general x9, matrix products, t_dot(): lax.dot_general(left, right, (((0,), (0,)), ((), ())), preferred_element_...  39.3 us
    ppermute x27, waiting for transfers between devices, xor_seq(): return lax.ppermute(block, 'seq', [(i, i ^ mask) for i in range(count)])  30.3 us
    unnamed x235, local copies, waits for them, and re-layouts  29 us
  transfers between devices with their start and end apart: 47, of which 11 were waited for; matrix products, arithmetic and copies ran while one was open for 26% of the time, Pallas kernels for 36%

profile of v2, /device:TPU:0, one launch (start us, length us, event | category | flops | bytes accessed | tf_op | source)
XLA Modules:
  0.0 779.0 jit_solution(1936114767500486393)
XLA Ops:
  10.9 4.0 collective-permute-start.1
  20.8 4.3 fusion.45
  25.4 3.0 fusion.46
  34.8 3.3 shard_map.162.refs_5_.refs_4_
  39.1 3.3 shard_map.163.refs_6_.refs_5_
  43.4 7.5 shard_map.161.refs_4_
  54.6 8.3 %shard_map.164.wg = bf16[1024,1536]{1,0:T(8,128)(2,1)} custom-call(s32[2]{0:T(128)S(1)} %pad_add_fusion.3.place, bf16[122898,128]{1,0:T(8,128)(2,1)} %bitcast.193, bf16[122898,128]{1,0:T(8,128)(2,1)} %bitcast.194), custom_call_target="tpu_custom_call" | custom-call | flops 1000 | bytes 1000 | tf_op jit(solution)/shard_map/pallas_call | solution.py:558
  62.9 8.2 %shard_map.165.wu = bf16[1024,1536]{1,0:T(8,128)(2,1)} custom-call(s32[2]{0:T(128)S(1)} %pad_add_fusion.3.place, bf16[122898,128]{1,0:T(8,128)(2,1)} %bitcast.195, bf16[122898,128]{1,0:T(8,128)(2,1)} %bitcast.196), custom_call_target="tpu_custom_call" | custom-call | flops 1000 | bytes 1000 | tf_op jit(solution)/shard_map/pallas_call | solution.py:558
  80.1 14.1 %shard_map.166 = (bf16[1536,1024]{1,0:T(8,128)(2,1)}, bf16[1536,1024]{1,0:T(8,128)(2,1)}, bf16[1536,1024]{1,0:T(8,128)(2,1)}, bf16[1536,512]{1,0:T(8,128)(2,1)},...) custom-call(bf16[1536,1024]{1,0:T(8,128)(2,1)} %copy-done.11, f32[1,1024]{1,0:T(1,128)S(1)} %bitcast.181, ...), custom_call_target="tpu_custom_call" | custom-call | flops 1000 | bytes 1000 | tf_op jit(solution)/shard_map/pallas_call | solution.py:136
  97.0 5.6 shard_map.167.wd
  102.6 5.2 shard_map.168.wo
  108.3 4.2 constant_dynamic-update-slice_fusion.39
  115.4 6.8 shard_map.169
  122.1 35.8 %shard_map.170 = (bf16[1024,1024]{1,0:T(8,128)(2,1)}, f32[4,2,1024]{2,1,0:T(2,128)S(1)}) custom-call(bf16[1536,1024]{1,0:T(8,128)(2,1)} %get-tuple-element.163.q, bf16[1536,512]{1,0:T(8,128)(2,1)} %get-tuple-element.152.k_own, bf16[1536,512]{1,0:T(8,128)(2,1)} %get-tuple-element.153.v_own, bf16[1024,512]{1,0:T(8,128)(2,1)} %get-tuple-element.159.k_oth, ...), custom_call_target="tpu_custom_call" | custom-call | flops 1000 | bytes 1000 | tf_op jit(solution)/shard_map/pallas_call | solution.py:195
  158.0 5.3 convolution_convert_fusion.5.part
  165.6 19.6 %shard_map.171 = (bf16[512,1024]{1,0:T(8,128)(2,1)}, f32[4,2,512]{2,1,0:T(2,128)S(1)}) custom-call(bf16[1536,1024]{1,0:T(8,128)(2,1)} %get-tuple-element.163.q, bf16[1536,512]{1,0:T(8,128)(2,1)} %get-tuple-element.152.k_own, bf16[1536,512]{1,0:T(8,128)(2,1)} %get-tuple-element.153.v_own, bf16[1024,512]{1,0:T(8,128)(2,1)} %get-tuple-element.159.k_oth, ...), custom_call_target="tpu_custom_call" | custom-call | flops 1000 | bytes 1000 | tf_op jit(solution)/shard_map/pallas_call | solution.py:195
  194.3 29.1 %shard_map.172 = (f32[1536,1024]{1,0:T(8,128)}, bf16[1536,1024]{1,0:T(8,128)(2,1)}, bf16[1536,1536]{1,0:T(8,128)(2,1)}, bf16[1536,1536]{1,0:T(8,128)(2,1)}, bf16...) custom-call(bf16[1536,1024]{1,0:T(8,128)(2,1)} %copy-done.11, ...), custom_call_target="tpu_custom_call" | custom-call | flops 1000 | bytes 1000 | tf_op jit(solution)/shard_map/pallas_call | solution.py:439
  224.4 17.1 %shard_map.173 = (f32[1536,1024]{1,0:T(8,128)}, bf16[1536,1024]{1,0:T(8,128)(2,1)}, bf16[1536,1536]{1,0:T(8,128)(2,1)}, bf16[1536,1536]{1,0:T(8,128)(2,1)}, bf16...) custom-call(bf16[1536,1024]{1,0:T(8,128)(2,1)} %copy-done.11, ...), custom_call_target="tpu_custom_call", output_to_operand_aliasing={{0}: (8, {}), {1}: (9, {}), {2}: (10, {}), {3}: (11, {}), {... | custom-call | flops 1000 | bytes 1000 | tf_op jit(solution)/shard_map/pallas_call | solution.py:439
  248.3 5.6 convolution_convert_fusion
  253.9 5.4 convolution_convert_fusion.1
  278.7 11.3 %shard_map.174 = (f32[1536,1024]{1,0:T(8,128)}, bf16[1536,1024]{1,0:T(8,128)(2,1)}, bf16[1536,1024]{1,0:T(8,128)(2,1)}, f32[8,1024]{1,0:T(8,128)S(1)}) custom-call(f32[1536,1024]{1,0:T(8,128)} %get-tuple-element.178.h1, bf16[1536,1024]{1,0:T(8,128)(2,1)} %copy-done.14, bf16[1024,1024]{1,0:T(8,128)(2,1)} %get-tuple-element.171.mine, ...), custom_call_target="tpu_custom_call" | custom-call | flops 1000 | bytes 1000 | tf_op jit(solution)/shard_map/pallas_call | solution.py:490
  290.0 6.8 shard_map.175
  296.8 3.4 convolution_convert_fusion.7
  300.2 3.7 broadcast_select_fusion.2
  319.9 29.3 %shard_map.176 = (bf16[1536,1024]{1,0:T(8,128)(2,1)}, bf16[1536,512]{1,0:T(8,128)(2,1)}, bf16[1536,512]{1,0:T(8,128)(2,1)}, bf16[1024,512]{1,0:T(8,128)(2,1)}, b...) custom-call(bf16[1536,1024]{1,0:T(8,128)(2,1)} %get-tuple-element.163.q, ...), custom_call_target="tpu_custom_call" | custom-call | flops 1000 | bytes 1000 | tf_op jit(solution)/shard_map/pallas_call | solution.py:371
  349.2 29.0 %shard_map.177 = (bf16[1536,1024]{1,0:T(8,128)(2,1)}, bf16[1536,512]{1,0:T(8,128)(2,1)}, bf16[1536,512]{1,0:T(8,128)(2,1)}, bf16[1024,512]{1,0:T(8,128)(2,1)}, b...) custom-call(bf16[1536,1024]{1,0:T(8,128)(2,1)} %get-tuple-element.16, ...), custom_call_target="tpu_custom_call", output_to_operand_aliasing={{0}: (23, {}), {1}: (24, {}), {2}: (25, {}), {3}: (26, {}),... | custom-call | flops 1000 | bytes 1000 | tf_op jit(solution)/shard_map/pallas_call | solution.py:371
  396.8 29.1 %shard_map.178 = (bf16[1536,1024]{1,0:T(8,128)(2,1)}, bf16[1536,512]{1,0:T(8,128)(2,1)}, bf16[1536,512]{1,0:T(8,128)(2,1)}, bf16[1024,512]{1,0:T(8,128)(2,1)}, b...) custom-call(bf16[1536,1024]{1,0:T(8,128)(2,1)} %get-tuple-element.16, ...), custom_call_target="tpu_custom_call", output_to_operand_aliasing={{0}: (23, {}), {1}: (24, {}), {2}: (25, {}), {3}: (26, {}),... | custom-call | flops 1000 | bytes 1000 | tf_op jit(solution)/shard_map/pallas_call | solution.py:371
  431.5 29.0 %shard_map.179 = (bf16[1536,1024]{1,0:T(8,128)(2,1)}, bf16[1536,512]{1,0:T(8,128)(2,1)}, bf16[1536,512]{1,0:T(8,128)(2,1)}, bf16[1024,512]{1,0:T(8,128)(2,1)}, b...) custom-call(bf16[1536,1024]{1,0:T(8,128)(2,1)} %get-tuple-element.16, ...), custom_call_target="tpu_custom_call", output_to_operand_aliasing={{0}: (23, {}), {1}: (24, {}), {2}: (25, {}), {3}: (26, {}),... | custom-call | flops 1000 | bytes 1000 | tf_op jit(solution)/shard_map/pallas_call | solution.py:371
  460.5 6.3 fusion.30
  466.9 5.4 fusion.33
  474.8 4.6 fusion.63
  483.6 4.1 convolution_convert_fusion.4
  491.3 4.5 fusion.62
  498.4 8.9 %fusion.1 = (f32[1024]{0:T(1024)S(1)}, bf16[1536,1024]{1,0:T(8,128)(2,1)}) fusion(bf16[1536,1024]{1,0:T(8,128)(2,1)S(1)} %copy-done.13, f32[1536]{0:T(1024)S(1)} %copy-done.81, f32[1536,1024]{1,0:T(8,128)} %fusion.63, f32[1536,1024]{1,0:T(8,128)} %fusion.62, bf16[1536,1024]{1,0:T(8,128)(2,1)S(1)} %copy-done.17, bf16[1024,1024]{1,0:T(8,128)(2,1)S(1)} %copy-done.32), kind=kOutput, calls=%fused_computation.6 | convolution fusion | flops 3233807360 | bytes 24127488 | tf_op jit(solution)/shard_map/dot_general | solution.py:46
  524.0 4.2 all-to-all-start
  528.2 4.4 collective-permute-done.30
  534.0 5.6 collective-permute-done.31
  547.4 21.0 %collective-permute-done.34 = bf16[1,512,1024]{2,1,0:T(8,128)(2,1)S(1)} collective-permute-done((bf16[1,512,1024]{2,1,0:T(8,128)(2,1)S(1)}, bf16[1,512,1024]{2,1,0:T(8,128)(2,1)S(1)}, u32[]{:S(2)}, u32[]{:S(2)}) %collective-permute-start.34) | collective-permute-done | bytes 1048608 | tf_op jit(solution)/shard_map/ppermute | solution.py:55
  570.9 5.2 collective-permute-done.32
  583.3 3.5 all-to-all-start.1
  593.4 3.5 fusion.57
  601.0 20.4 %collective-permute-done.36 = bf16[288,128]{1,0:T(8,128)(2,1)S(1)} collective-permute-done((bf16[288,128]{1,0:T(8,128)(2,1)S(1)}, bf16[288,128]{1,0:T(8,128)(2,1)S(1)}, u32[]{:S(2)}, u32[]{:S(2)}) %collective-permute-start.36) | collective-permute-done | bytes 73760 | tf_op jit(solution)/shard_map/ppermute | solution.py:887
  622.2 4.1 collective-permute-start.37
  635.0 14.7 %collective-permute-start.42 = (f32[16,128]{1,0:T(8,128)S(1)}, f32[16,128]{1,0:T(8,128)S(1)}, u32[]{:S(2)}, u32[]{:S(2)}) collective-permute-start(f32[16,128]{1,0:T(8,128)S(1)} %slice.436), channel_id=1, source_target_pairs={{0,2},{1,3},{2,4},{3,5},{4,6},{5,7},{6,8},{7,9},{8,10},{9,11},{10,... | collective-permute-start | bytes 24584 | tf_op jit(solution)/shard_map/ppermute | solution.py:901
  661.2 16.2 %shard_map.181 = (f32[3872,128]{1,0:T(8,128)}, f32[3872,128]{1,0:T(8,128)}, f32[3872,128]{1,0:T(8,128)}, bf16[3872,128]{1,0:T(8,128)(2,1)}) custom-call(s32[6]{0:T(128)S(1)} %stack.157.info, bf16[4,1312,128]{2,1,0:T(8,128)(2,1)} %pad_maximum_fusion.9.who, bf16[4,1312,128]{2,1,0:T(8,128)(2,1)} %collective-permute-done.43.other, f32[7680,128]{1,0:T(8,128)} %shard_map.180.flat, ...), custom_call_target="tpu_custom_call" | custom-call | flops 1000 | bytes 1000 | tf_op jit(solution)/shard_map/pallas_call | solution.py:841
  691.4 69.0 %all-gather.3.cloned.1.call-done = bf16[30976,128]{1,0:T(8,128)(2,1)} async-done(((bf16[3872,128]{1,0:T(8,128)(2,1)}), bf16[30976,128]{1,0:T(8,128)(2,1)}) %all-gather.3.cloned.1.call-update) | async-done | bytes 7929872 | tf_op jit(solution)/shard_map/all_gather | solution.py:921
  760.4 3.8 slice.445
  766.2 5.7 maximum_bitcast_fusion
  (501 shorter events, 210.2 us)
Async XLA Ops:
  10.9 43.7 %collective-permute-start.1 = (bf16[384,1024]{1,0:T(8,128)(2,1)}, bf16[384,1024]{1,0:T(8,128)(2,1)}, u32[]{:S(2)}, u32[]{:S(2)}) collective-permute-start(bf16[384,1024]{1,0:T(8,128)(2,1)} %get-tuple-element.354), channel_id=1, source_target_pairs={{0,4},{1,5},{2,6},{3,7},{4,0},{5,1},{6,2},{7,3},{8,12},{9,13},{10,... | collective-permute-start | bytes 2359304 | tf_op jit(solution)/shard_map/ppermute | solution.py:55
  14.9 58.7 %collective-permute-start = (bf16[384,1024]{1,0:T(8,128)(2,1)}, bf16[384,1024]{1,0:T(8,128)(2,1)}, u32[]{:S(2)}, u32[]{:S(2)}) collective-permute-start(bf16[384,1024]{1,0:T(8,128)(2,1)} %get-tuple-element.355), channel_id=1, source_target_pairs={{0,1},{1,0},{2,3},{3,2},{4,5},{5,4},{6,7},{7,6},{8,9},{9,8},{10,11... | collective-permute-start | bytes 2359304 | tf_op jit(solution)/shard_map/ppermute | solution.py:55
  15.7 57.9 %collective-permute-start.3 = (bf16[1,256,1024]{2,1,0:T(8,128)(2,1)}, bf16[1,256,1024]{2,1,0:T(8,128)(2,1)}, u32[]{:S(2)}, u32[]{:S(2)}) collective-permute-start(bf16[1,256,1024]{2,1,0:T(8,128)(2,1)} %constant_dynamic-slice_fusion), channel_id=1, source_target_pairs={{0,2},{1,3},{2,0},{3,1},{4,6},{5,7},{6,4},{7,5},{8,10},{9,11},{10,... | collective-permute-start | bytes 1572872 | tf_op jit(solution)/shard_map/ppermute | solution.py:55
  71.1 5.8 collective-permute-start.2
  73.2 21.0 %collective-permute-start.5 = (bf16[1,256,1024]{2,1,0:T(8,128)(2,1)}, bf16[1,256,1024]{2,1,0:T(8,128)(2,1)}, u32[]{:S(2)}, u32[]{:S(2)}) collective-permute-start(bf16[1,256,1024]{2,1,0:T(8,128)(2,1)} %slice_bitcast_fusion.1), channel_id=1, source_target_pairs={{0,2},{1,3},{2,0},{3,1},{4,6},{5,7},{6,4},{7,5},{8,10},{9,11},{10,... | collective-permute-start | bytes 1572872 | tf_op jit(solution)/shard_map/ppermute | solution.py:55
  73.6 2.1 collective-permute-start.4
  94.2 18.3 %collective-permute-start.6 = (bf16[1,256,1024]{2,1,0:T(8,128)(2,1)}, bf16[1,256,1024]{2,1,0:T(8,128)(2,1)S(1)}, u32[]{:S(2)}, u32[]{:S(2)}) collective-permute-start(bf16[1,256,1024]{2,1,0:T(8,128)(2,1)} %collective-permute-done.5), channel_id=1, source_target_pairs={{0,1},{1,0},{2,3},{3,2},{4,5},{5,4},{6,7},{7,6},{8,9},{9,8},{10,11... | collective-permute-start | bytes 1572872 | tf_op jit(solution)/shard_map/ppermute | solution.py:55
  107.8 55.5 %collective-permute-start.7 = (bf16[384,1024]{1,0:T(8,128)(2,1)S(1)}, bf16[384,1024]{1,0:T(8,128)(2,1)}, u32[]{:S(2)}, u32[]{:S(2)}) collective-permute-start(bf16[384,1024]{1,0:T(8,128)(2,1)S(1)} %copy-done.77), channel_id=1, source_target_pairs={{0,4},{1,5},{2,6},{3,7},{4,0},{5,1},{6,2},{7,3},{8,12},{9,13},{10,... | collective-permute-start | bytes 2359304 | tf_op jit(solution)/shard_map/ppermute | solution.py:55
  108.0 79.8 %collective-permute-start.12 = (bf16[384,1024]{1,0:T(8,128)(2,1)}, bf16[384,1024]{1,0:T(8,128)(2,1)}, u32[]{:S(2)}, u32[]{:S(2)}) collective-permute-start(bf16[384,1024]{1,0:T(8,128)(2,1)} %get-tuple-element.169), channel_id=1, source_target_pairs={{0,1},{1,0},{2,3},{3,2},{4,5},{5,4},{6,7},{7,6},{8,9},{9,8},{10,11... | collective-permute-start | bytes 2359304 | tf_op jit(solution)/shard_map/ppermute | solution.py:55
  163.2 21.9 %collective-permute-start.8 = (bf16[384,1024]{1,0:T(8,128)(2,1)}, bf16[384,1024]{1,0:T(8,128)(2,1)}, u32[]{:S(2)}, u32[]{:S(2)}) collective-permute-start(bf16[384,1024]{1,0:T(8,128)(2,1)} %collective-permute-done.7), channel_id=1, source_target_pairs={{0,1},{1,0},{2,3},{3,2},{4,5},{5,4},{6,7},{7,6},{8,9},{9,8},{10,11... | collective-permute-start | bytes 2359304 | tf_op jit(solution)/shard_map/ppermute | solution.py:55
  165.1 27.6 %collective-permute-start.11 = (bf16[1024,1024]{1,0:T(8,128)(2,1)}, bf16[1024,1024]{1,0:T(8,128)(2,1)}, u32[]{:S(2)}, u32[]{:S(2)}) collective-permute-start(bf16[1024,1024]{1,0:T(8,128)(2,1)} %convolution_convert_fusion.5.part), channel_id=1, source_target_pairs={{0,1},{1,0},{2,3},{3,2},{4,5},{5,4},{6,7},{7,6},{8,9},{9,8},{10,11... | collective-permute-start | bytes 6291464 | tf_op jit(solution)/shard_map/ppermute | solution.py:55
  186.5 36.9 %collective-permute-start.10 = (bf16[1536,1024]{1,0:T(8,128)(2,1)S(1)}, bf16[1536,1024]{1,0:T(8,128)(2,1)}, u32[]{:S(2)}, u32[]{:S(2)}) collective-permute-start(bf16[1536,1024]{1,0:T(8,128)(2,1)S(1)} %constant_dynamic-update-slice_fusion.5.o), channel_id=1, source_target_pairs={{0,1},{1,0},{2,3},{3,2},{4,5},{5,4},{6,7},{7,6},{8,9},{9,8},{10,11... | collective-permute-start | bytes 9437192 | tf_op jit(solution)/shard_map/ppermute | solution.py:55
  190.6 32.8 %collective-permute-start.9 = (bf16[512,1024]{1,0:T(8,128)(2,1)S(1)}, bf16[512,1024]{1,0:T(8,128)(2,1)S(1)}, u32[]{:S(2)}, u32[]{:S(2)}) collective-permute-start(bf16[512,1024]{1,0:T(8,128)(2,1)S(1)} %convolution_convert_fusion.8.part), channel_id=1, source_target_pairs={{0,1},{1,0},{2,3},{3,2},{4,5},{5,4},{6,7},{7,6},{8,9},{9,8},{10,11... | collective-permute-start | bytes 3145736 | tf_op jit(solution)/shard_map/ppermute | solution.py:55
  241.5 30.3 %collective-permute-start.13 = (bf16[1536,1536]{1,0:T(8,128)(2,1)}, bf16[1536,1536]{1,0:T(8,128)(2,1)S(1)}, u32[]{:S(2)}, u32[]{:S(2)}) collective-permute-start(bf16[1536,1536]{1,0:T(8,128)(2,1)} %get-tuple-element.181), channel_id=1, source_target_pairs={{0,1},{1,0},{2,3},{3,2},{4,5},{5,4},{6,7},{7,6},{8,9},{9,8},{10,11... | collective-permute-start | bytes 14155784 | tf_op jit(solution)/shard_map/ppermute | solution.py:55
  243.4 33.0 %collective-permute-start.15 = (bf16[1024,1024]{1,0:T(8,128)(2,1)S(1)}, bf16[1024,1024]{1,0:T(8,128)(2,1)S(1)}, u32[]{:S(2)}, u32[]{:S(2)}) collective-permute-start(bf16[1024,1024]{1,0:T(8,128)(2,1)S(1)} %copy-done.56), channel_id=1, source_target_pairs={{0,1},{1,0},{2,3},{3,2},{4,5},{5,4},{6,7},{7,6},{8,9},{9,8},{10,11... | collective-permute-start | bytes 6291464 | tf_op jit(solution)/shard_map/ppermute | solution.py:55
  246.0 24.2 %collective-permute-start.14 = (bf16[768,1024]{1,0:T(8,128)(2,1)S(1)}, bf16[768,1024]{1,0:T(8,128)(2,1)S(1)}, u32[]{:S(2)}, u32[]{:S(2)}) collective-permute-start(bf16[768,1024]{1,0:T(8,128)(2,1)S(1)} %pad_maximum_fusion.5), channel_id=1, source_target_pairs={{0,1},{1,0},{2,3},{3,2},{4,5},{5,4},{6,7},{7,6},{8,9},{9,8},{10,11... | collective-permute-start | bytes 4718600 | tf_op jit(solution)/shard_map/ppermute | solution.py:55
  259.4 17.0 %collective-permute-start.16 = (bf16[512,1024]{1,0:T(8,128)(2,1)S(1)}, bf16[512,1024]{1,0:T(8,128)(2,1)S(1)}, u32[]{:S(2)}, u32[]{:S(2)}) collective-permute-start(bf16[512,1024]{1,0:T(8,128)(2,1)S(1)} %copy-done.8), channel_id=1, source_target_pairs={{0,1},{1,0},{2,3},{3,2},{4,5},{5,4},{6,7},{7,6},{8,9},{9,8},{10,11... | collective-permute-start | bytes 3145736 | tf_op jit(solution)/shard_map/ppermute | solution.py:55
  261.5 43.9 %collective-permute-start.18 = (bf16[1024,768]{1,0:T(8,128)(2,1)}, bf16[1024,768]{1,0:T(8,128)(2,1)}, u32[]{:S(2)}, u32[]{:S(2)}) collective-permute-start(bf16[1024,768]{1,0:T(8,128)(2,1)} %get-tuple-element.314), channel_id=1, source_target_pairs={{0,16},{8,24},{16,0},{24,8},{1,17},{9,25},{17,1},{25,9},{2,18},{10... | collective-permute-start | bytes 4718600 | tf_op jit(solution)/shard_map/ppermute | solution.py:645
  270.3 36.7 %collective-permute-start.17 = (bf16[1024,768]{1,0:T(8,128)(2,1)}, bf16[1024,768]{1,0:T(8,128)(2,1)}, u32[]{:S(2)}, u32[]{:S(2)}) collective-permute-start(bf16[1024,768]{1,0:T(8,128)(2,1)} %get-tuple-element.316), channel_id=1, source_target_pairs={{0,8},{8,0},{16,24},{24,16},{1,9},{9,1},{17,25},{25,17},{2,10},{10... | collective-permute-start | bytes 4718600 | tf_op jit(solution)/shard_map/ppermute | solution.py:645
  307.0 72.9 %collective-permute-start.19 = (bf16[3072,256]{1,0:T(8,128)(2,1)}, bf16[3072,256]{1,0:T(8,128)(2,1)}, u32[]{:S(2)}, u32[]{:S(2)}) collective-permute-start(bf16[3072,256]{1,0:T(8,128)(2,1)} %get-tuple-element.312), channel_id=1, source_target_pairs={{0,8},{8,0},{16,24},{24,16},{1,9},{9,1},{17,25},{25,17},{2,10},{10... | collective-permute-start | bytes 4718600 | tf_op jit(solution)/shard_map/ppermute | solution.py:645
  311.7 68.1 %collective-permute-start.22 = (bf16[1024,384]{1,0:T(8,128)(2,1)}, bf16[1024,384]{1,0:T(8,128)(2,1)}, u32[]{:S(2)}, u32[]{:S(2)}) collective-permute-start(bf16[1024,384]{1,0:T(8,128)(2,1)} %get-tuple-element.340), channel_id=1, source_target_pairs={{0,8},{8,0},{16,24},{24,16},{1,9},{9,1},{17,25},{25,17},{2,10},{10... | collective-permute-start | bytes 2359304 | tf_op jit(solution)/shard_map/ppermute | solution.py:645
  312.2 67.7 %collective-permute-start.21 = (bf16[2048,256]{1,0:T(8,128)(2,1)}, bf16[2048,256]{1,0:T(8,128)(2,1)}, u32[]{:S(2)}, u32[]{:S(2)}) collective-permute-start(bf16[2048,256]{1,0:T(8,128)(2,1)} %get-tuple-element.334), channel_id=1, source_target_pairs={{0,16},{8,24},{16,0},{24,8},{1,17},{9,25},{17,1},{25,9},{2,18},{10... | collective-permute-start | bytes 3145736 | tf_op jit(solution)/shard_map/ppermute | solution.py:645
  316.1 63.7 %collective-permute-start.20 = (bf16[1024,384]{1,0:T(8,128)(2,1)}, bf16[1024,384]{1,0:T(8,128)(2,1)}, u32[]{:S(2)}, u32[]{:S(2)}) collective-permute-start(bf16[1024,384]{1,0:T(8,128)(2,1)} %get-tuple-element.342), channel_id=1, source_target_pairs={{0,16},{8,24},{16,0},{24,8},{1,17},{9,25},{17,1},{25,9},{2,18},{10... | collective-permute-start | bytes 2359304 | tf_op jit(solution)/shard_map/ppermute | solution.py:645
  319.9 58.3 %slice-start.4 = ((s8[6291456]{0:T(1024)(128)(4,1)}), s8[4194304]{0:T(1024)(128)(4,1)S(1)}, s32[]{:S(2)}) async-start(s8[6291456]{0:T(1024)(128)(4,1)} %bitcast.209), calls=%async_computation.7 | async-start | bytes 8388608
  382.4 43.6 %collective-permute-start.25 = (bf16[2048,128]{1,0:T(8,128)(2,1)}, bf16[2048,128]{1,0:T(8,128)(2,1)}, u32[]{:S(2)}, u32[]{:S(2)}) collective-permute-start(bf16[2048,128]{1,0:T(8,128)(2,1)} %get-tuple-element.360), channel_id=1, source_target_pairs={{0,8},{8,0},{16,24},{24,16},{1,9},{9,1},{17,25},{25,17},{2,10},{10... | collective-permute-start | bytes 1572872 | tf_op jit(solution)/shard_map/ppermute | solution.py:645
  387.1 38.9 %collective-permute-start.24 = (bf16[3072,128]{1,0:T(8,128)(2,1)}, bf16[3072,128]{1,0:T(8,128)(2,1)S(1)}, u32[]{:S(2)}, u32[]{:S(2)}) collective-permute-start(bf16[3072,128]{1,0:T(8,128)(2,1)} %get-tuple-element.338), channel_id=1, source_target_pairs={{0,16},{8,24},{16,0},{24,8},{1,17},{9,25},{17,1},{25,9},{2,18},{10... | collective-permute-start | bytes 2359304 | tf_op jit(solution)/shard_map/ppermute | solution.py:645
  393.0 34.7 %collective-permute-start.23 = (bf16[384,1024]{1,0:T(8,128)(2,1)S(1)}, bf16[384,1024]{1,0:T(8,128)(2,1)S(1)}, u32[]{:S(2)}, u32[]{:S(2)}) collective-permute-start(bf16[384,1024]{1,0:T(8,128)(2,1)S(1)} %pad_maximum_fusion.16), channel_id=1, source_target_pairs={{0,4},{1,5},{2,6},{3,7},{4,0},{5,1},{6,2},{7,3},{8,12},{9,13},{10,... | collective-permute-start | bytes 2359304 | tf_op jit(solution)/shard_map/ppermute | solution.py:55
  429.9 49.5 %collective-permute-start.26 = (bf16[2,2880,128]{2,1,0:T(8,128)(2,1)S(1)}, bf16[2,2880,128]{2,1,0:T(8,128)(2,1)S(1)}, u32[]{:S(2)}, u32[]{:S(2)}) collective-permute-start(bf16[2,2880,128]{2,1,0:T(8,128)(2,1)S(1)} %get-tuple-element.324), channel_id=1, source_target_pairs={{0,2},{1,3},{2,0},{3,1},{4,6},{5,7},{6,4},{7,5},{8,10},{9,11},{10,... | collective-permute-start | bytes 4423688 | tf_op jit(solution)/shard_map/ppermute | solution.py:55
  473.8 41.3 %collective-permute-start.28 = (bf16[2048,256]{1,0:T(8,128)(2,1)}, bf16[2048,256]{1,0:T(8,128)(2,1)}, u32[]{:S(2)}, u32[]{:S(2)}) collective-permute-start(bf16[2048,256]{1,0:T(8,128)(2,1)} %get-tuple-element.330), channel_id=1, source_target_pairs={{0,16},{8,24},{16,0},{24,8},{1,17},{9,25},{17,1},{25,9},{2,18},{10... | collective-permute-start | bytes 3145736 | tf_op jit(solution)/shard_map/ppermute | solution.py:645
  481.1 34.5 %collective-permute-start.29 = (bf16[2880,128]{1,0:T(8,128)(2,1)}, bf16[2880,128]{1,0:T(8,128)(2,1)}, u32[]{:S(2)}, u32[]{:S(2)}) collective-permute-start(bf16[2880,128]{1,0:T(8,128)(2,1)} %get-tuple-element.356), channel_id=1, source_target_pairs={{0,4},{1,5},{2,6},{3,7},{4,0},{5,1},{6,2},{7,3},{8,12},{9,13},{10,... | collective-permute-start | bytes 2211848 | tf_op jit(solution)/shard_map/ppermute | solution.py:55
  489.3 26.3 %collective-permute-start.27 = (bf16[1024,512]{1,0:T(8,128)(2,1)}, bf16[1024,512]{1,0:T(8,128)(2,1)}, u32[]{:S(2)}, u32[]{:S(2)}) collective-permute-start(bf16[1024,512]{1,0:T(8,128)(2,1)} %get-tuple-element.332), channel_id=1, source_target_pairs={{0,8},{8,0},{16,24},{24,16},{1,9},{9,1},{17,25},{25,17},{2,10},{10... | collective-permute-start | bytes 3145736 | tf_op jit(solution)/shard_map/ppermute | solution.py:645
  513.9 26.8 %collective-permute-start.33 = (bf16[1280,1024]{1,0:T(8,128)(2,1)}, bf16[1280,1024]{1,0:T(8,128)(2,1)}, u32[]{:S(2)}, u32[]{:S(2)}) collective-permute-start(bf16[1280,1024]{1,0:T(8,128)(2,1)} %pad_maximum_fusion.3), channel_id=1, source_target_pairs={{0,1},{1,0},{2,3},{3,2},{4,5},{5,4},{6,7},{7,6},{8,9},{9,8},{10,11... | collective-permute-start | bytes 7864328 | tf_op jit(solution)/shard_map/ppermute | solution.py:55
  518.0 14.6 %collective-permute-start.30 = (bf16[1024,256]{1,0:T(8,128)(2,1)}, bf16[1024,256]{1,0:T(8,128)(2,1)}, u32[]{:S(2)}, u32[]{:S(2)}) collective-permute-start(bf16[1024,256]{1,0:T(8,128)(2,1)} %constant_dynamic-slice_fusion.11), channel_id=1, source_target_pairs={{0,16},{8,24},{16,0},{24,8},{1,17},{9,25},{17,1},{25,9},{2,18},{10... | collective-permute-start | bytes 1572872 | tf_op jit(solution)/shard_map/ppermute | solution.py:645
  522.5 17.0 %collective-permute-start.31 = (bf16[2048,128]{1,0:T(8,128)(2,1)}, bf16[2048,128]{1,0:T(8,128)(2,1)}, u32[]{:S(2)}, u32[]{:S(2)}) collective-permute-start(bf16[2048,128]{1,0:T(8,128)(2,1)} %constant_dynamic-slice_fusion.9), channel_id=1, source_target_pairs={{0,8},{8,0},{16,24},{24,16},{1,9},{9,1},{17,25},{25,17},{2,10},{10... | collective-permute-start | bytes 1572872 | tf_op jit(solution)/shard_map/ppermute | solution.py:645
  524.0 47.0 %all-to-all-start = ((f32[32,18,128]{2,1,0:T(8,128)}), f32[32,18,128]{2,1,0:T(8,128)}, u32[]{:S(2)}, u32[]{:S(2)}) async-start(f32[32,18,128]{2,1,0:T(8,128)} %broadcast_in_dim.62), calls=%async_computation | async-start | bytes 786432 | tf_op jit(solution)/shard_map/all_to_all | solution.py:859
  542.3 26.2 %collective-permute-start.34 = (bf16[1,512,1024]{2,1,0:T(8,128)(2,1)S(1)}, bf16[1,512,1024]{2,1,0:T(8,128)(2,1)S(1)}, u32[]{:S(2)}, u32[]{:S(2)}) collective-permute-start(bf16[1,512,1024]{2,1,0:T(8,128)(2,1)S(1)} %fusion.40), channel_id=1, source_target_pairs={{0,2},{1,3},{2,0},{3,1},{4,6},{5,7},{6,4},{7,5},{8,10},{9,11},{10,... | collective-permute-start | bytes 3145736 | tf_op jit(solution)/shard_map/ppermute | solution.py:55
  543.5 32.7 %collective-permute-start.32 = (bf16[2,1024,128]{2,1,0:T(8,128)(2,1)}, bf16[2,1024,128]{2,1,0:T(8,128)(2,1)S(1)}, u32[]{:S(2)}, u32[]{:S(2)}) collective-permute-start(bf16[2,1024,128]{2,1,0:T(8,128)(2,1)} %get-tuple-element.358), channel_id=1, source_target_pairs={{0,2},{1,3},{2,0},{3,1},{4,6},{5,7},{6,4},{7,5},{8,10},{9,11},{10,... | collective-permute-start | bytes 1572872 | tf_op jit(solution)/shard_map/ppermute | solution.py:55
  578.2 11.5 %collective-permute-start.35 = (bf16[1024,128]{1,0:T(8,128)(2,1)S(1)}, bf16[1024,128]{1,0:T(8,128)(2,1)}, u32[]{:S(2)}, u32[]{:S(2)}) collective-permute-start(bf16[1024,128]{1,0:T(8,128)(2,1)S(1)} %dynamic-slice_bitcast_fusion.11), channel_id=1, source_target_pairs={{0,4},{1,5},{2,6},{3,7},{4,0},{5,1},{6,2},{7,3},{8,12},{9,13},{10,... | collective-permute-start | bytes 786440 | tf_op jit(solution)/shard_map/ppermute | solution.py:55
  583.3 14.5 %all-to-all-start.1 = ((bf16[4,960,128]{2,1,0:T(8,128)(2,1)}), bf16[4,960,128]{2,1,0:T(8,128)(2,1)S(1)}, u32[]{:S(2)}, u32[]{:S(2)}) async-start(bf16[4,960,128]{2,1,0:T(8,128)(2,1)} %pad_maximum_fusion.13), calls=%async_computation.1 | async-start | bytes 1966080 | tf_op jit(solution)/shard_map/all_to_all | solution.py:874
  586.8 173.6 %all-gather.3.cloned.1.call-start = ((), (), s32[]{:S(2)}) async-start(), calls=%async_computation.2 | async-start | bytes 8921088 | tf_op jit(solution)/shard_map/all_gather | solution.py:921
  597.8 33.6 %collective-permute-start.41 = (bf16[4,960,128]{2,1,0:T(8,128)(2,1)S(1)}, bf16[4,960,128]{2,1,0:T(8,128)(2,1)S(1)}, u32[]{:S(2)}, u32[]{:S(2)}) collective-permute-start(bf16[4,960,128]{2,1,0:T(8,128)(2,1)S(1)} %all-to-all-done.1.who), channel_id=1, source_target_pairs={{0,1},{1,0},{2,3},{3,2},{4,5},{5,4},{6,7},{7,6},{8,9},{9,8},{10,11... | collective-permute-start | bytes 2949128 | tf_op jit(solution)/shard_map/ppermute | solution.py:55
  598.7 52.3 %collective-permute-start.40 = (bf16[384,1024]{1,0:T(8,128)(2,1)}, bf16[384,1024]{1,0:T(8,128)(2,1)}, u32[]{:S(2)}, u32[]{:S(2)}) collective-permute-start(bf16[384,1024]{1,0:T(8,128)(2,1)} %pad_maximum_fusion.17), channel_id=1, source_target_pairs={{0,4},{1,5},{2,6},{3,7},{4,0},{5,1},{6,2},{7,3},{8,12},{9,13},{10,... | collective-permute-start | bytes 2359304 | tf_op jit(solution)/shard_map/ppermute | solution.py:55
  599.4 22.0 %collective-permute-start.36 = (bf16[288,128]{1,0:T(8,128)(2,1)S(1)}, bf16[288,128]{1,0:T(8,128)(2,1)S(1)}, u32[]{:S(2)}, u32[]{:S(2)}) collective-permute-start(bf16[288,128]{1,0:T(8,128)(2,1)S(1)} %slice_select_fusion), channel_id=1, source_target_pairs={{0,2},{1,3},{2,4},{3,5},{4,6},{5,7},{6,0},{7,1},{8,10},{9,11},{10,... | collective-permute-start | bytes 221192 | tf_op jit(solution)/shard_map/ppermute | solution.py:887
  622.2 28.9 %collective-permute-start.37 = (bf16[1312,128]{1,0:T(8,128)(2,1)}, bf16[1312,128]{1,0:T(8,128)(2,1)S(1)}, u32[]{:S(2)}, u32[]{:S(2)}) collective-permute-start(bf16[1312,128]{1,0:T(8,128)(2,1)} %pad_maximum_fusion.20), channel_id=1, source_target_pairs={{0,8},{1,9},{8,0},{9,1},{10,2},{11,3},{12,4},{13,5},{14,6},{15,7}} | collective-permute-start | bytes 1007624 | tf_op jit(solution)/shard_map/ppermute | solution.py:891
  626.3 24.7 %collective-permute-start.38 = (bf16[1312,128]{1,0:T(8,128)(2,1)}, bf16[1312,128]{1,0:T(8,128)(2,1)}, u32[]{:S(2)}, u32[]{:S(2)}) collective-permute-start(bf16[1312,128]{1,0:T(8,128)(2,1)} %pad_maximum_fusion.20), channel_id=1, source_target_pairs={{16,0},{17,1},{18,2},{19,3},{20,4},{21,5},{22,6},{23,7},{24,8},{25... | collective-permute-start | bytes 1007624 | tf_op jit(solution)/shard_map/ppermute | solution.py:891
  627.6 23.4 %collective-permute-start.39 = (bf16[1312,128]{1,0:T(8,128)(2,1)}, bf16[1312,128]{1,0:T(8,128)(2,1)}, u32[]{:S(2)}, u32[]{:S(2)}) collective-permute-start(bf16[1312,128]{1,0:T(8,128)(2,1)} %pad_maximum_fusion.20), channel_id=1, source_target_pairs={{16,8},{17,9},{24,0},{25,1},{26,2},{27,3},{28,4},{29,5},{30,6},{31... | collective-permute-start | bytes 1007624 | tf_op jit(solution)/shard_map/ppermute | solution.py:891
  635.0 16.0 %collective-permute-start.42 = (f32[16,128]{1,0:T(8,128)S(1)}, f32[16,128]{1,0:T(8,128)S(1)}, u32[]{:S(2)}, u32[]{:S(2)}) collective-permute-start(f32[16,128]{1,0:T(8,128)S(1)} %slice.436), channel_id=1, source_target_pairs={{0,2},{1,3},{2,4},{3,5},{4,6},{5,7},{6,8},{7,9},{8,10},{9,11},{10,... | collective-permute-start | bytes 24584 | tf_op jit(solution)/shard_map/ppermute | solution.py:901
  653.5 7.7 collective-permute-start.43
  (94 other events, 713.7 us)
Sparse Core Ops, SparseCore 0:
  677.5 82.8 all-gather.2

commit v3 on v2

--- a/solution.py
+++ b/solution.py
@@ -48,6 +48,10 @@
 
 def t_dot(left, right):
     return lax.dot_general(left, right, (((0,), (0,)), ((), ())), preferred_element_type=F32)
+
+
+def turned(block):
+    return block.astype(F32).T.astype(BF)
 
 
 def xor_seq(block, mask):
@@ -184,16 +188,77 @@
     run(1 if cont else 0)
 
 
-def attend(q, k_own, v_own, k_oth, v_oth, pos, own_p, cont, bq=256):
+def attend_wide_kernel(
+    own_p, oth, cont, q, k_own, v_own, k_oth, v_oth, qpos, kpos, cqc, ckc,
+    o_out, l_out, vt_own, vt_oth,
+):
+    bq = q.shape[0]
+
+    @pl.when(pl.program_id(1) == 0)
+    def _():
+        vt_own[...] = turned(v_own[...])
+        vt_oth[...] = turned(v_oth[...])
+
+    def twice(row):
+        return jnp.concatenate([row] * GROUP, axis=1)
+
+    heads = [slice(g * HEAD_DIM, (g + 1) * HEAD_DIM) for g in range(GROUP)]
+    q2 = jnp.concatenate([q[:, c] for c in heads], axis=0)
+    parts = [(dot_t(k_own[:own_p, :], q2), vt_own[:, :own_p])]
+    parts.append((dot_t(k_oth[...], q2), vt_oth[...]))
+    if cont:
+        s = dot_t(k_own[own_p:, :], q2)
+        code, lowest = twice(cqc[0:1, :]), twice(cqc[1:2, :])
+        ok = (ckc[...] <= code) & (ckc[...] >= lowest)
+        parts.append((jnp.where(ok, s, -1e30), vt_own[:, own_p:]))
+    else:
+        at = 0
+        for n, (s, v) in enumerate(parts):
+            ok = kpos[at : at + s.shape[0], :] <= twice(qpos[...])
+            parts[n] = (jnp.where(ok, s, -1e30), v)
+            at += s.shape[0]
+    top = functools.reduce(jnp.maximum, [jnp.max(s, axis=0, keepdims=True) for s, _ in parts])
+    total = jnp.zeros((1, GROUP * bq), F32)
+    acc = jnp.zeros((HEAD_DIM, GROUP * bq), F32)
+    for s, v in parts:
+        e = jnp.exp2(s - top)
+        total += jnp.sum(e, axis=0, keepdims=True)
+        acc += dot(v, e.astype(BF))
+    level = top + jnp.log2(total)
+    out = acc / total
+    for g, c in enumerate(heads):
+        rows = slice(g * bq, (g + 1) * bq)
+        o_out[:, c] = out[:, rows].T.astype(BF)
+        l_out[0, g : g + 1, :] = level[:, rows]
+
+
+def attend(q, k_own, v_own, k_oth, v_oth, pos, own_p, cont):
     rows = q.shape[0]
     oth = k_oth.shape[0]
     keys = own_p + oth
+    bq = 256 if cont else min(512, own_p)
     base = own_p // bq if cont else 0
     here = rows - own_p if cont else own_p
     head_col = lambda n: pl.BlockSpec((n, HEAD_DIM), lambda h, i: (0, h))
-    cont_block = lambda h, i: (i if cont else 0, 0)
+    if cont:
+        masks = [
+            pl.BlockSpec((bq, 1), lambda h, i: (base + i, 0)),
+            whole((1, keys)),
+            pl.BlockSpec((bq, 2), lambda h, i: (i, 0)),
+            whole((1, rows - own_p)),
+        ]
+        names, scratch = ("q_col", "k_row", "cq_col", "ck_row"), []
+    else:
+        masks = [
+            pl.BlockSpec((1, bq), lambda h, i: (0, i)),
+            whole((keys, 1)),
+            whole((2, rows - own_p)),
+            whole((rows - own_p, 1)),
+        ]
+        names = ("q_row", "k_col", "cq_row", "ck_col")
+        scratch = [pltpu.VMEM((HEAD_DIM, rows), BF), pltpu.VMEM((HEAD_DIM, oth), BF)]
     return pl.pallas_call(
-        functools.partial(attend_kernel, own_p, oth, cont),
+        functools.partial(attend_kernel if cont else attend_wide_kernel, own_p, oth, cont),
         out_shape=[
             jax.ShapeDtypeStruct((here, QW), BF),
             jax.ShapeDtypeStruct((KV_HEADS_C, GROUP, here), F32),
@@ -205,18 +270,16 @@
             head_col(rows),
             head_col(oth),
             head_col(oth),
-            pl.BlockSpec((bq, 1), lambda h, i: (base + i, 0)),
-            whole((1, keys)),
-            pl.BlockSpec((bq, 2), cont_block),
-            whole((1, rows - own_p)),
+            *masks,
         ],
         out_specs=[
             pl.BlockSpec((bq, GROUP * HEAD_DIM), lambda h, i: (i, h)),
             pl.BlockSpec((1, GROUP, bq), lambda h, i: (h, 0, i)),
         ],
+        scratch_shapes=scratch,
         compiler_params=params(),
         cost_estimate=SMALL,
-    )(q, k_own, v_own, k_oth, v_oth, pos["q_col"], pos["k_row"], pos["cq_col"], pos["ck_row"])
+    )(q, k_own, v_own, k_oth, v_oth, *[pos[name] for name in names])
 
 
 def attend_back_kernel(
@@ -857,7 +920,13 @@
     gains = jnp.concatenate(gains).reshape(1, -1, LANES)
     gains = jnp.broadcast_to(gains, (32,) + gains.shape[1:])
     gains = lax.all_to_all(gains, ("dp", "seq"), 0, 0, tiled=True)
+    feed_part = added(feed_stage).reshape(3, 960, LANES)
+    feed_part = after(feed_part, kept(head_q, head_kv))
+
+    feed_got = jnp.concatenate([feed_part[:1], feed_part])
+    feed_got = lax.all_to_all(feed_got, "dp", 0, 0, tiled=True)
     head_q, head_kv = added(head_q), added(head_kv)
+    head_q, head_kv, da = after((head_q, head_kv, da))
     head_stage = line_start(
         jnp.stack(
             [
@@ -868,39 +937,33 @@
             ]
         )
     )
-    feed_part = added(feed_stage).reshape(3, 960, LANES)
-    feed_part = after(feed_part, head_stage[0])
-    feed_got = jnp.concatenate([feed_part[:1], feed_part])
-    feed_got = lax.all_to_all(feed_got, "dp", 0, 0, tiled=True)
-    head_stage, da, gains = after((head_stage, da, gains))
-    head_stage = line_next(head_stage)
-    feed_got = after(feed_got, head_stage[0])
-    feed_far = xor_seq(feed_got, 1)
-    dx_rows = to_home(after(da, head_stage[0]))
-    head_part = added(head_stage)
+    feed_flat = local(
+        feed_flat_kernel,
+        jax.ShapeDtypeStruct((7680, LANES), F32),
+        [],
+        (core, spot),
+        feed_got,
+        xor_seq(feed_got, 1),
+    )
+    chain = [(8 * d + s, 8 * d + s + 2) for d in range(4) for s in range(8) if 8 * d + s < 30]
+    before = lax.ppermute(feed_flat[-16:], ("dp", "seq"), chain)
+    head_stage, gains, before = after((head_stage, gains, before))
+    head_part = added(line_next(head_stage))
     tail = jnp.where(
         line < 2,
         jnp.concatenate([head_part[512 - TAIL // 2 : 512], head_part[1024 - TAIL // 2 :]]),
         head_part[1024 - TAIL :],
     )
     ring = [(8 * d + s, 8 * d + (s + 2) % 8) for d in range(4) for s in range(8)]
-    head_all = jnp.concatenate([head_part, lax.ppermute(tail, ("dp", "seq"), ring)])
+    tail = lax.ppermute(tail, ("dp", "seq"), ring)
+    tail, da = after((tail, da))
+    dx_rows = to_home(da)
+    head_all = after(jnp.concatenate([head_part, tail]), dx_rows[0])
     head_got = [head_all]
     for distance in (1, 2, 3):
         pairs = plane_pairs(distance, lambda d, s: d == 0 or (d == 1 and s < 2))
         head_got.append(lax.ppermute(head_all, ("dp", "seq"), pairs))
-    feed_flat = local(
-        feed_flat_kernel,
-        jax.ShapeDtypeStruct((7680, LANES), F32),
-        [],
-        (core, spot),
-        feed_got,
-        after(feed_far, head_all),
-    )
-    chain = [(8 * d + s, 8 * d + s + 2) for d in range(4) for s in range(8) if 8 * d + s < 30]
-    before = lax.ppermute(feed_flat[-16:], ("dp", "seq"), chain)
     gains = jnp.sum(gains, axis=0)
-    head_got, dx_rows, before = after((head_got, dx_rows, before))
     head_got = jnp.stack(head_got)
     head_far = xor_seq(head_got, 1)
 
@@ -914,6 +977,7 @@
         [pltpu.VMEM((WIDE, LANES), F32), pltpu.VMEM((ROWS + 16, LANES), F32)],
         info, head_got, head_far, feed_flat, before, gains, *states,
     )
+    results, dx_rows = after((results, dx_rows))
     return *results, dx_rows
 
 
@@ -934,10 +998,39 @@
     return r * (dg - xh * jnp.mean(dg * xh, axis=-1, keepdims=True))
 
 
-def gain_sum(x, grad):
-    x = x.astype(F32)
-    r = lax.rsqrt(jnp.mean(x * x, axis=-1, keepdims=True) + EPS_NORM)
-    return jnp.sum(grad.astype(F32) * x * r, axis=0)
+def into_kernel(count, *refs):
+    grads, weights = refs[:count], refs[count : 2 * count]
+    x, out, gain_out = refs[2 * count :]
+    total = None
+    for grad, weight in zip(grads, weights):
+        part = dot_t(grad[...], weight[...])
+        total = part if total is None else total + part
+    out[...] = total.astype(BF)
+    xv = x[...].astype(F32)
+    xh = xv * lax.rsqrt(jnp.mean(xv * xv, axis=-1, keepdims=True) + EPS_NORM)
+
+    @pl.when(pl.program_id(0) == 0)
+    def _():
+        gain_out[...] = jnp.zeros_like(gain_out)
+
+    gain_out[...] += jnp.sum((total * xh).reshape(xv.shape[0] // 8, 8, D), axis=0)
+
+
+def into_input(grads, weights, x):
+    rows = x.shape[0]
+    bm = 256
+    row = lambda width: pl.BlockSpec((bm, width), lambda i: (i, 0))
+    return pl.pallas_call(
+        functools.partial(into_kernel, len(grads)),
+        out_shape=[jax.ShapeDtypeStruct((rows, D), BF), jax.ShapeDtypeStruct((8, D), F32)],
+        grid=(rows // bm,),
+        in_specs=[row(grad.shape[1]) for grad in grads]
+        + [whole(weight.shape) for weight in weights]
+        + [row(D)],
+        out_specs=[row(D), whole((8, D))],
+        compiler_params=params(),
+        cost_estimate=SMALL,
+    )(*grads, *weights, x)
 
 
 def tables(positions):
@@ -1082,8 +1175,10 @@
 
     y_got = xor_seq(core_rows(y_part, 1 - core), 1)
     if fast:
-        flow = {"wg": plane_step(t_dot(b, dgate).astype(BF), "wg", 0)}
-        flow["wu"] = plane_step(t_dot(b, dup).astype(BF), "wu", 0)
+        grad_g, grad_u = t_dot(b, dgate).astype(BF), t_dot(b, dup).astype(BF)
+        grad_g, db_p_got, db_c_got = after((grad_g, db_p_got, db_c_got))
+        flow = {"wg": plane_step(grad_g, "wg", 0)}
+        flow["wu"] = plane_step(after(grad_u, kept(flow["wg"])), "wu", 0)
         dy_cols = cut(dy, core)
         grad_d = t_dot(hid, dy_cols).astype(BF)
         hid_got, y_got = after((hid_got, y_got), kept(flow["wg"], flow["wu"]))
@@ -1136,23 +1231,24 @@
     y_prompt, y_cont = home_end(y_rows, side, p)
 
     if fast:
-        dq, feed_stage = after((dq, feed_stage))
-        head_q = plane_step(t_dot(a, dq).astype(BF), "wq", 0)
-        a_all = jnp.concatenate([a, a_far])
+        grad_q = t_dot(a, dq).astype(BF)
+        grad_q, feed_stage = after((grad_q, feed_stage))
+        head_q = plane_step(grad_q, "wq", 0)
+        a_all = after(jnp.concatenate([a, a_far]), kept(head_q))
         pair = [(dk_own, dk_far), (dv_own, dv_far)]
         pair = [t_dot(a_all, jnp.concatenate(part)).astype(BF) for part in pair]
         head_kv = plane_step(jnp.concatenate(pair), "wk", 0)
         feed_stage = line_next(feed_stage)
         dk_own, dk_far = after((dk_own, dk_far), kept(feed_stage, head_q, head_kv))
 
-    da_far = (dot_t(dk_far, w_k) + dot_t(dv_far, w_v)).astype(BF)
+    da_far, gain_far = into_input((dk_far, dv_far), (w_k, w_v), x_far)
     da_far = da_far.reshape(chips - 1, CORES, 2 * p, D)
-    da_own = (dot_t(dq, w_q) + dot_t(dk_own, w_k) + dot_t(dv_own, w_v)).astype(BF)
+    da_own, gain_own = into_input((dq, dk_own, dv_own), (w_q, w_k, w_v), x)
+    dg1 = jnp.sum(gain_far + gain_own, axis=0)
     far_keep = lax.dynamic_index_in_dim(da_far, core, 1, keepdims=False)
     far_send = lax.dynamic_index_in_dim(da_far, 1 - core, 1, keepdims=False)
     sent = jnp.concatenate([core_rows(da_own, 1 - core), far_send.reshape(-1, D)])
     got = xor_seq(sent, 1)
-    dg1 = gain_sum(x, da_own) + gain_sum(x_far, da_far.reshape(-1, D))
     if fast:
         head_q, head_kv, feed_stage = after((head_q, head_kv, feed_stage))
         head_q = plane_step(added(head_q), "wq", 1)
@@ -1163,8 +1259,10 @@
     blocks = jnp.concatenate([mine[None, : 2 * p], far_sum])
     mask = half // 2
     while mask > 1:
-        near, away = blocks[: mask // 2], blocks[mask // 2 :]
-        blocks = near + xor_seq(away.astype(BF), mask).astype(F32)
+        near, away = blocks[: mask // 2], blocks[mask // 2 :].astype(BF)
+        if fast:
+            head_q, head_kv = after((head_q, head_kv), away)
+        blocks = near + xor_seq(away, mask).astype(F32)
         mask //= 2
     da = jnp.concatenate([blocks[0], mine[2 * p :]])
 

time: 790 us -> 766 us (0.970)
  matrix products: 66.7 us -> 45.3 us
  waiting for transfers between devices: 132 us -> 151 us
  starting transfers between devices: 65.1 us -> 50.1 us
  other arithmetic: 96.1 us -> 82.5 us
  Pallas kernels: 317 us -> 329 us
    ppermute x27, waiting for transfers between devices: 30.3 us -> 55.9 us  [xor_seq(): return lax.ppermute(block, 'seq', [(i, i ^ mask) for i in range(count)])]
    dot_general x5 -> x0, matrix products: 20.9 us -> none  [dot_t(): lax.dot_general(left, right, (((1,), (1,)), ((), ())), preferred_element_...]
    ppermute x1, waiting for transfers between devices: 20.4 us -> 4.8 us  [fast_grads(): tail = lax.ppermute(tail, ('dp', 'seq'), ring)]
    ppermute x3, waiting for transfers between devices: 0.01 us -> 14.6 us  [fast_grads(): head_got.append(lax.ppermute(head_all, ('dp', 'seq'), pairs))]
    pallas_call x2 -> x4, Pallas kernels: 55.4 us -> 68.4 us  [the longest x2 50.1 us: attend(): pl.pallas_call(functools.partial(attend_kernel if cont else attend_wide_k...]
    ppermute x1, starting transfers between devices: 14.7 us -> 2.24 us  [fast_grads(): before = lax.ppermute(feed_flat[-16:], ('dp', 'seq'), chain)]
    unnamed x235 -> x207, local copies, waits for them, and re-layouts: 29 us -> 28.4 us
  transfers between devices with their start and end apart: 47 -> 47, of which waited for: 11 -> 14; matrix products, arithmetic and copies ran while one was open for 26% -> 20% of each run, Pallas kernels for 36% -> 40%
where the time goes in v3:
time: 766 us; the launch traced here: 755 us
  Pallas kernels  329 us (43%)
  waiting for transfers between devices  151 us (20%)
  other arithmetic  82.5 us (11%)
  local copies, waits for them, and re-layouts  80.6 us (11%)
  starting transfers between devices  50.1 us (7%)
  matrix products  45.3 us (6%)
  between operations  16.4 us (2%)
    pallas_call x4, Pallas kernels, attend_back(): pl.pallas_call(functools.partial(attend_back_kernel, own_p, n_oth, chunk)...  116 us
    all_gather x1, waiting for transfers between devices, gather_weights(): blocks = lax.all_gather(block, 'seq', axis=0)  61.6 us
    ppermute x27, waiting for transfers between devices, xor_seq(): return lax.ppermute(block, 'seq', [(i, i ^ mask) for i in range(count)])  55.9 us
    pallas_call x2, Pallas kernels, attend(): pl.pallas_call(functools.partial(attend_kernel if cont else attend_wide_k...  50.1 us
    pallas_call x2, Pallas kernels, feed(): pl.pallas_call(feed_kernel, out_shape=[jax.ShapeDtypeStruct((total, D), F...  45.7 us
    pallas_call x7, Pallas kernels, matrix(): pl.pallas_call(functools.partial(matrix_kernel, per, split), out_shape=ja...  41 us
    dot_general x9, matrix products, t_dot(): lax.dot_general(left, right, (((0,), (0,)), ((), ())), preferred_element_...  38.6 us
    unnamed x207, local copies, waits for them, and re-layouts  28.4 us
  transfers between devices with their start and end apart: 47, of which 14 were waited for; matrix products, arithmetic and copies ran while one was open for 20% of the time, Pallas kernels for 40%

profile of v3, /device:TPU:0, one launch (start us, length us, event | category | flops | bytes accessed | tf_op | source)
XLA Modules:
  0.0 754.8 jit_solution(12066202930068829407)
XLA Ops:
  10.9 4.0 collective-permute-start.1
  20.1 4.2 fusion.43
  38.3 7.5 shard_map.161.refs_4_.refs_3_
  49.6 8.2 %shard_map.164.wg = bf16[1024,1536]{1,0:T(8,128)(2,1)} custom-call(s32[2]{0:T(128)S(1)} %pad_add_fusion.3.place, bf16[122898,128]{1,0:T(8,128)(2,1)} %bitcast.182, bf16[122898,128]{1,0:T(8,128)(2,1)} %bitcast.183), custom_call_target="tpu_custom_call" | custom-call | flops 1000 | bytes 1000 | tf_op jit(solution)/shard_map/pallas_call | solution.py:621
  57.8 8.2 %shard_map.165.wu = bf16[1024,1536]{1,0:T(8,128)(2,1)} custom-call(s32[2]{0:T(128)S(1)} %pad_add_fusion.3.place, bf16[122898,128]{1,0:T(8,128)(2,1)} %bitcast.184, bf16[122898,128]{1,0:T(8,128)(2,1)} %bitcast.185), custom_call_target="tpu_custom_call" | custom-call | flops 1000 | bytes 1000 | tf_op jit(solution)/shard_map/pallas_call | solution.py:621
  72.8 14.2 %shard_map.166 = (bf16[1536,1024]{1,0:T(8,128)(2,1)}, bf16[1536,1024]{1,0:T(8,128)(2,1)}, bf16[1536,1024]{1,0:T(8,128)(2,1)}, bf16[1536,512]{1,0:T(8,128)(2,1)},...) custom-call(bf16[1536,1024]{1,0:T(8,128)(2,1)} %copy-done.12, f32[1,1024]{1,0:T(1,128)S(1)} %bitcast.168, ...), custom_call_target="tpu_custom_call" | custom-call | flops 1000 | bytes 1000 | tf_op jit(solution)/shard_map/pallas_call | solution.py:140
  90.3 5.6 shard_map.167.wd
  95.9 4.9 shard_map.168.wo
  100.8 3.4 collective-permute-start.7
  106.8 6.8 shard_map.169
  114.8 30.5 %shard_map.170 = (bf16[1024,1024]{1,0:T(8,128)(2,1)}, f32[4,2,1024]{2,1,0:T(2,128)S(1)}) custom-call(bf16[1536,1024]{1,0:T(8,128)(2,1)} %get-tuple-element.178.q, bf16[1536,512]{1,0:T(8,128)(2,1)} %get-tuple-element.167.k_own, bf16[1536,512]{1,0:T(8,128)(2,1)} %get-tuple-element.168.v_own, bf16[1024,512]{1,0:T(8,128)(2,1)S(1)} %copy-done.4, ...), custom_call_target="tpu_custom_call" | custom-call | flops 1000 | bytes 1000 | tf_op jit(solution)/shard_map/pallas_call | solution.py:260
  145.4 5.4 convolution_convert_fusion.5.part
  153.5 19.6 %shard_map.171 = (bf16[512,1024]{1,0:T(8,128)(2,1)}, f32[4,2,512]{2,1,0:T(2,128)S(1)}) custom-call(bf16[1536,1024]{1,0:T(8,128)(2,1)} %get-tuple-element.178.q, bf16[1536,512]{1,0:T(8,128)(2,1)} %get-tuple-element.167.k_own, bf16[1536,512]{1,0:T(8,128)(2,1)} %get-tuple-element.168.v_own, bf16[1024,512]{1,0:T(8,128)(2,1)} %get-tuple-element.174.k_oth, ...), custom_call_target="tpu_custom_call" | custom-call | flops 1000 | bytes 1000 | tf_op jit(solution)/shard_map/pallas_call | solution.py:260
  180.5 4.3 collective-permute-done.11.got
  184.8 28.7 %shard_map.172 = (f32[1536,1024]{1,0:T(8,128)}, bf16[1536,1024]{1,0:T(8,128)(2,1)}, bf16[1536,1536]{1,0:T(8,128)(2,1)}, bf16[1536,1536]{1,0:T(8,128)(2,1)}, bf16...) custom-call(bf16[1536,1024]{1,0:T(8,128)(2,1)} %copy-done.12, ...), custom_call_target="tpu_custom_call" | custom-call | flops 1000 | bytes 1000 | tf_op jit(solution)/shard_map/pallas_call | solution.py:502
  214.6 17.0 %shard_map.173 = (f32[1536,1024]{1,0:T(8,128)}, bf16[1536,1024]{1,0:T(8,128)(2,1)}, bf16[1536,1536]{1,0:T(8,128)(2,1)}, bf16[1536,1536]{1,0:T(8,128)(2,1)}, bf16...) custom-call(bf16[1536,1024]{1,0:T(8,128)(2,1)} %copy-done.12, ...), custom_call_target="tpu_custom_call", output_to_operand_aliasing={{0}: (8, {}), {1}: (9, {}), {2}: (10, {}), {3}: (11, {}), {... | custom-call | flops 1000 | bytes 1000 | tf_op jit(solution)/shard_map/pallas_call | solution.py:502
  237.4 5.9 convolution_convert_fusion
  246.5 5.5 convolution_convert_fusion.1
  258.6 5.6 broadcast_select_fusion
  266.1 11.1 %shard_map.174 = (f32[1536,1024]{1,0:T(8,128)}, bf16[1536,1024]{1,0:T(8,128)(2,1)}, bf16[1536,1024]{1,0:T(8,128)(2,1)}, f32[8,1024]{1,0:T(8,128)S(1)}) custom-call(f32[1536,1024]{1,0:T(8,128)} %get-tuple-element.193.h1, bf16[1536,1024]{1,0:T(8,128)(2,1)} %copy-done.13, bf16[1024,1024]{1,0:T(8,128)(2,1)} %get-tuple-element.186.mine, ...), custom_call_target="tpu_custom_call" | custom-call | flops 1000 | bytes 1000 | tf_op jit(solution)/shard_map/pallas_call | solution.py:553
  277.2 7.0 shard_map.175
  284.2 3.4 convolution_convert_fusion.7
  287.6 3.8 broadcast_select_fusion.2
  308.1 28.8 %shard_map.176 = (bf16[1536,1024]{1,0:T(8,128)(2,1)}, bf16[1536,512]{1,0:T(8,128)(2,1)}, bf16[1536,512]{1,0:T(8,128)(2,1)}, bf16[1024,512]{1,0:T(8,128)(2,1)}, b...) custom-call(bf16[1536,1024]{1,0:T(8,128)(2,1)} %get-tuple-element.178.q, ...), custom_call_target="tpu_custom_call" | custom-call | flops 1000 | bytes 1000 | tf_op jit(solution)/shard_map/pallas_call | solution.py:434
  336.8 29.1 %shard_map.177 = (bf16[1536,1024]{1,0:T(8,128)(2,1)}, bf16[1536,512]{1,0:T(8,128)(2,1)}, bf16[1536,512]{1,0:T(8,128)(2,1)}, bf16[1024,512]{1,0:T(8,128)(2,1)}, b...) custom-call(bf16[1536,1024]{1,0:T(8,128)(2,1)} %get-tuple-element.17, ...), custom_call_target="tpu_custom_call", output_to_operand_aliasing={{0}: (23, {}), {1}: (24, {}), {2}: (25, {}), {3}: (26, {}),... | custom-call | flops 1000 | bytes 1000 | tf_op jit(solution)/shard_map/pallas_call | solution.py:434
  380.4 28.9 %shard_map.178 = (bf16[1536,1024]{1,0:T(8,128)(2,1)}, bf16[1536,512]{1,0:T(8,128)(2,1)}, bf16[1536,512]{1,0:T(8,128)(2,1)}, bf16[1024,512]{1,0:T(8,128)(2,1)}, b...) custom-call(bf16[1536,1024]{1,0:T(8,128)(2,1)} %get-tuple-element.17, ...), custom_call_target="tpu_custom_call", output_to_operand_aliasing={{0}: (23, {}), {1}: (24, {}), {2}: (25, {}), {3}: (26, {}),... | custom-call | flops 1000 | bytes 1000 | tf_op jit(solution)/shard_map/pallas_call | solution.py:434
  413.9 5.5 pad_maximum_fusion.1
  420.3 28.9 %shard_map.179 = (bf16[1536,1024]{1,0:T(8,128)(2,1)}, bf16[1536,512]{1,0:T(8,128)(2,1)}, bf16[1536,512]{1,0:T(8,128)(2,1)}, bf16[1024,512]{1,0:T(8,128)(2,1)}, b...) custom-call(bf16[1536,1024]{1,0:T(8,128)(2,1)} %get-tuple-element.17, ...), custom_call_target="tpu_custom_call", output_to_operand_aliasing={{0}: (23, {}), {1}: (24, {}), {2}: (25, {}), {3}: (26, {}),... | custom-call | flops 1000 | bytes 1000 | tf_op jit(solution)/shard_map/pallas_call | solution.py:434
  449.2 5.9 convolution_convert_fusion.4
  466.8 11.8 %shard_map.181 = (bf16[1536,1024]{1,0:T(8,128)(2,1)}, f32[8,1024]{1,0:T(8,128)S(1)}) custom-call(bf16[1536,1024]{1,0:T(8,128)(2,1)} %get-tuple-element.258.refs_0_, bf16[1536,512]{1,0:T(8,128)(2,1)} %get-tuple-element.274.refs_1_, bf16[1536,512]{1,0:T(8,128)(2,1)} %get-tuple-element.264.refs_2_, bf16[1024,1024]{1,0:T(8,128)(2,1)} %shard_map.161.refs_4_.refs_3_, ...), custom_call_target="tpu_custom_call" | custom-call | flops 1000 | bytes 1000 | tf_op jit(solution)/shard_map/pallas_call | solution.py:1023
  485.5 6.5 shard_map.180
  493.7 20.7 %collective-permute-done.29 = bf16[2880,128]{1,0:T(8,128)(2,1)} collective-permute-done((bf16[2880,128]{1,0:T(8,128)(2,1)}, bf16[2880,128]{1,0:T(8,128)(2,1)}, u32[]{:S(2)}, u32[]{:S(2)}) %collective-permute-start.29) | collective-permute-done | bytes 737312 | tf_op jit(solution)/shard_map/ppermute | solution.py:59
  524.5 4.1 collective-permute-done.31
  533.3 3.5 all-to-all-start.1
  541.6 6.4 all-to-all-done.1.who
  548.8 6.4 all-to-all-start
  571.7 5.7 collective-permute-done.34
  581.8 11.2 %collective-permute-done.37 = bf16[1024,128]{1,0:T(8,128)(2,1)S(1)} collective-permute-done((bf16[1024,128]{1,0:T(8,128)(2,1)S(1)}, bf16[1024,128]{1,0:T(8,128)(2,1)S(1)}, u32[]{:S(2)}, u32[]{:S(2)}) %collective-permute-start.37) | collective-permute-done | bytes 262176 | tf_op jit(solution)/shard_map/ppermute | solution.py:59
  594.6 4.8 collective-permute-done.38
  602.3 3.5 collective-permute-start.39
  608.6 4.3 collective-permute-done.39
  613.0 10.3 %collective-permute-done.40 = bf16[1312,128]{1,0:T(8,128)(2,1)S(1)} collective-permute-done((bf16[1312,128]{1,0:T(8,128)(2,1)S(1)}, bf16[1312,128]{1,0:T(8,128)(2,1)S(1)}, u32[]{:S(2)}, u32[]{:S(2)}) %collective-permute-start.40) | collective-permute-done | bytes 335904 | tf_op jit(solution)/shard_map/ppermute | solution.py:965
  628.2 4.4 pad_bitcast_fusion
  632.7 15.9 %shard_map.183 = (f32[3872,128]{1,0:T(8,128)}, f32[3872,128]{1,0:T(8,128)}, f32[3872,128]{1,0:T(8,128)}, bf16[3872,128]{1,0:T(8,128)(2,1)}) custom-call(s32[6]{0:T(128)S(1)} %stack.143.info, bf16[4,1312,128]{2,1,0:T(8,128)(2,1)} %pad_maximum_fusion.10.who, bf16[4,1312,128]{2,1,0:T(8,128)(2,1)} %collective-permute-done.42.other, ...), custom_call_target="tpu_custom_call" | custom-call | flops 1000 | bytes 1000 | tf_op jit(solution)/shard_map/pallas_call | solution.py:904
  648.7 11.5 %collective-permute-done.43 = bf16[384,1024]{1,0:T(8,128)(2,1)} collective-permute-done((bf16[384,1024]{1,0:T(8,128)(2,1)}, bf16[384,1024]{1,0:T(8,128)(2,1)}, u32[]{:S(2)}, u32[]{:S(2)}) %collective-permute-start.43) | collective-permute-done | bytes 786464 | tf_op jit(solution)/shard_map/ppermute | solution.py:59
  674.4 61.6 %all-gather.3.cloned.1.call-done = bf16[30976,128]{1,0:T(8,128)(2,1)} async-done(((bf16[3872,128]{1,0:T(8,128)(2,1)}), bf16[30976,128]{1,0:T(8,128)(2,1)}) %all-gather.3.cloned.1.call-update) | async-done | bytes 7929872 | tf_op jit(solution)/shard_map/all_gather | solution.py:985
  736.0 3.8 slice.439
  741.8 5.7 maximum_bitcast_fusion
  (467 shorter events, 194.4 us)
Async XLA Ops:
  10.9 38.7 %collective-permute-start.1 = (bf16[384,1024]{1,0:T(8,128)(2,1)}, bf16[384,1024]{1,0:T(8,128)(2,1)}, u32[]{:S(2)}, u32[]{:S(2)}) collective-permute-start(bf16[384,1024]{1,0:T(8,128)(2,1)} %get-tuple-element.376), channel_id=1, source_target_pairs={{0,4},{1,5},{2,6},{3,7},{4,0},{5,1},{6,2},{7,3},{8,12},{9,13},{10,... | collective-permute-start | bytes 2359304 | tf_op jit(solution)/shard_map/ppermute | solution.py:59
  14.9 53.2 %collective-permute-start = (bf16[384,1024]{1,0:T(8,128)(2,1)}, bf16[384,1024]{1,0:T(8,128)(2,1)}, u32[]{:S(2)}, u32[]{:S(2)}) collective-permute-start(bf16[384,1024]{1,0:T(8,128)(2,1)} %get-tuple-element.377), channel_id=1, source_target_pairs={{0,1},{1,0},{2,3},{3,2},{4,5},{5,4},{6,7},{7,6},{8,9},{9,8},{10,11... | collective-permute-start | bytes 2359304 | tf_op jit(solution)/shard_map/ppermute | solution.py:59
  15.7 52.2 %collective-permute-start.3 = (bf16[1,256,1024]{2,1,0:T(8,128)(2,1)}, bf16[1,256,1024]{2,1,0:T(8,128)(2,1)S(1)}, u32[]{:S(2)}, u32[]{:S(2)}) collective-permute-start(bf16[1,256,1024]{2,1,0:T(8,128)(2,1)} %constant_dynamic-slice_fusion), channel_id=1, source_target_pairs={{0,2},{1,3},{2,0},{3,1},{4,6},{5,7},{6,4},{7,5},{8,10},{9,11},{10,... | collective-permute-start | bytes 1572872 | tf_op jit(solution)/shard_map/ppermute | solution.py:59
  24.6 46.6 %copy-start.2 = (f32[1536,128]{1,0:T(8,128)}, f32[1536,128]{1,0:T(8,128)S(1)}, u32[]{:S(2)}) copy-start(f32[1536,128]{1,0:T(8,128)S(1)} %pad_maximum_fusion.15.refs_2_.cos_q.cos_o) | copy-start | bytes 2359300
  66.0 3.6 collective-permute-start.2
  67.1 19.9 %collective-permute-start.5 = (bf16[1,256,1024]{2,1,0:T(8,128)(2,1)S(1)}, bf16[1,256,1024]{2,1,0:T(8,128)(2,1)S(1)}, u32[]{:S(2)}, u32[]{:S(2)}) collective-permute-start(bf16[1,256,1024]{2,1,0:T(8,128)(2,1)S(1)} %slice_bitcast_fusion.1), channel_id=1, source_target_pairs={{0,2},{1,3},{2,0},{3,1},{4,6},{5,7},{6,4},{7,5},{8,10},{9,11},{10,... | collective-permute-start | bytes 1572872 | tf_op jit(solution)/shard_map/ppermute | solution.py:59
  67.9 21.2 %collective-permute-start.4 = (bf16[1,256,1024]{2,1,0:T(8,128)(2,1)S(1)}, bf16[1,256,1024]{2,1,0:T(8,128)(2,1)}, u32[]{:S(2)}, u32[]{:S(2)}) collective-permute-start(bf16[1,256,1024]{2,1,0:T(8,128)(2,1)S(1)} %collective-permute-done.3), channel_id=1, source_target_pairs={{0,1},{1,0},{2,3},{3,2},{4,5},{5,4},{6,7},{7,6},{8,9},{9,8},{10,11... | collective-permute-start | bytes 1572872 | tf_op jit(solution)/shard_map/ppermute | solution.py:59
  87.0 17.2 %collective-permute-start.6 = (bf16[1,256,1024]{2,1,0:T(8,128)(2,1)S(1)}, bf16[1,256,1024]{2,1,0:T(8,128)(2,1)}, u32[]{:S(2)}, u32[]{:S(2)}) collective-permute-start(bf16[1,256,1024]{2,1,0:T(8,128)(2,1)S(1)} %collective-permute-done.5), channel_id=1, source_target_pairs={{0,1},{1,0},{2,3},{3,2},{4,5},{5,4},{6,7},{7,6},{8,9},{9,8},{10,11... | collective-permute-start | bytes 1572872 | tf_op jit(solution)/shard_map/ppermute | solution.py:59
  100.8 50.0 %collective-permute-start.7 = (bf16[384,1024]{1,0:T(8,128)(2,1)S(1)}, bf16[384,1024]{1,0:T(8,128)(2,1)}, u32[]{:S(2)}, u32[]{:S(2)}) collective-permute-start(bf16[384,1024]{1,0:T(8,128)(2,1)S(1)} %copy-done.63), channel_id=1, source_target_pairs={{0,4},{1,5},{2,6},{3,7},{4,0},{5,1},{6,2},{7,3},{8,12},{9,13},{10,... | collective-permute-start | bytes 2359304 | tf_op jit(solution)/shard_map/ppermute | solution.py:59
  150.8 22.3 %collective-permute-start.8 = (bf16[384,1024]{1,0:T(8,128)(2,1)}, bf16[384,1024]{1,0:T(8,128)(2,1)}, u32[]{:S(2)}, u32[]{:S(2)}) collective-permute-start(bf16[384,1024]{1,0:T(8,128)(2,1)} %collective-permute-done.7), channel_id=1, source_target_pairs={{0,1},{1,0},{2,3},{3,2},{4,5},{5,4},{6,7},{7,6},{8,9},{9,8},{10,11... | collective-permute-start | bytes 2359304 | tf_op jit(solution)/shard_map/ppermute | solution.py:59
  150.8 24.4 %collective-permute-start.12 = (bf16[384,1024]{1,0:T(8,128)(2,1)S(1)}, bf16[384,1024]{1,0:T(8,128)(2,1)}, u32[]{:S(2)}, u32[]{:S(2)}) collective-permute-start(bf16[384,1024]{1,0:T(8,128)(2,1)S(1)} %copy-done.37), channel_id=1, source_target_pairs={{0,1},{1,0},{2,3},{3,2},{4,5},{5,4},{6,7},{7,6},{8,9},{9,8},{10,11... | collective-permute-start | bytes 2359304 | tf_op jit(solution)/shard_map/ppermute | solution.py:59
  174.6 39.0 %collective-permute-start.10 = (bf16[1536,1024]{1,0:T(8,128)(2,1)S(1)}, bf16[1536,1024]{1,0:T(8,128)(2,1)}, u32[]{:S(2)}, u32[]{:S(2)}) collective-permute-start(bf16[1536,1024]{1,0:T(8,128)(2,1)S(1)} %constant_dynamic-update-slice_fusion.5.o), channel_id=1, source_target_pairs={{0,1},{1,0},{2,3},{3,2},{4,5},{5,4},{6,7},{7,6},{8,9},{9,8},{10,11... | collective-permute-start | bytes 9437192 | tf_op jit(solution)/shard_map/ppermute | solution.py:59
  174.7 10.1 %collective-permute-start.11 = (bf16[1024,1024]{1,0:T(8,128)(2,1)}, bf16[1024,1024]{1,0:T(8,128)(2,1)}, u32[]{:S(2)}, u32[]{:S(2)}) collective-permute-start(bf16[1024,1024]{1,0:T(8,128)(2,1)} %convolution_convert_fusion.5.part), channel_id=1, source_target_pairs={{0,1},{1,0},{2,3},{3,2},{4,5},{5,4},{6,7},{7,6},{8,9},{9,8},{10,11... | collective-permute-start | bytes 6291464 | tf_op jit(solution)/shard_map/ppermute | solution.py:59
  178.4 35.2 %collective-permute-start.9 = (bf16[512,1024]{1,0:T(8,128)(2,1)S(1)}, bf16[512,1024]{1,0:T(8,128)(2,1)S(1)}, u32[]{:S(2)}, u32[]{:S(2)}) collective-permute-start(bf16[512,1024]{1,0:T(8,128)(2,1)S(1)} %convolution_convert_fusion.8.part), channel_id=1, source_target_pairs={{0,1},{1,0},{2,3},{3,2},{4,5},{5,4},{6,7},{7,6},{8,9},{9,8},{10,11... | collective-permute-start | bytes 3145736 | tf_op jit(solution)/shard_map/ppermute | solution.py:59
  231.5 27.1 %collective-permute-start.13 = (bf16[1536,1536]{1,0:T(8,128)(2,1)}, bf16[1536,1536]{1,0:T(8,128)(2,1)}, u32[]{:S(2)}, u32[]{:S(2)}) collective-permute-start(bf16[1536,1536]{1,0:T(8,128)(2,1)} %get-tuple-element.196), channel_id=1, source_target_pairs={{0,1},{1,0},{2,3},{3,2},{4,5},{5,4},{6,7},{7,6},{8,9},{9,8},{10,11... | collective-permute-start | bytes 14155784 | tf_op jit(solution)/shard_map/ppermute | solution.py:59
  232.6 19.4 %collective-permute-start.15 = (bf16[1024,1024]{1,0:T(8,128)(2,1)}, bf16[1024,1024]{1,0:T(8,128)(2,1)S(1)}, u32[]{:S(2)}, u32[]{:S(2)}) collective-permute-start(bf16[1024,1024]{1,0:T(8,128)(2,1)} %get-tuple-element.186.mine), channel_id=1, source_target_pairs={{0,1},{1,0},{2,3},{3,2},{4,5},{5,4},{6,7},{7,6},{8,9},{9,8},{10,11... | collective-permute-start | bytes 6291464 | tf_op jit(solution)/shard_map/ppermute | solution.py:59
  236.2 22.4 %collective-permute-start.14 = (bf16[768,1024]{1,0:T(8,128)(2,1)S(1)}, bf16[768,1024]{1,0:T(8,128)(2,1)S(1)}, u32[]{:S(2)}, u32[]{:S(2)}) collective-permute-start(bf16[768,1024]{1,0:T(8,128)(2,1)S(1)} %pad_maximum_fusion.6), channel_id=1, source_target_pairs={{0,1},{1,0},{2,3},{3,2},{4,5},{5,4},{6,7},{7,6},{8,9},{9,8},{10,11... | collective-permute-start | bytes 4718600 | tf_op jit(solution)/shard_map/ppermute | solution.py:59
  246.1 5.9 collective-permute-start.16
  255.6 37.0 %collective-permute-start.18 = (bf16[1024,768]{1,0:T(8,128)(2,1)}, bf16[1024,768]{1,0:T(8,128)(2,1)}, u32[]{:S(2)}, u32[]{:S(2)}) collective-permute-start(bf16[1024,768]{1,0:T(8,128)(2,1)} %get-tuple-element.336), channel_id=1, source_target_pairs={{0,16},{8,24},{16,0},{24,8},{1,17},{9,25},{17,1},{25,9},{2,18},{10... | collective-permute-start | bytes 4718600 | tf_op jit(solution)/shard_map/ppermute | solution.py:708
  257.1 36.5 %collective-permute-start.17 = (bf16[1024,768]{1,0:T(8,128)(2,1)}, bf16[1024,768]{1,0:T(8,128)(2,1)}, u32[]{:S(2)}, u32[]{:S(2)}) collective-permute-start(bf16[1024,768]{1,0:T(8,128)(2,1)} %get-tuple-element.338), channel_id=1, source_target_pairs={{0,8},{8,0},{16,24},{24,16},{1,9},{9,1},{17,25},{25,17},{2,10},{10... | collective-permute-start | bytes 4718600 | tf_op jit(solution)/shard_map/ppermute | solution.py:708
  293.6 72.3 %collective-permute-start.19 = (bf16[3072,256]{1,0:T(8,128)(2,1)S(1)}, bf16[3072,256]{1,0:T(8,128)(2,1)S(1)}, u32[]{:S(2)}, u32[]{:S(2)}) collective-permute-start(bf16[3072,256]{1,0:T(8,128)(2,1)S(1)} %copy-done.57), channel_id=1, source_target_pairs={{0,8},{8,0},{16,24},{24,16},{1,9},{9,1},{17,25},{25,17},{2,10},{10... | collective-permute-start | bytes 4718600 | tf_op jit(solution)/shard_map/ppermute | solution.py:708
  298.4 67.5 %collective-permute-start.22 = (bf16[1024,384]{1,0:T(8,128)(2,1)}, bf16[1024,384]{1,0:T(8,128)(2,1)}, u32[]{:S(2)}, u32[]{:S(2)}) collective-permute-start(bf16[1024,384]{1,0:T(8,128)(2,1)} %get-tuple-element.362), channel_id=1, source_target_pairs={{0,8},{8,0},{16,24},{24,16},{1,9},{9,1},{17,25},{25,17},{2,10},{10... | collective-permute-start | bytes 2359304 | tf_op jit(solution)/shard_map/ppermute | solution.py:708
  298.9 67.1 %collective-permute-start.21 = (bf16[2048,256]{1,0:T(8,128)(2,1)S(1)}, bf16[2048,256]{1,0:T(8,128)(2,1)S(1)}, u32[]{:S(2)}, u32[]{:S(2)}) collective-permute-start(bf16[2048,256]{1,0:T(8,128)(2,1)S(1)} %get-tuple-element.356), channel_id=1, source_target_pairs={{0,16},{8,24},{16,0},{24,8},{1,17},{9,25},{17,1},{25,9},{2,18},{10... | collective-permute-start | bytes 3145736 | tf_op jit(solution)/shard_map/ppermute | solution.py:708
  302.5 63.5 %collective-permute-start.20 = (bf16[1024,384]{1,0:T(8,128)(2,1)S(1)}, bf16[1024,384]{1,0:T(8,128)(2,1)S(1)}, u32[]{:S(2)}, u32[]{:S(2)}) collective-permute-start(bf16[1024,384]{1,0:T(8,128)(2,1)S(1)} %get-tuple-element.364), channel_id=1, source_target_pairs={{0,16},{8,24},{16,0},{24,8},{1,17},{9,25},{17,1},{25,9},{2,18},{10... | collective-permute-start | bytes 2359304 | tf_op jit(solution)/shard_map/ppermute | solution.py:708
  369.2 40.1 %collective-permute-start.25 = (bf16[2048,128]{1,0:T(8,128)(2,1)}, bf16[2048,128]{1,0:T(8,128)(2,1)S(1)}, u32[]{:S(2)}, u32[]{:S(2)}) collective-permute-start(bf16[2048,128]{1,0:T(8,128)(2,1)} %get-tuple-element.386), channel_id=1, source_target_pairs={{0,8},{8,0},{16,24},{24,16},{1,9},{9,1},{17,25},{25,17},{2,10},{10... | collective-permute-start | bytes 1572872 | tf_op jit(solution)/shard_map/ppermute | solution.py:708
  372.6 36.7 %collective-permute-start.24 = (bf16[3072,128]{1,0:T(8,128)(2,1)}, bf16[3072,128]{1,0:T(8,128)(2,1)S(1)}, u32[]{:S(2)}, u32[]{:S(2)}) collective-permute-start(bf16[3072,128]{1,0:T(8,128)(2,1)} %get-tuple-element.360), channel_id=1, source_target_pairs={{0,16},{8,24},{16,0},{24,8},{1,17},{9,25},{17,1},{25,9},{2,18},{10... | collective-permute-start | bytes 2359304 | tf_op jit(solution)/shard_map/ppermute | solution.py:708
  378.1 41.3 %collective-permute-start.23 = (bf16[384,1024]{1,0:T(8,128)(2,1)S(1)}, bf16[384,1024]{1,0:T(8,128)(2,1)S(1)}, u32[]{:S(2)}, u32[]{:S(2)}) collective-permute-start(bf16[384,1024]{1,0:T(8,128)(2,1)S(1)} %pad_maximum_fusion.17), channel_id=1, source_target_pairs={{0,4},{1,5},{2,6},{3,7},{4,0},{5,1},{6,2},{7,3},{8,12},{9,13},{10,... | collective-permute-start | bytes 2359304 | tf_op jit(solution)/shard_map/ppermute | solution.py:59
  413.7 41.5 %collective-permute-start.26 = (bf16[2,2880,128]{2,1,0:T(8,128)(2,1)}, bf16[2,2880,128]{2,1,0:T(8,128)(2,1)}, u32[]{:S(2)}, u32[]{:S(2)}) collective-permute-start(bf16[2,2880,128]{2,1,0:T(8,128)(2,1)} %get-tuple-element.346), channel_id=1, source_target_pairs={{0,2},{1,3},{2,0},{3,1},{4,6},{5,7},{6,4},{7,5},{8,10},{9,11},{10,... | collective-permute-start | bytes 4423688 | tf_op jit(solution)/shard_map/ppermute | solution.py:59
  481.6 32.8 %collective-permute-start.29 = (bf16[2880,128]{1,0:T(8,128)(2,1)}, bf16[2880,128]{1,0:T(8,128)(2,1)}, u32[]{:S(2)}, u32[]{:S(2)}) collective-permute-start(bf16[2880,128]{1,0:T(8,128)(2,1)} %get-tuple-element.378), channel_id=1, source_target_pairs={{0,4},{1,5},{2,6},{3,7},{4,0},{5,1},{6,2},{7,3},{8,12},{9,13},{10,... | collective-permute-start | bytes 2211848 | tf_op jit(solution)/shard_map/ppermute | solution.py:59
  483.7 30.7 %collective-permute-start.28 = (bf16[2048,256]{1,0:T(8,128)(2,1)}, bf16[2048,256]{1,0:T(8,128)(2,1)}, u32[]{:S(2)}, u32[]{:S(2)}) collective-permute-start(bf16[2048,256]{1,0:T(8,128)(2,1)} %get-tuple-element.352), channel_id=1, source_target_pairs={{0,16},{8,24},{16,0},{24,8},{1,17},{9,25},{17,1},{25,9},{2,18},{10... | collective-permute-start | bytes 3145736 | tf_op jit(solution)/shard_map/ppermute | solution.py:708
  485.0 29.4 %collective-permute-start.27 = (bf16[1024,512]{1,0:T(8,128)(2,1)}, bf16[1024,512]{1,0:T(8,128)(2,1)}, u32[]{:S(2)}, u32[]{:S(2)}) collective-permute-start(bf16[1024,512]{1,0:T(8,128)(2,1)} %get-tuple-element.354), channel_id=1, source_target_pairs={{0,8},{8,0},{16,24},{24,16},{1,9},{9,1},{17,25},{25,17},{2,10},{10... | collective-permute-start | bytes 3145736 | tf_op jit(solution)/shard_map/ppermute | solution.py:708
  493.5 28.1 %collective-permute-start.32 = (bf16[1280,1024]{1,0:T(8,128)(2,1)S(1)}, bf16[1280,1024]{1,0:T(8,128)(2,1)S(1)}, u32[]{:S(2)}, u32[]{:S(2)}) collective-permute-start(bf16[1280,1024]{1,0:T(8,128)(2,1)S(1)} %pad_maximum_fusion.4), channel_id=1, source_target_pairs={{0,1},{1,0},{2,3},{3,2},{4,5},{5,4},{6,7},{7,6},{8,9},{9,8},{10,11... | collective-permute-start | bytes 7864328 | tf_op jit(solution)/shard_map/ppermute | solution.py:59
  516.0 12.7 %collective-permute-start.31 = (bf16[2048,128]{1,0:T(8,128)(2,1)S(1)}, bf16[2048,128]{1,0:T(8,128)(2,1)S(1)}, u32[]{:S(2)}, u32[]{:S(2)}) collective-permute-start(bf16[2048,128]{1,0:T(8,128)(2,1)S(1)} %get-tuple-element.382), channel_id=1, source_target_pairs={{0,8},{8,0},{16,24},{24,16},{1,9},{9,1},{17,25},{25,17},{2,10},{10... | collective-permute-start | bytes 1572872 | tf_op jit(solution)/shard_map/ppermute | solution.py:708
  519.1 12.4 %collective-permute-start.30 = (bf16[1024,256]{1,0:T(8,128)(2,1)S(1)}, bf16[1024,256]{1,0:T(8,128)(2,1)S(1)}, u32[]{:S(2)}, u32[]{:S(2)}) collective-permute-start(bf16[1024,256]{1,0:T(8,128)(2,1)S(1)} %get-tuple-element.384), channel_id=1, source_target_pairs={{0,16},{8,24},{16,0},{24,8},{1,17},{9,25},{17,1},{25,9},{2,18},{10... | collective-permute-start | bytes 1572872 | tf_op jit(solution)/shard_map/ppermute | solution.py:708
  524.5 31.2 %collective-permute-start.33 = (bf16[1,512,1024]{2,1,0:T(8,128)(2,1)}, bf16[1,512,1024]{2,1,0:T(8,128)(2,1)}, u32[]{:S(2)}, u32[]{:S(2)}) collective-permute-start(bf16[1,512,1024]{2,1,0:T(8,128)(2,1)} %fusion.37), channel_id=1, source_target_pairs={{0,2},{1,3},{2,0},{3,1},{4,6},{5,7},{6,4},{7,5},{8,10},{9,11},{10,... | collective-permute-start | bytes 3145736 | tf_op jit(solution)/shard_map/ppermute | solution.py:59
  533.3 14.6 %all-to-all-start.1 = ((bf16[4,960,128]{2,1,0:T(8,128)(2,1)}), bf16[4,960,128]{2,1,0:T(8,128)(2,1)S(1)}, u32[]{:S(2)}, u32[]{:S(2)}) async-start(bf16[4,960,128]{2,1,0:T(8,128)(2,1)} %pad_maximum_fusion.14), calls=%async_computation.1 | async-start | bytes 1966080 | tf_op jit(solution)/shard_map/all_to_all | solution.py:927
  548.8 22.9 %all-to-all-start = ((f32[32,18,128]{2,1,0:T(8,128)}), f32[32,18,128]{2,1,0:T(8,128)S(1)}, u32[]{:S(2)}, u32[]{:S(2)}) async-start(f32[32,18,128]{2,1,0:T(8,128)} %broadcast_in_dim.60), calls=%async_computation | async-start | bytes 786432 | tf_op jit(solution)/shard_map/all_to_all | solution.py:922
  555.2 180.8 %all-gather.3.cloned.1.call-start = ((), (), s32[]{:S(2)}) async-start(), calls=%async_computation.2 | async-start | bytes 8921088 | tf_op jit(solution)/shard_map/all_gather | solution.py:985
  555.5 10.1 %collective-permute-start.35 = (bf16[4,960,128]{2,1,0:T(8,128)(2,1)S(1)}, bf16[4,960,128]{2,1,0:T(8,128)(2,1)S(1)}, u32[]{:S(2)}, u32[]{:S(2)}) collective-permute-start(bf16[4,960,128]{2,1,0:T(8,128)(2,1)S(1)} %all-to-all-done.1.who), channel_id=1, source_target_pairs={{0,1},{1,0},{2,3},{3,2},{4,5},{5,4},{6,7},{7,6},{8,9},{9,8},{10,11... | collective-permute-start | bytes 2949128 | tf_op jit(solution)/shard_map/ppermute | solution.py:59
  561.2 16.2 %collective-permute-start.34 = (bf16[2,1024,128]{2,1,0:T(8,128)(2,1)}, bf16[2,1024,128]{2,1,0:T(8,128)(2,1)}, u32[]{:S(2)}, u32[]{:S(2)}) collective-permute-start(bf16[2,1024,128]{2,1,0:T(8,128)(2,1)} %get-tuple-element.380), channel_id=1, source_target_pairs={{0,2},{1,3},{2,0},{3,1},{4,6},{5,7},{6,4},{7,5},{8,10},{9,11},{10,... | collective-permute-start | bytes 1572872 | tf_op jit(solution)/shard_map/ppermute | solution.py:59
  569.0 8.4 %collective-permute-start.36 = (f32[16,128]{1,0:T(8,128)S(1)}, f32[16,128]{1,0:T(8,128)S(1)}, u32[]{:S(2)}, u32[]{:S(2)}) collective-permute-start(f32[16,128]{1,0:T(8,128)S(1)} %slice.423), channel_id=1, source_target_pairs={{0,2},{1,3},{2,4},{3,5},{4,6},{5,7},{6,8},{7,9},{8,10},{9,11},{10,... | collective-permute-start | bytes 24584 | tf_op jit(solution)/shard_map/ppermute | solution.py:949
  578.8 14.2 %collective-permute-start.37 = (bf16[1024,128]{1,0:T(8,128)(2,1)S(1)}, bf16[1024,128]{1,0:T(8,128)(2,1)S(1)}, u32[]{:S(2)}, u32[]{:S(2)}) collective-permute-start(bf16[1024,128]{1,0:T(8,128)(2,1)S(1)} %dynamic-slice_bitcast_fusion.11), channel_id=1, source_target_pairs={{0,4},{1,5},{2,6},{3,7},{4,0},{5,1},{6,2},{7,3},{8,12},{9,13},{10,... | collective-permute-start | bytes 786440 | tf_op jit(solution)/shard_map/ppermute | solution.py:59
  593.2 6.2 collective-permute-start.38
  602.3 10.7 %collective-permute-start.39 = (bf16[1312,128]{1,0:T(8,128)(2,1)S(1)}, bf16[1312,128]{1,0:T(8,128)(2,1)S(1)}, u32[]{:S(2)}, u32[]{:S(2)}) collective-permute-start(bf16[1312,128]{1,0:T(8,128)(2,1)S(1)} %pad_maximum_fusion.21), channel_id=1, source_target_pairs={{0,8},{1,9},{8,0},{9,1},{10,2},{11,3},{12,4},{13,5},{14,6},{15,7}} | collective-permute-start | bytes 1007624 | tf_op jit(solution)/shard_map/ppermute | solution.py:965
  605.8 17.5 %collective-permute-start.40 = (bf16[1312,128]{1,0:T(8,128)(2,1)S(1)}, bf16[1312,128]{1,0:T(8,128)(2,1)S(1)}, u32[]{:S(2)}, u32[]{:S(2)}) collective-permute-start(bf16[1312,128]{1,0:T(8,128)(2,1)S(1)} %pad_maximum_fusion.21), channel_id=1, source_target_pairs={{16,0},{17,1},{18,2},{19,3},{20,4},{21,5},{22,6},{23,7},{24,8},{25... | collective-permute-start | bytes 1007624 | tf_op jit(solution)/shard_map/ppermute | solution.py:965
  607.1 16.2 %collective-permute-start.41 = (bf16[1312,128]{1,0:T(8,128)(2,1)S(1)}, bf16[1312,128]{1,0:T(8,128)(2,1)S(1)}, u32[]{:S(2)}, u32[]{:S(2)}) collective-permute-start(bf16[1312,128]{1,0:T(8,128)(2,1)S(1)} %pad_maximum_fusion.21), channel_id=1, source_target_pairs={{16,8},{17,9},{24,0},{25,1},{26,2},{27,3},{28,4},{29,5},{30,6},{31... | collective-permute-start | bytes 1007624 | tf_op jit(solution)/shard_map/ppermute | solution.py:965
  624.5 8.2 %collective-permute-start.42 = (bf16[4,1312,128]{2,1,0:T(8,128)(2,1)}, bf16[4,1312,128]{2,1,0:T(8,128)(2,1)}, u32[]{:S(2)}, u32[]{:S(2)}) collective-permute-start(bf16[4,1312,128]{2,1,0:T(8,128)(2,1)} %pad_maximum_fusion.10.who), channel_id=1, source_target_pairs={{0,1},{1,0},{2,3},{3,2},{4,5},{5,4},{6,7},{7,6},{8,9},{9,8},{10,11... | collective-permute-start | bytes 4030472 | tf_op jit(solution)/shard_map/ppermute | solution.py:59
  625.5 34.6 %collective-permute-start.43 = (bf16[384,1024]{1,0:T(8,128)(2,1)}, bf16[384,1024]{1,0:T(8,128)(2,1)}, u32[]{:S(2)}, u32[]{:S(2)}) collective-permute-start(bf16[384,1024]{1,0:T(8,128)(2,1)} %pad_maximum_fusion.18), channel_id=1, source_target_pairs={{0,4},{1,5},{2,6},{3,7},{4,0},{5,1},{6,2},{7,3},{8,12},{9,13},{10,... | collective-permute-start | bytes 2359304 | tf_op jit(solution)/shard_map/ppermute | solution.py:59
  (82 other events, 522.7 us)
Sparse Core Ops, SparseCore 0:
  660.3 75.6 all-gather.2

commit v4 on v3

--- a/solution.py
+++ b/solution.py
@@ -926,7 +926,6 @@
     feed_got = jnp.concatenate([feed_part[:1], feed_part])
     feed_got = lax.all_to_all(feed_got, "dp", 0, 0, tiled=True)
     head_q, head_kv = added(head_q), added(head_kv)
-    head_q, head_kv, da = after((head_q, head_kv, da))
     head_stage = line_start(
         jnp.stack(
             [
@@ -947,7 +946,6 @@
     )
     chain = [(8 * d + s, 8 * d + s + 2) for d in range(4) for s in range(8) if 8 * d + s < 30]
     before = lax.ppermute(feed_flat[-16:], ("dp", "seq"), chain)
-    head_stage, gains, before = after((head_stage, gains, before))
     head_part = added(line_next(head_stage))
     tail = jnp.where(
         line < 2,
@@ -955,6 +953,7 @@
         head_part[1024 - TAIL :],
     )
     ring = [(8 * d + s, 8 * d + (s + 2) % 8) for d in range(4) for s in range(8)]
+    tail, gains, before = after((tail, gains, before))
     tail = lax.ppermute(tail, ("dp", "seq"), ring)
     tail, da = after((tail, da))
     dx_rows = to_home(da)
@@ -998,39 +997,48 @@
     return r * (dg - xh * jnp.mean(dg * xh, axis=-1, keepdims=True))
 
 
-def into_kernel(count, *refs):
-    grads, weights = refs[:count], refs[count : 2 * count]
-    x, out, gain_out = refs[2 * count :]
-    total = None
-    for grad, weight in zip(grads, weights):
-        part = dot_t(grad[...], weight[...])
-        total = part if total is None else total + part
-    out[...] = total.astype(BF)
-    xv = x[...].astype(F32)
-    xh = xv * lax.rsqrt(jnp.mean(xv * xv, axis=-1, keepdims=True) + EPS_NORM)
-
-    @pl.when(pl.program_id(0) == 0)
+def into_kernel(own_blocks, dq, dk, dv, dk_far, dv_far, x, x_far, wq, wk, wv, own, far, gain_out):
+    step = pl.program_id(0)
+
+    @pl.when(step == 0)
     def _():
         gain_out[...] = jnp.zeros_like(gain_out)
 
-    gain_out[...] += jnp.sum((total * xh).reshape(xv.shape[0] // 8, 8, D), axis=0)
-
-
-def into_input(grads, weights, x):
-    rows = x.shape[0]
+    def finish(total, rows, out):
+        out[...] = total.astype(BF)
+        xv = rows[...].astype(F32)
+        xh = xv * lax.rsqrt(jnp.mean(xv * xv, axis=-1, keepdims=True) + EPS_NORM)
+        gain_out[...] += jnp.sum((total * xh).reshape(xv.shape[0] // 8, 8, D), axis=0)
+
+    @pl.when(step < own_blocks)
+    def _():
+        total = dot_t(dk[...], wk[...]) + dot_t(dv[...], wv[...]) + dot_t(dq[...], wq[...])
+        finish(total, x, own)
+
+    @pl.when(step >= own_blocks)
+    def _():
+        finish(dot_t(dk_far[...], wk[...]) + dot_t(dv_far[...], wv[...]), x_far, far)
+
+
+def into_input(dq, dk, dv, dk_far, dv_far, x, x_far, wq, wk, wv):
     bm = 256
-    row = lambda width: pl.BlockSpec((bm, width), lambda i: (i, 0))
+    own_blocks, far_blocks = x.shape[0] // bm, x_far.shape[0] // bm
+    near = lambda width: pl.BlockSpec((bm, width), lambda i: (jnp.minimum(i, own_blocks - 1), 0))
+    away = lambda width: pl.BlockSpec((bm, width), lambda i: (jnp.maximum(i - own_blocks, 0), 0))
     return pl.pallas_call(
-        functools.partial(into_kernel, len(grads)),
-        out_shape=[jax.ShapeDtypeStruct((rows, D), BF), jax.ShapeDtypeStruct((8, D), F32)],
-        grid=(rows // bm,),
-        in_specs=[row(grad.shape[1]) for grad in grads]
-        + [whole(weight.shape) for weight in weights]
-        + [row(D)],
-        out_specs=[row(D), whole((8, D))],
+        functools.partial(into_kernel, own_blocks),
+        out_shape=[
+            jax.ShapeDtypeStruct(x.shape, BF),
+            jax.ShapeDtypeStruct(x_far.shape, BF),
+            jax.ShapeDtypeStruct((8, D), F32),
+        ],
+        grid=(own_blocks + far_blocks,),
+        in_specs=[near(QW), near(KW), near(KW), away(KW), away(KW), near(D), away(D)]
+        + [whole(weight.shape) for weight in (wq, wk, wv)],
+        out_specs=[near(D), away(D), whole((8, D))],
         compiler_params=params(),
         cost_estimate=SMALL,
-    )(*grads, *weights, x)
+    )(dq, dk, dv, dk_far, dv_far, x, x_far, wq, wk, wv)
 
 
 def tables(positions):
@@ -1194,6 +1202,11 @@
     filled, waits = (), [y_core]
     back = []
     if fast:
+        states = [
+            jnp.concatenate([state, jnp.zeros((ROWS * LANES - SHARD,), F32)]).reshape(ROWS, LANES)
+            for state in (master, moment1, moment2)
+        ]
+        waits += states
         cols = cut(da_out, core)
         grad_o = share(t_dot(o, cols).astype(BF), t_dot(o_got, cols).astype(BF))
         flow["wo"] = plane_step(jnp.concatenate(grad_o), "wo", 0)
@@ -1241,10 +1254,11 @@
         feed_stage = line_next(feed_stage)
         dk_own, dk_far = after((dk_own, dk_far), kept(feed_stage, head_q, head_kv))
 
-    da_far, gain_far = into_input((dk_far, dv_far), (w_k, w_v), x_far)
+    da_own, da_far, gain_rows = into_input(
+        dq, dk_own, dv_own, dk_far, dv_far, x, x_far, w_q, w_k, w_v
+    )
+    dg1 = jnp.sum(gain_rows, axis=0)
     da_far = da_far.reshape(chips - 1, CORES, 2 * p, D)
-    da_own, gain_own = into_input((dq, dk_own, dv_own), (w_q, w_k, w_v), x)
-    dg1 = jnp.sum(gain_far + gain_own, axis=0)
     far_keep = lax.dynamic_index_in_dim(da_far, core, 1, keepdims=False)
     far_send = lax.dynamic_index_in_dim(da_far, 1 - core, 1, keepdims=False)
     sent = jnp.concatenate([core_rows(da_own, 1 - core), far_send.reshape(-1, D)])
@@ -1271,11 +1285,6 @@
 
     if fast:
         gains = [dg1, jnp.sum(dgq, 0), jnp.sum(dgk, 0), 0.5 * dg2]
-        states = [
-            jnp.concatenate([state, jnp.zeros((ROWS * LANES - SHARD,), F32)]).reshape(ROWS, LANES)
-            for state in (master, moment1, moment2)
-        ]
-        states = after(states, x)
         *results, block, dx_rows = fast_grads(
             core, feed_stage, head_q, head_kv, gains, states, da, lambda da: home_start(to_dx(da), half, p, c)
         )

time: 766 us -> 767 us (level)
    ppermute x27, waiting for transfers between devices: 55.9 us -> 65.2 us  [xor_seq(): return lax.ppermute(block, 'seq', [(i, i ^ mask) for i in range(count)])]
    unnamed x207 -> x209, local copies, waits for them, and re-layouts: 28.4 us -> 23.8 us
    pallas_call x2 -> x1, Pallas kernels: 18.3 us -> 16.6 us  [into_input(): pl.pallas_call(functools.partial(into_kernel, own_blocks), out_shape=[jax...]
  transfers between devices with their start and end apart: 47 -> 47, of which waited for: 14 -> 13; matrix products, arithmetic and copies ran while one was open for 20% -> 20% of each run, Pallas kernels for 40% -> 39%
where the time goes in v4:
time: 767 us; the launch traced here: 757 us
  Pallas kernels  327 us (43%)
  waiting for transfers between devices  153 us (20%)
  other arithmetic  82.5 us (11%)
  local copies, waits for them, and re-layouts  77.8 us (10%)
  starting transfers between devices  53.9 us (7%)
  matrix products  45.1 us (6%)
  between operations  16.6 us (2%)
    pallas_call x4, Pallas kernels, attend_back(): pl.pallas_call(functools.partial(attend_back_kernel, own_p, n_oth, chunk)...  116 us
    ppermute x27, waiting for transfers between devices, xor_seq(): return lax.ppermute(block, 'seq', [(i, i ^ mask) for i in range(count)])  65.2 us
    all_gather x1, waiting for transfers between devices, gather_weights(): blocks = lax.all_gather(block, 'seq', axis=0)  63.7 us
    pallas_call x2, Pallas kernels, attend(): pl.pallas_call(functools.partial(attend_kernel if cont else attend_wide_k...  50 us
    pallas_call x2, Pallas kernels, feed(): pl.pallas_call(feed_kernel, out_shape=[jax.ShapeDtypeStruct((total, D), F...  45.8 us
    pallas_call x7, Pallas kernels, matrix(): pl.pallas_call(functools.partial(matrix_kernel, per, split), out_shape=ja...  41.1 us
    dot_general x9, matrix products, t_dot(): lax.dot_general(left, right, (((0,), (0,)), ((), ())), preferred_element_...  38.4 us
    unnamed x209, local copies, waits for them, and re-layouts  23.8 us
  transfers between devices with their start and end apart: 47, of which 13 were waited for; matrix products, arithmetic and copies ran while one was open for 20% of the time, Pallas kernels for 39%

profile of v4, /device:TPU:0, one launch (start us, length us, event | category | flops | bytes accessed | tf_op | source)
XLA Modules:
  0.0 756.5 jit_solution(16404837718961625280)
XLA Ops:
  10.9 4.0 collective-permute-start.1
  20.1 4.2 fusion.44
  30.3 3.3 shard_map.162.refs_5_.refs_4_.wk
  34.6 3.3 shard_map.163.refs_6_.refs_5_.wv
  38.9 7.5 shard_map.161.refs_4_.wq
  49.6 8.3 %shard_map.164.wg = bf16[1024,1536]{1,0:T(8,128)(2,1)} custom-call(s32[2]{0:T(128)S(1)} %pad_add_fusion.3.place, bf16[122898,128]{1,0:T(8,128)(2,1)} %bitcast.181, bf16[122898,128]{1,0:T(8,128)(2,1)} %bitcast.182), custom_call_target="tpu_custom_call" | custom-call | flops 1000 | bytes 1000 | tf_op jit(solution)/shard_map/pallas_call | solution.py:621
  57.9 8.2 %shard_map.165.wu = bf16[1024,1536]{1,0:T(8,128)(2,1)} custom-call(s32[2]{0:T(128)S(1)} %pad_add_fusion.3.place, bf16[122898,128]{1,0:T(8,128)(2,1)} %bitcast.183, bf16[122898,128]{1,0:T(8,128)(2,1)} %bitcast.184), custom_call_target="tpu_custom_call" | custom-call | flops 1000 | bytes 1000 | tf_op jit(solution)/shard_map/pallas_call | solution.py:621
  73.0 14.1 %shard_map.166 = (bf16[1536,1024]{1,0:T(8,128)(2,1)}, bf16[1536,1024]{1,0:T(8,128)(2,1)}, bf16[1536,1024]{1,0:T(8,128)(2,1)}, bf16[1536,512]{1,0:T(8,128)(2,1)},...) custom-call(bf16[1536,1024]{1,0:T(8,128)(2,1)} %copy-done.13, f32[1,1024]{1,0:T(1,128)S(1)} %bitcast.167, ...), custom_call_target="tpu_custom_call" | custom-call | flops 1000 | bytes 1000 | tf_op jit(solution)/shard_map/pallas_call | solution.py:140
  90.4 5.6 shard_map.167.wd
  96.0 4.9 shard_map.168.wo
  100.9 3.4 collective-permute-start.7
  107.1 6.8 shard_map.169
  115.1 30.5 %shard_map.170 = (bf16[1024,1024]{1,0:T(8,128)(2,1)}, f32[4,2,1024]{2,1,0:T(2,128)S(1)}) custom-call(bf16[1536,1024]{1,0:T(8,128)(2,1)} %get-tuple-element.170.q, bf16[1536,512]{1,0:T(8,128)(2,1)} %get-tuple-element.159.k_own, bf16[1536,512]{1,0:T(8,128)(2,1)} %get-tuple-element.160.v_own, bf16[1024,512]{1,0:T(8,128)(2,1)S(1)} %copy-done.4, ...), custom_call_target="tpu_custom_call" | custom-call | flops 1000 | bytes 1000 | tf_op jit(solution)/shard_map/pallas_call | solution.py:260
  145.6 5.4 convolution_convert_fusion.5.part
  156.2 19.6 %shard_map.171 = (bf16[512,1024]{1,0:T(8,128)(2,1)}, f32[4,2,512]{2,1,0:T(2,128)S(1)}) custom-call(bf16[1536,1024]{1,0:T(8,128)(2,1)} %get-tuple-element.170.q, bf16[1536,512]{1,0:T(8,128)(2,1)} %get-tuple-element.159.k_own, bf16[1536,512]{1,0:T(8,128)(2,1)} %get-tuple-element.160.v_own, bf16[1024,512]{1,0:T(8,128)(2,1)} %get-tuple-element.166.k_oth, ...), custom_call_target="tpu_custom_call" | custom-call | flops 1000 | bytes 1000 | tf_op jit(solution)/shard_map/pallas_call | solution.py:260
  183.9 4.0 collective-permute-done.11.got
  187.9 28.8 %shard_map.172 = (f32[1536,1024]{1,0:T(8,128)}, bf16[1536,1024]{1,0:T(8,128)(2,1)}, bf16[1536,1536]{1,0:T(8,128)(2,1)}, bf16[1536,1536]{1,0:T(8,128)(2,1)}, bf16...) custom-call(bf16[1536,1024]{1,0:T(8,128)(2,1)} %copy-done.13, ...), custom_call_target="tpu_custom_call" | custom-call | flops 1000 | bytes 1000 | tf_op jit(solution)/shard_map/pallas_call | solution.py:502
  217.7 17.0 %shard_map.173 = (f32[1536,1024]{1,0:T(8,128)}, bf16[1536,1024]{1,0:T(8,128)(2,1)}, bf16[1536,1536]{1,0:T(8,128)(2,1)}, bf16[1536,1536]{1,0:T(8,128)(2,1)}, bf16...) custom-call(bf16[1536,1024]{1,0:T(8,128)(2,1)} %copy-done.13, ...), custom_call_target="tpu_custom_call", output_to_operand_aliasing={{0}: (8, {}), {1}: (9, {}), {2}: (10, {}), {3}: (11, {}), {... | custom-call | flops 1000 | bytes 1000 | tf_op jit(solution)/shard_map/pallas_call | solution.py:502
  235.0 3.2 pad_bitcast_fusion.2.rest_1_.master
  243.5 5.8 convolution_convert_fusion
  252.4 5.4 convolution_convert_fusion.1
  265.3 5.6 broadcast_select_fusion
  272.8 11.1 %shard_map.174 = (f32[1536,1024]{1,0:T(8,128)}, bf16[1536,1024]{1,0:T(8,128)(2,1)}, bf16[1536,1024]{1,0:T(8,128)(2,1)}, f32[8,1024]{1,0:T(8,128)S(1)}) custom-call(f32[1536,1024]{1,0:T(8,128)} %get-tuple-element.185.h1, bf16[1536,1024]{1,0:T(8,128)(2,1)} %copy-done.14, bf16[1024,1024]{1,0:T(8,128)(2,1)} %get-tuple-element.178.mine, ...), custom_call_target="tpu_custom_call" | custom-call | flops 1000 | bytes 1000 | tf_op jit(solution)/shard_map/pallas_call | solution.py:553
  283.9 6.9 shard_map.175
  290.8 3.4 convolution_convert_fusion.7
  294.2 3.8 broadcast_select_fusion.2
  315.1 28.8 %shard_map.176 = (bf16[1536,1024]{1,0:T(8,128)(2,1)}, bf16[1536,512]{1,0:T(8,128)(2,1)}, bf16[1536,512]{1,0:T(8,128)(2,1)}, bf16[1024,512]{1,0:T(8,128)(2,1)}, b...) custom-call(bf16[1536,1024]{1,0:T(8,128)(2,1)} %get-tuple-element.170.q, ...), custom_call_target="tpu_custom_call" | custom-call | flops 1000 | bytes 1000 | tf_op jit(solution)/shard_map/pallas_call | solution.py:434
  343.9 29.1 %shard_map.177 = (bf16[1536,1024]{1,0:T(8,128)(2,1)}, bf16[1536,512]{1,0:T(8,128)(2,1)}, bf16[1536,512]{1,0:T(8,128)(2,1)}, bf16[1024,512]{1,0:T(8,128)(2,1)}, b...) custom-call(bf16[1536,1024]{1,0:T(8,128)(2,1)} %get-tuple-element.17, ...), custom_call_target="tpu_custom_call", output_to_operand_aliasing={{0}: (23, {}), {1}: (24, {}), {2}: (25, {}), {3}: (26, {}),... | custom-call | flops 1000 | bytes 1000 | tf_op jit(solution)/shard_map/pallas_call | solution.py:434
  388.1 28.9 %shard_map.178 = (bf16[1536,1024]{1,0:T(8,128)(2,1)}, bf16[1536,512]{1,0:T(8,128)(2,1)}, bf16[1536,512]{1,0:T(8,128)(2,1)}, bf16[1024,512]{1,0:T(8,128)(2,1)}, b...) custom-call(bf16[1536,1024]{1,0:T(8,128)(2,1)} %get-tuple-element.17, ...), custom_call_target="tpu_custom_call", output_to_operand_aliasing={{0}: (23, {}), {1}: (24, {}), {2}: (25, {}), {3}: (26, {}),... | custom-call | flops 1000 | bytes 1000 | tf_op jit(solution)/shard_map/pallas_call | solution.py:434
  428.3 28.8 %shard_map.179 = (bf16[1536,1024]{1,0:T(8,128)(2,1)}, bf16[1536,512]{1,0:T(8,128)(2,1)}, bf16[1536,512]{1,0:T(8,128)(2,1)}, bf16[1024,512]{1,0:T(8,128)(2,1)}, b...) custom-call(bf16[1536,1024]{1,0:T(8,128)(2,1)} %get-tuple-element.17, ...), custom_call_target="tpu_custom_call", output_to_operand_aliasing={{0}: (23, {}), {1}: (24, {}), {2}: (25, {}), {3}: (26, {}),... | custom-call | flops 1000 | bytes 1000 | tf_op jit(solution)/shard_map/pallas_call | solution.py:434
  457.1 5.9 convolution_convert_fusion.4
  472.8 16.6 %shard_map.180 = (bf16[1536,1024]{1,0:T(8,128)(2,1)}, bf16[1024,1024]{1,0:T(8,128)(2,1)}, f32[8,1024]{1,0:T(8,128)S(1)}) custom-call(bf16[1536,1024]{1,0:T(8,128)(2,1)} %get-tuple-element.250.dq, bf16[1536,512]{1,0:T(8,128)(2,1)} %get-tuple-element.264.dk, bf16[1536,512]{1,0:T(8,128)(2,1)} %get-tuple-element.256.dv, bf16[1024,512]{1,0:T(8,128)(2,1)S(1)} %copy-done.7, ...), custom_call_target="tpu_custom_call" | custom-call | flops 1000 | bytes 1000 | tf_op jit(solution)/shard_map/pallas_call | solution.py:1028
  499.2 3.2 constant_dynamic-slice_fusion.4
  502.4 24.7 %collective-permute-done.29 = bf16[2880,128]{1,0:T(8,128)(2,1)S(1)} collective-permute-done((bf16[2880,128]{1,0:T(8,128)(2,1)S(1)}, bf16[2880,128]{1,0:T(8,128)(2,1)S(1)}, u32[]{:S(2)}, u32[]{:S(2)}) %collective-permute-start.29) | collective-permute-done | bytes 737312 | tf_op jit(solution)/shard_map/ppermute | solution.py:59
  531.6 9.3 %collective-permute-done.31 = bf16[2048,128]{1,0:T(8,128)(2,1)S(1)} collective-permute-done((bf16[2048,128]{1,0:T(8,128)(2,1)S(1)}, bf16[2048,128]{1,0:T(8,128)(2,1)S(1)}, u32[]{:S(2)}, u32[]{:S(2)}) %collective-permute-start.31) | collective-permute-done | bytes 524320 | tf_op jit(solution)/shard_map/ppermute | solution.py:708
  544.2 3.5 all-to-all-start.1
  552.3 6.1 collective-permute-done.33
  562.6 4.1 all-to-all-start
  570.7 13.1 %collective-permute-done.34 = bf16[1024,128]{1,0:T(8,128)(2,1)} collective-permute-done((bf16[1024,128]{1,0:T(8,128)(2,1)S(1)}, bf16[1024,128]{1,0:T(8,128)(2,1)}, u32[]{:S(2)}, u32[]{:S(2)}) %collective-permute-start.34) | collective-permute-done | bytes 262176 | tf_op jit(solution)/shard_map/ppermute | solution.py:59
  588.5 5.8 collective-permute-start.36
  600.0 3.5 collective-permute-done.37
  607.6 4.2 collective-permute-start.39
  617.0 7.5 collective-permute-done.40
  629.2 16.3 %shard_map.182 = (f32[3872,128]{1,0:T(8,128)}, f32[3872,128]{1,0:T(8,128)}, f32[3872,128]{1,0:T(8,128)}, bf16[3872,128]{1,0:T(8,128)(2,1)}) custom-call(s32[6]{0:T(128)S(1)} %stack.143.info, bf16[4,1312,128]{2,1,0:T(8,128)(2,1)} %pad_maximum_fusion.10.who, bf16[4,1312,128]{2,1,0:T(8,128)(2,1)} %collective-permute-done.42.other, ...), custom_call_target="tpu_custom_call" | custom-call | flops 1000 | bytes 1000 | tf_op jit(solution)/shard_map/pallas_call | solution.py:904
  645.5 15.5 %collective-permute-done.43 = bf16[384,1024]{1,0:T(8,128)(2,1)} collective-permute-done((bf16[384,1024]{1,0:T(8,128)(2,1)}, bf16[384,1024]{1,0:T(8,128)(2,1)}, u32[]{:S(2)}, u32[]{:S(2)}) %collective-permute-start.43) | collective-permute-done | bytes 786464 | tf_op jit(solution)/shard_map/ppermute | solution.py:59
  674.1 63.7 %all-gather.3.cloned.1.call-done = bf16[30976,128]{1,0:T(8,128)(2,1)} async-done(((bf16[3872,128]{1,0:T(8,128)(2,1)}), bf16[30976,128]{1,0:T(8,128)(2,1)}) %all-gather.3.cloned.1.call-update) | async-done | bytes 7929872 | tf_op jit(solution)/shard_map/all_gather | solution.py:984
  737.8 3.7 slice.445
  743.5 5.7 maximum_bitcast_fusion
  (467 shorter events, 187.9 us)
Async XLA Ops:
  10.9 38.7 %collective-permute-start.1 = (bf16[384,1024]{1,0:T(8,128)(2,1)}, bf16[384,1024]{1,0:T(8,128)(2,1)}, u32[]{:S(2)}, u32[]{:S(2)}) collective-permute-start(bf16[384,1024]{1,0:T(8,128)(2,1)} %get-tuple-element.360), channel_id=1, source_target_pairs={{0,4},{1,5},{2,6},{3,7},{4,0},{5,1},{6,2},{7,3},{8,12},{9,13},{10,... | collective-permute-start | bytes 2359304 | tf_op jit(solution)/shard_map/ppermute | solution.py:59
  14.9 53.3 %collective-permute-start = (bf16[384,1024]{1,0:T(8,128)(2,1)}, bf16[384,1024]{1,0:T(8,128)(2,1)}, u32[]{:S(2)}, u32[]{:S(2)}) collective-permute-start(bf16[384,1024]{1,0:T(8,128)(2,1)} %get-tuple-element.361), channel_id=1, source_target_pairs={{0,1},{1,0},{2,3},{3,2},{4,5},{5,4},{6,7},{7,6},{8,9},{9,8},{10,11... | collective-permute-start | bytes 2359304 | tf_op jit(solution)/shard_map/ppermute | solution.py:59
  15.7 52.3 %collective-permute-start.3 = (bf16[1,256,1024]{2,1,0:T(8,128)(2,1)}, bf16[1,256,1024]{2,1,0:T(8,128)(2,1)S(1)}, u32[]{:S(2)}, u32[]{:S(2)}) collective-permute-start(bf16[1,256,1024]{2,1,0:T(8,128)(2,1)} %constant_dynamic-slice_fusion), channel_id=1, source_target_pairs={{0,2},{1,3},{2,0},{3,1},{4,6},{5,7},{6,4},{7,5},{8,10},{9,11},{10,... | collective-permute-start | bytes 1572872 | tf_op jit(solution)/shard_map/ppermute | solution.py:59
  24.6 46.7 %copy-start.2 = (f32[1536,128]{1,0:T(8,128)}, f32[1536,128]{1,0:T(8,128)S(1)}, u32[]{:S(2)}) copy-start(f32[1536,128]{1,0:T(8,128)S(1)} %pad_maximum_fusion.15.refs_2_.cos_q.cos_o) | copy-start | bytes 2359300
  66.1 3.6 collective-permute-start.2
  67.2 19.9 %collective-permute-start.5 = (bf16[1,256,1024]{2,1,0:T(8,128)(2,1)S(1)}, bf16[1,256,1024]{2,1,0:T(8,128)(2,1)S(1)}, u32[]{:S(2)}, u32[]{:S(2)}) collective-permute-start(bf16[1,256,1024]{2,1,0:T(8,128)(2,1)S(1)} %slice_bitcast_fusion.1), channel_id=1, source_target_pairs={{0,2},{1,3},{2,0},{3,1},{4,6},{5,7},{6,4},{7,5},{8,10},{9,11},{10,... | collective-permute-start | bytes 1572872 | tf_op jit(solution)/shard_map/ppermute | solution.py:59
  68.0 21.3 %collective-permute-start.4 = (bf16[1,256,1024]{2,1,0:T(8,128)(2,1)S(1)}, bf16[1,256,1024]{2,1,0:T(8,128)(2,1)}, u32[]{:S(2)}, u32[]{:S(2)}) collective-permute-start(bf16[1,256,1024]{2,1,0:T(8,128)(2,1)S(1)} %collective-permute-done.3), channel_id=1, source_target_pairs={{0,1},{1,0},{2,3},{3,2},{4,5},{5,4},{6,7},{7,6},{8,9},{9,8},{10,11... | collective-permute-start | bytes 1572872 | tf_op jit(solution)/shard_map/ppermute | solution.py:59
  87.1 17.2 %collective-permute-start.6 = (bf16[1,256,1024]{2,1,0:T(8,128)(2,1)S(1)}, bf16[1,256,1024]{2,1,0:T(8,128)(2,1)}, u32[]{:S(2)}, u32[]{:S(2)}) collective-permute-start(bf16[1,256,1024]{2,1,0:T(8,128)(2,1)S(1)} %collective-permute-done.5), channel_id=1, source_target_pairs={{0,1},{1,0},{2,3},{3,2},{4,5},{5,4},{6,7},{7,6},{8,9},{9,8},{10,11... | collective-permute-start | bytes 1572872 | tf_op jit(solution)/shard_map/ppermute | solution.py:59
  100.9 50.1 %collective-permute-start.7 = (bf16[384,1024]{1,0:T(8,128)(2,1)S(1)}, bf16[384,1024]{1,0:T(8,128)(2,1)}, u32[]{:S(2)}, u32[]{:S(2)}) collective-permute-start(bf16[384,1024]{1,0:T(8,128)(2,1)S(1)} %copy-done.67), channel_id=1, source_target_pairs={{0,4},{1,5},{2,6},{3,7},{4,0},{5,1},{6,2},{7,3},{8,12},{9,13},{10,... | collective-permute-start | bytes 2359304 | tf_op jit(solution)/shard_map/ppermute | solution.py:59
  151.0 24.8 %collective-permute-start.8 = (bf16[384,1024]{1,0:T(8,128)(2,1)}, bf16[384,1024]{1,0:T(8,128)(2,1)}, u32[]{:S(2)}, u32[]{:S(2)}) collective-permute-start(bf16[384,1024]{1,0:T(8,128)(2,1)} %collective-permute-done.7), channel_id=1, source_target_pairs={{0,1},{1,0},{2,3},{3,2},{4,5},{5,4},{6,7},{7,6},{8,9},{9,8},{10,11... | collective-permute-start | bytes 2359304 | tf_op jit(solution)/shard_map/ppermute | solution.py:59
  151.0 28.1 %collective-permute-start.12 = (bf16[384,1024]{1,0:T(8,128)(2,1)S(1)}, bf16[384,1024]{1,0:T(8,128)(2,1)}, u32[]{:S(2)}, u32[]{:S(2)}) collective-permute-start(bf16[384,1024]{1,0:T(8,128)(2,1)S(1)} %copy-done.40), channel_id=1, source_target_pairs={{0,1},{1,0},{2,3},{3,2},{4,5},{5,4},{6,7},{7,6},{8,9},{9,8},{10,11... | collective-permute-start | bytes 2359304 | tf_op jit(solution)/shard_map/ppermute | solution.py:59
  177.3 39.4 %collective-permute-start.10 = (bf16[1536,1024]{1,0:T(8,128)(2,1)S(1)}, bf16[1536,1024]{1,0:T(8,128)(2,1)}, u32[]{:S(2)}, u32[]{:S(2)}) collective-permute-start(bf16[1536,1024]{1,0:T(8,128)(2,1)S(1)} %constant_dynamic-update-slice_fusion.5.o), channel_id=1, source_target_pairs={{0,1},{1,0},{2,3},{3,2},{4,5},{5,4},{6,7},{7,6},{8,9},{9,8},{10,11... | collective-permute-start | bytes 9437192 | tf_op jit(solution)/shard_map/ppermute | solution.py:59
  178.3 9.5 %collective-permute-start.11 = (bf16[1024,1024]{1,0:T(8,128)(2,1)}, bf16[1024,1024]{1,0:T(8,128)(2,1)}, u32[]{:S(2)}, u32[]{:S(2)}) collective-permute-start(bf16[1024,1024]{1,0:T(8,128)(2,1)} %convolution_convert_fusion.5.part), channel_id=1, source_target_pairs={{0,1},{1,0},{2,3},{3,2},{4,5},{5,4},{6,7},{7,6},{8,9},{9,8},{10,11... | collective-permute-start | bytes 6291464 | tf_op jit(solution)/shard_map/ppermute | solution.py:59
  181.7 34.9 %collective-permute-start.9 = (bf16[512,1024]{1,0:T(8,128)(2,1)S(1)}, bf16[512,1024]{1,0:T(8,128)(2,1)S(1)}, u32[]{:S(2)}, u32[]{:S(2)}) collective-permute-start(bf16[512,1024]{1,0:T(8,128)(2,1)S(1)} %convolution_convert_fusion.8.part), channel_id=1, source_target_pairs={{0,1},{1,0},{2,3},{3,2},{4,5},{5,4},{6,7},{7,6},{8,9},{9,8},{10,11... | collective-permute-start | bytes 3145736 | tf_op jit(solution)/shard_map/ppermute | solution.py:59
  234.7 30.7 %collective-permute-start.13 = (bf16[1536,1536]{1,0:T(8,128)(2,1)}, bf16[1536,1536]{1,0:T(8,128)(2,1)}, u32[]{:S(2)}, u32[]{:S(2)}) collective-permute-start(bf16[1536,1536]{1,0:T(8,128)(2,1)} %get-tuple-element.188), channel_id=1, source_target_pairs={{0,1},{1,0},{2,3},{3,2},{4,5},{5,4},{6,7},{7,6},{8,9},{9,8},{10,11... | collective-permute-start | bytes 14155784 | tf_op jit(solution)/shard_map/ppermute | solution.py:59
  239.4 18.4 %collective-permute-start.15 = (bf16[1024,1024]{1,0:T(8,128)(2,1)S(1)}, bf16[1024,1024]{1,0:T(8,128)(2,1)S(1)}, u32[]{:S(2)}, u32[]{:S(2)}) collective-permute-start(bf16[1024,1024]{1,0:T(8,128)(2,1)S(1)} %copy-done.47), channel_id=1, source_target_pairs={{0,1},{1,0},{2,3},{3,2},{4,5},{5,4},{6,7},{7,6},{8,9},{9,8},{10,11... | collective-permute-start | bytes 6291464 | tf_op jit(solution)/shard_map/ppermute | solution.py:59
  241.2 24.1 %collective-permute-start.14 = (bf16[768,1024]{1,0:T(8,128)(2,1)S(1)}, bf16[768,1024]{1,0:T(8,128)(2,1)S(1)}, u32[]{:S(2)}, u32[]{:S(2)}) collective-permute-start(bf16[768,1024]{1,0:T(8,128)(2,1)S(1)} %pad_maximum_fusion.6), channel_id=1, source_target_pairs={{0,1},{1,0},{2,3},{3,2},{4,5},{5,4},{6,7},{7,6},{8,9},{9,8},{10,11... | collective-permute-start | bytes 4718600 | tf_op jit(solution)/shard_map/ppermute | solution.py:59
  252.1 5.8 collective-permute-start.16
  262.3 37.1 %collective-permute-start.18 = (bf16[1024,768]{1,0:T(8,128)(2,1)}, bf16[1024,768]{1,0:T(8,128)(2,1)}, u32[]{:S(2)}, u32[]{:S(2)}) collective-permute-start(bf16[1024,768]{1,0:T(8,128)(2,1)} %get-tuple-element.320), channel_id=1, source_target_pairs={{0,16},{8,24},{16,0},{24,8},{1,17},{9,25},{17,1},{25,9},{2,18},{10... | collective-permute-start | bytes 4718600 | tf_op jit(solution)/shard_map/ppermute | solution.py:708
  263.8 36.6 %collective-permute-start.17 = (bf16[1024,768]{1,0:T(8,128)(2,1)}, bf16[1024,768]{1,0:T(8,128)(2,1)}, u32[]{:S(2)}, u32[]{:S(2)}) collective-permute-start(bf16[1024,768]{1,0:T(8,128)(2,1)} %get-tuple-element.322), channel_id=1, source_target_pairs={{0,8},{8,0},{16,24},{24,16},{1,9},{9,1},{17,25},{25,17},{2,10},{10... | collective-permute-start | bytes 4718600 | tf_op jit(solution)/shard_map/ppermute | solution.py:708
  300.4 72.6 %collective-permute-start.19 = (bf16[3072,256]{1,0:T(8,128)(2,1)}, bf16[3072,256]{1,0:T(8,128)(2,1)}, u32[]{:S(2)}, u32[]{:S(2)}) collective-permute-start(bf16[3072,256]{1,0:T(8,128)(2,1)} %get-tuple-element.318), channel_id=1, source_target_pairs={{0,8},{8,0},{16,24},{24,16},{1,9},{9,1},{17,25},{25,17},{2,10},{10... | collective-permute-start | bytes 4718600 | tf_op jit(solution)/shard_map/ppermute | solution.py:708
  305.3 67.6 %collective-permute-start.22 = (bf16[1024,384]{1,0:T(8,128)(2,1)}, bf16[1024,384]{1,0:T(8,128)(2,1)}, u32[]{:S(2)}, u32[]{:S(2)}) collective-permute-start(bf16[1024,384]{1,0:T(8,128)(2,1)} %get-tuple-element.346), channel_id=1, source_target_pairs={{0,8},{8,0},{16,24},{24,16},{1,9},{9,1},{17,25},{25,17},{2,10},{10... | collective-permute-start | bytes 2359304 | tf_op jit(solution)/shard_map/ppermute | solution.py:708
  305.8 67.2 %collective-permute-start.21 = (bf16[2048,256]{1,0:T(8,128)(2,1)}, bf16[2048,256]{1,0:T(8,128)(2,1)}, u32[]{:S(2)}, u32[]{:S(2)}) collective-permute-start(bf16[2048,256]{1,0:T(8,128)(2,1)} %get-tuple-element.340), channel_id=1, source_target_pairs={{0,16},{8,24},{16,0},{24,8},{1,17},{9,25},{17,1},{25,9},{2,18},{10... | collective-permute-start | bytes 3145736 | tf_op jit(solution)/shard_map/ppermute | solution.py:708
  309.6 63.4 %collective-permute-start.20 = (bf16[1024,384]{1,0:T(8,128)(2,1)}, bf16[1024,384]{1,0:T(8,128)(2,1)}, u32[]{:S(2)}, u32[]{:S(2)}) collective-permute-start(bf16[1024,384]{1,0:T(8,128)(2,1)} %get-tuple-element.348), channel_id=1, source_target_pairs={{0,16},{8,24},{16,0},{24,8},{1,17},{9,25},{17,1},{25,9},{2,18},{10... | collective-permute-start | bytes 2359304 | tf_op jit(solution)/shard_map/ppermute | solution.py:708
  375.5 41.5 %collective-permute-start.25 = (bf16[2048,128]{1,0:T(8,128)(2,1)}, bf16[2048,128]{1,0:T(8,128)(2,1)}, u32[]{:S(2)}, u32[]{:S(2)}) collective-permute-start(bf16[2048,128]{1,0:T(8,128)(2,1)} %get-tuple-element.368), channel_id=1, source_target_pairs={{0,8},{8,0},{16,24},{24,16},{1,9},{9,1},{17,25},{25,17},{2,10},{10... | collective-permute-start | bytes 1572872 | tf_op jit(solution)/shard_map/ppermute | solution.py:708
  379.9 37.1 %collective-permute-start.24 = (bf16[3072,128]{1,0:T(8,128)(2,1)S(1)}, bf16[3072,128]{1,0:T(8,128)(2,1)S(1)}, u32[]{:S(2)}, u32[]{:S(2)}) collective-permute-start(bf16[3072,128]{1,0:T(8,128)(2,1)S(1)} %get-tuple-element.344), channel_id=1, source_target_pairs={{0,16},{8,24},{16,0},{24,8},{1,17},{9,25},{17,1},{25,9},{2,18},{10... | collective-permute-start | bytes 2359304 | tf_op jit(solution)/shard_map/ppermute | solution.py:708
  386.6 40.8 %collective-permute-start.23 = (bf16[384,1024]{1,0:T(8,128)(2,1)}, bf16[384,1024]{1,0:T(8,128)(2,1)S(1)}, u32[]{:S(2)}, u32[]{:S(2)}) collective-permute-start(bf16[384,1024]{1,0:T(8,128)(2,1)} %pad_maximum_fusion.17), channel_id=1, source_target_pairs={{0,4},{1,5},{2,6},{3,7},{4,0},{5,1},{6,2},{7,3},{8,12},{9,13},{10,... | collective-permute-start | bytes 2359304 | tf_op jit(solution)/shard_map/ppermute | solution.py:59
  422.2 40.9 %collective-permute-start.26 = (bf16[2,2880,128]{2,1,0:T(8,128)(2,1)S(1)}, bf16[2,2880,128]{2,1,0:T(8,128)(2,1)S(1)}, u32[]{:S(2)}, u32[]{:S(2)}) collective-permute-start(bf16[2,2880,128]{2,1,0:T(8,128)(2,1)S(1)} %get-tuple-element.330), channel_id=1, source_target_pairs={{0,2},{1,3},{2,0},{3,1},{4,6},{5,7},{6,4},{7,5},{8,10},{9,11},{10,... | collective-permute-start | bytes 4423688 | tf_op jit(solution)/shard_map/ppermute | solution.py:59
  494.4 32.7 %collective-permute-start.29 = (bf16[2880,128]{1,0:T(8,128)(2,1)S(1)}, bf16[2880,128]{1,0:T(8,128)(2,1)S(1)}, u32[]{:S(2)}, u32[]{:S(2)}) collective-permute-start(bf16[2880,128]{1,0:T(8,128)(2,1)S(1)} %get-tuple-element.362), channel_id=1, source_target_pairs={{0,4},{1,5},{2,6},{3,7},{4,0},{5,1},{6,2},{7,3},{8,12},{9,13},{10,... | collective-permute-start | bytes 2211848 | tf_op jit(solution)/shard_map/ppermute | solution.py:59
  497.0 30.0 %collective-permute-start.28 = (bf16[2048,256]{1,0:T(8,128)(2,1)S(1)}, bf16[2048,256]{1,0:T(8,128)(2,1)S(1)}, u32[]{:S(2)}, u32[]{:S(2)}) collective-permute-start(bf16[2048,256]{1,0:T(8,128)(2,1)S(1)} %get-tuple-element.336), channel_id=1, source_target_pairs={{0,16},{8,24},{16,0},{24,8},{1,17},{9,25},{17,1},{25,9},{2,18},{10... | collective-permute-start | bytes 3145736 | tf_op jit(solution)/shard_map/ppermute | solution.py:708
  498.3 28.7 %collective-permute-start.27 = (bf16[1024,512]{1,0:T(8,128)(2,1)}, bf16[1024,512]{1,0:T(8,128)(2,1)S(1)}, u32[]{:S(2)}, u32[]{:S(2)}) collective-permute-start(bf16[1024,512]{1,0:T(8,128)(2,1)} %get-tuple-element.338), channel_id=1, source_target_pairs={{0,8},{8,0},{16,24},{24,16},{1,9},{9,1},{17,25},{25,17},{2,10},{10... | collective-permute-start | bytes 3145736 | tf_op jit(solution)/shard_map/ppermute | solution.py:708
  499.1 30.8 %collective-permute-start.32 = (bf16[1280,1024]{1,0:T(8,128)(2,1)S(1)}, bf16[1280,1024]{1,0:T(8,128)(2,1)S(1)}, u32[]{:S(2)}, u32[]{:S(2)}) collective-permute-start(bf16[1280,1024]{1,0:T(8,128)(2,1)S(1)} %pad_maximum_fusion.4), channel_id=1, source_target_pairs={{0,1},{1,0},{2,3},{3,2},{4,5},{5,4},{6,7},{7,6},{8,9},{9,8},{10,11... | collective-permute-start | bytes 7864328 | tf_op jit(solution)/shard_map/ppermute | solution.py:59
  527.5 13.4 %collective-permute-start.31 = (bf16[2048,128]{1,0:T(8,128)(2,1)S(1)}, bf16[2048,128]{1,0:T(8,128)(2,1)S(1)}, u32[]{:S(2)}, u32[]{:S(2)}) collective-permute-start(bf16[2048,128]{1,0:T(8,128)(2,1)S(1)} %get-tuple-element.364), channel_id=1, source_target_pairs={{0,8},{8,0},{16,24},{24,16},{1,9},{9,1},{17,25},{25,17},{2,10},{10... | collective-permute-start | bytes 1572872 | tf_op jit(solution)/shard_map/ppermute | solution.py:708
  528.4 13.1 %collective-permute-start.30 = (bf16[1024,256]{1,0:T(8,128)(2,1)S(1)}, bf16[1024,256]{1,0:T(8,128)(2,1)S(1)}, u32[]{:S(2)}, u32[]{:S(2)}) collective-permute-start(bf16[1024,256]{1,0:T(8,128)(2,1)S(1)} %get-tuple-element.366), channel_id=1, source_target_pairs={{0,16},{8,24},{16,0},{24,8},{1,17},{9,25},{17,1},{25,9},{2,18},{10... | collective-permute-start | bytes 1572872 | tf_op jit(solution)/shard_map/ppermute | solution.py:708
  543.2 15.2 %collective-permute-start.33 = (bf16[2,1024,128]{2,1,0:T(8,128)(2,1)}, bf16[2,1024,128]{2,1,0:T(8,128)(2,1)}, u32[]{:S(2)}, u32[]{:S(2)}) collective-permute-start(bf16[2,1024,128]{2,1,0:T(8,128)(2,1)} %dynamic-slice_bitcast_fusion.9), channel_id=1, source_target_pairs={{0,2},{1,3},{2,0},{3,1},{4,6},{5,7},{6,4},{7,5},{8,10},{9,11},{10,... | collective-permute-start | bytes 1572872 | tf_op jit(solution)/shard_map/ppermute | solution.py:59
  544.2 17.6 %all-to-all-start.1 = ((bf16[4,960,128]{2,1,0:T(8,128)(2,1)}), bf16[4,960,128]{2,1,0:T(8,128)(2,1)S(1)}, u32[]{:S(2)}, u32[]{:S(2)}) async-start(bf16[4,960,128]{2,1,0:T(8,128)(2,1)} %pad_maximum_fusion.14), calls=%async_computation.1 | async-start | bytes 1966080 | tf_op jit(solution)/shard_map/all_to_all | solution.py:927
  550.2 44.2 %collective-permute-start.38 = (bf16[1,512,1024]{2,1,0:T(8,128)(2,1)}, bf16[1,512,1024]{2,1,0:T(8,128)(2,1)}, u32[]{:S(2)}, u32[]{:S(2)}) collective-permute-start(bf16[1,512,1024]{2,1,0:T(8,128)(2,1)} %fusion.37), channel_id=1, source_target_pairs={{0,2},{1,3},{2,0},{3,1},{4,6},{5,7},{6,4},{7,5},{8,10},{9,11},{10,... | collective-permute-start | bytes 3145736 | tf_op jit(solution)/shard_map/ppermute | solution.py:59
  560.5 23.4 %collective-permute-start.34 = (bf16[1024,128]{1,0:T(8,128)(2,1)S(1)}, bf16[1024,128]{1,0:T(8,128)(2,1)}, u32[]{:S(2)}, u32[]{:S(2)}) collective-permute-start(bf16[1024,128]{1,0:T(8,128)(2,1)S(1)} %dynamic-slice_bitcast_fusion.10), channel_id=1, source_target_pairs={{0,4},{1,5},{2,6},{3,7},{4,0},{5,1},{6,2},{7,3},{8,12},{9,13},{10,... | collective-permute-start | bytes 786440 | tf_op jit(solution)/shard_map/ppermute | solution.py:59
  562.6 34.7 %all-to-all-start = ((f32[32,18,128]{2,1,0:T(8,128)}), f32[32,18,128]{2,1,0:T(8,128)}, u32[]{:S(2)}, u32[]{:S(2)}) async-start(f32[32,18,128]{2,1,0:T(8,128)} %broadcast_in_dim.59), calls=%async_computation | async-start | bytes 786432 | tf_op jit(solution)/shard_map/all_to_all | solution.py:922
  566.7 171.1 %all-gather.3.cloned.1.call-start = ((), (), s32[]{:S(2)}) async-start(), calls=%async_computation.2 | async-start | bytes 8921088 | tf_op jit(solution)/shard_map/all_gather | solution.py:984
  567.0 18.0 %collective-permute-start.35 = (bf16[4,960,128]{2,1,0:T(8,128)(2,1)S(1)}, bf16[4,960,128]{2,1,0:T(8,128)(2,1)S(1)}, u32[]{:S(2)}, u32[]{:S(2)}) collective-permute-start(bf16[4,960,128]{2,1,0:T(8,128)(2,1)S(1)} %all-to-all-done.1.who), channel_id=1, source_target_pairs={{0,1},{1,0},{2,3},{3,2},{4,5},{5,4},{6,7},{7,6},{8,9},{9,8},{10,11... | collective-permute-start | bytes 2949128 | tf_op jit(solution)/shard_map/ppermute | solution.py:59
  588.5 8.9 %collective-permute-start.36 = (f32[16,128]{1,0:T(8,128)S(1)}, f32[16,128]{1,0:T(8,128)S(1)}, u32[]{:S(2)}, u32[]{:S(2)}) collective-permute-start(f32[16,128]{1,0:T(8,128)S(1)} %slice.430), channel_id=1, source_target_pairs={{0,2},{1,3},{2,4},{3,5},{4,6},{5,7},{6,8},{7,9},{8,10},{9,11},{10,... | collective-permute-start | bytes 24584 | tf_op jit(solution)/shard_map/ppermute | solution.py:948
  597.4 6.2 collective-permute-start.37
  607.6 9.3 %collective-permute-start.39 = (bf16[1312,128]{1,0:T(8,128)(2,1)S(1)}, bf16[1312,128]{1,0:T(8,128)(2,1)S(1)}, u32[]{:S(2)}, u32[]{:S(2)}) collective-permute-start(bf16[1312,128]{1,0:T(8,128)(2,1)S(1)} %pad_maximum_fusion.21), channel_id=1, source_target_pairs={{0,8},{1,9},{8,0},{9,1},{10,2},{11,3},{12,4},{13,5},{14,6},{15,7}} | collective-permute-start | bytes 1007624 | tf_op jit(solution)/shard_map/ppermute | solution.py:964
  611.8 12.7 %collective-permute-start.40 = (bf16[1312,128]{1,0:T(8,128)(2,1)S(1)}, bf16[1312,128]{1,0:T(8,128)(2,1)S(1)}, u32[]{:S(2)}, u32[]{:S(2)}) collective-permute-start(bf16[1312,128]{1,0:T(8,128)(2,1)S(1)} %pad_maximum_fusion.21), channel_id=1, source_target_pairs={{16,0},{17,1},{18,2},{19,3},{20,4},{21,5},{22,6},{23,7},{24,8},{25... | collective-permute-start | bytes 1007624 | tf_op jit(solution)/shard_map/ppermute | solution.py:964
  613.1 11.4 %collective-permute-start.41 = (bf16[1312,128]{1,0:T(8,128)(2,1)S(1)}, bf16[1312,128]{1,0:T(8,128)(2,1)S(1)}, u32[]{:S(2)}, u32[]{:S(2)}) collective-permute-start(bf16[1312,128]{1,0:T(8,128)(2,1)S(1)} %pad_maximum_fusion.21), channel_id=1, source_target_pairs={{16,8},{17,9},{24,0},{25,1},{26,2},{27,3},{28,4},{29,5},{30,6},{31... | collective-permute-start | bytes 1007624 | tf_op jit(solution)/shard_map/ppermute | solution.py:964
  625.7 3.4 collective-permute-start.42
  626.7 34.2 %collective-permute-start.43 = (bf16[384,1024]{1,0:T(8,128)(2,1)}, bf16[384,1024]{1,0:T(8,128)(2,1)}, u32[]{:S(2)}, u32[]{:S(2)}) collective-permute-start(bf16[384,1024]{1,0:T(8,128)(2,1)} %pad_maximum_fusion.18), channel_id=1, source_target_pairs={{0,4},{1,5},{2,6},{3,7},{4,0},{5,1},{6,2},{7,3},{8,12},{9,13},{10,... | collective-permute-start | bytes 2359304 | tf_op jit(solution)/shard_map/ppermute | solution.py:59
  (82 other events, 540.6 us)
Sparse Core Ops, SparseCore 0:
  661.1 76.6 all-gather.2

commit v5 on v3

--- a/solution.py
+++ b/solution.py
@@ -926,7 +926,6 @@
     feed_got = jnp.concatenate([feed_part[:1], feed_part])
     feed_got = lax.all_to_all(feed_got, "dp", 0, 0, tiled=True)
     head_q, head_kv = added(head_q), added(head_kv)
-    head_q, head_kv, da = after((head_q, head_kv, da))
     head_stage = line_start(
         jnp.stack(
             [
@@ -1194,6 +1193,11 @@
     filled, waits = (), [y_core]
     back = []
     if fast:
+        states = [
+            jnp.concatenate([state, jnp.zeros((ROWS * LANES - SHARD,), F32)]).reshape(ROWS, LANES)
+            for state in (master, moment1, moment2)
+        ]
+        waits += states
         cols = cut(da_out, core)
         grad_o = share(t_dot(o, cols).astype(BF), t_dot(o_got, cols).astype(BF))
         flow["wo"] = plane_step(jnp.concatenate(grad_o), "wo", 0)
@@ -1271,11 +1275,6 @@
 
     if fast:
         gains = [dg1, jnp.sum(dgq, 0), jnp.sum(dgk, 0), 0.5 * dg2]
-        states = [
-            jnp.concatenate([state, jnp.zeros((ROWS * LANES - SHARD,), F32)]).reshape(ROWS, LANES)
-            for state in (master, moment1, moment2)
-        ]
-        states = after(states, x)
         *results, block, dx_rows = fast_grads(
             core, feed_stage, head_q, head_kv, gains, states, da, lambda da: home_start(to_dx(da), half, p, c)
         )

time: 766 us -> 772 us (level)
  waiting for transfers between devices: 151 us -> 164 us
    unnamed x207 -> x211, local copies, waits for them, and re-layouts: 28.4 us -> 33.4 us
  transfers between devices with their start and end apart: 47 -> 47, of which waited for: 14 -> 13; matrix products, arithmetic and copies ran while one was open for 20% -> 19% of each run, Pallas kernels for 40% -> 39%
where the time goes in v5:
time: 772 us; the launch traced here: 761 us
  Pallas kernels  329 us (43%)
  waiting for transfers between devices  164 us (21%)
  local copies, waits for them, and re-layouts  82.8 us (11%)
  other arithmetic  75.1 us (10%)
  starting transfers between devices  48 us (6%)
  matrix products  45.1 us (6%)
  between operations  16.4 us (2%)
    pallas_call x4, Pallas kernels, attend_back(): pl.pallas_call(functools.partial(attend_back_kernel, own_p, n_oth, chunk)...  115 us
    all_gather x1, waiting for transfers between devices, gather_weights(): blocks = lax.all_gather(block, 'seq', axis=0)  62.5 us
    ppermute x27, waiting for transfers between devices, xor_seq(): return lax.ppermute(block, 'seq', [(i, i ^ mask) for i in range(count)])  58.9 us
    pallas_call x2, Pallas kernels, attend(): pl.pallas_call(functools.partial(attend_kernel if cont else attend_wide_k...  50.1 us
    pallas_call x2, Pallas kernels, feed(): pl.pallas_call(feed_kernel, out_shape=[jax.ShapeDtypeStruct((total, D), F...  46 us
    pallas_call x7, Pallas kernels, matrix(): pl.pallas_call(functools.partial(matrix_kernel, per, split), out_shape=ja...  41.1 us
    dot_general x9, matrix products, t_dot(): lax.dot_general(left, right, (((0,), (0,)), ((), ())), preferred_element_...  38.4 us
    unnamed x211, local copies, waits for them, and re-layouts  33.4 us
  transfers between devices with their start and end apart: 47, of which 13 were waited for; matrix products, arithmetic and copies ran while one was open for 19% of the time, Pallas kernels for 39%

profile of v5, /device:TPU:0, one launch (start us, length us, event | category | flops | bytes accessed | tf_op | source)
XLA Modules:
  0.0 760.9 jit_solution(13346423998417421171)
XLA Ops:
  10.9 4.0 collective-permute-start.1
  20.1 4.2 fusion.43
  29.7 3.3 shard_map.162.refs_5_.refs_4_.refs_2_
  34.0 3.3 shard_map.163.refs_6_.refs_5_.refs_3_
  38.3 7.5 shard_map.161.refs_4_.refs_3_
  49.6 8.2 %shard_map.164.wg = bf16[1024,1536]{1,0:T(8,128)(2,1)} custom-call(s32[2]{0:T(128)S(1)} %pad_add_fusion.3.place, bf16[122898,128]{1,0:T(8,128)(2,1)} %bitcast.182, bf16[122898,128]{1,0:T(8,128)(2,1)} %bitcast.183), custom_call_target="tpu_custom_call" | custom-call | flops 1000 | bytes 1000 | tf_op jit(solution)/shard_map/pallas_call | solution.py:621
  57.8 8.2 %shard_map.165.wu = bf16[1024,1536]{1,0:T(8,128)(2,1)} custom-call(s32[2]{0:T(128)S(1)} %pad_add_fusion.3.place, bf16[122898,128]{1,0:T(8,128)(2,1)} %bitcast.184, bf16[122898,128]{1,0:T(8,128)(2,1)} %bitcast.185), custom_call_target="tpu_custom_call" | custom-call | flops 1000 | bytes 1000 | tf_op jit(solution)/shard_map/pallas_call | solution.py:621
  72.9 14.1 %shard_map.166 = (bf16[1536,1024]{1,0:T(8,128)(2,1)}, bf16[1536,1024]{1,0:T(8,128)(2,1)}, bf16[1536,1024]{1,0:T(8,128)(2,1)}, bf16[1536,512]{1,0:T(8,128)(2,1)},...) custom-call(bf16[1536,1024]{1,0:T(8,128)(2,1)} %copy-done.12, f32[1,1024]{1,0:T(1,128)S(1)} %bitcast.168, ...), custom_call_target="tpu_custom_call" | custom-call | flops 1000 | bytes 1000 | tf_op jit(solution)/shard_map/pallas_call | solution.py:140
  90.3 5.6 shard_map.167.wd
  96.0 4.9 shard_map.168.wo
  100.8 3.4 collective-permute-start.7
  106.9 6.8 shard_map.169
  114.9 30.5 %shard_map.170 = (bf16[1024,1024]{1,0:T(8,128)(2,1)}, f32[4,2,1024]{2,1,0:T(2,128)S(1)}) custom-call(bf16[1536,1024]{1,0:T(8,128)(2,1)} %get-tuple-element.172.q, bf16[1536,512]{1,0:T(8,128)(2,1)} %get-tuple-element.161.k_own, bf16[1536,512]{1,0:T(8,128)(2,1)} %get-tuple-element.162.v_own, bf16[1024,512]{1,0:T(8,128)(2,1)S(1)} %copy-done.4, ...), custom_call_target="tpu_custom_call" | custom-call | flops 1000 | bytes 1000 | tf_op jit(solution)/shard_map/pallas_call | solution.py:260
  145.4 5.4 convolution_convert_fusion.5.part
  153.5 19.7 %shard_map.171 = (bf16[512,1024]{1,0:T(8,128)(2,1)}, f32[4,2,512]{2,1,0:T(2,128)S(1)}) custom-call(bf16[1536,1024]{1,0:T(8,128)(2,1)} %get-tuple-element.172.q, bf16[1536,512]{1,0:T(8,128)(2,1)} %get-tuple-element.161.k_own, bf16[1536,512]{1,0:T(8,128)(2,1)} %get-tuple-element.162.v_own, bf16[1024,512]{1,0:T(8,128)(2,1)} %get-tuple-element.168.k_oth, ...), custom_call_target="tpu_custom_call" | custom-call | flops 1000 | bytes 1000 | tf_op jit(solution)/shard_map/pallas_call | solution.py:260
  185.7 28.9 %shard_map.172 = (f32[1536,1024]{1,0:T(8,128)}, bf16[1536,1024]{1,0:T(8,128)(2,1)}, bf16[1536,1536]{1,0:T(8,128)(2,1)}, bf16[1536,1536]{1,0:T(8,128)(2,1)}, bf16...) custom-call(bf16[1536,1024]{1,0:T(8,128)(2,1)} %copy-done.12, ...), custom_call_target="tpu_custom_call" | custom-call | flops 1000 | bytes 1000 | tf_op jit(solution)/shard_map/pallas_call | solution.py:502
  215.5 17.1 %shard_map.173 = (f32[1536,1024]{1,0:T(8,128)}, bf16[1536,1024]{1,0:T(8,128)(2,1)}, bf16[1536,1536]{1,0:T(8,128)(2,1)}, bf16[1536,1536]{1,0:T(8,128)(2,1)}, bf16...) custom-call(bf16[1536,1024]{1,0:T(8,128)(2,1)} %copy-done.12, ...), custom_call_target="tpu_custom_call", output_to_operand_aliasing={{0}: (8, {}), {1}: (9, {}), {2}: (10, {}), {3}: (11, {}), {... | custom-call | flops 1000 | bytes 1000 | tf_op jit(solution)/shard_map/pallas_call | solution.py:502
  243.6 5.8 convolution_convert_fusion
  252.5 5.4 convolution_convert_fusion.1
  264.9 5.6 broadcast_select_fusion
  272.4 11.1 %shard_map.174 = (f32[1536,1024]{1,0:T(8,128)}, bf16[1536,1024]{1,0:T(8,128)(2,1)}, bf16[1536,1024]{1,0:T(8,128)(2,1)}, f32[8,1024]{1,0:T(8,128)S(1)}) custom-call(f32[1536,1024]{1,0:T(8,128)} %get-tuple-element.187.h1, bf16[1536,1024]{1,0:T(8,128)(2,1)} %copy-done.13, bf16[1024,1024]{1,0:T(8,128)(2,1)} %get-tuple-element.180.mine, ...), custom_call_target="tpu_custom_call" | custom-call | flops 1000 | bytes 1000 | tf_op jit(solution)/shard_map/pallas_call | solution.py:553
  283.5 6.9 shard_map.175
  290.5 3.4 convolution_convert_fusion.7
  293.9 3.8 broadcast_select_fusion.2
  314.9 28.8 %shard_map.176 = (bf16[1536,1024]{1,0:T(8,128)(2,1)}, bf16[1536,512]{1,0:T(8,128)(2,1)}, bf16[1536,512]{1,0:T(8,128)(2,1)}, bf16[1024,512]{1,0:T(8,128)(2,1)}, b...) custom-call(bf16[1536,1024]{1,0:T(8,128)(2,1)} %get-tuple-element.172.q, ...), custom_call_target="tpu_custom_call" | custom-call | flops 1000 | bytes 1000 | tf_op jit(solution)/shard_map/pallas_call | solution.py:434
  343.7 29.1 %shard_map.177 = (bf16[1536,1024]{1,0:T(8,128)(2,1)}, bf16[1536,512]{1,0:T(8,128)(2,1)}, bf16[1536,512]{1,0:T(8,128)(2,1)}, bf16[1024,512]{1,0:T(8,128)(2,1)}, b...) custom-call(bf16[1536,1024]{1,0:T(8,128)(2,1)} %get-tuple-element.17, ...), custom_call_target="tpu_custom_call", output_to_operand_aliasing={{0}: (23, {}), {1}: (24, {}), {2}: (25, {}), {3}: (26, {}),... | custom-call | flops 1000 | bytes 1000 | tf_op jit(solution)/shard_map/pallas_call | solution.py:434
  387.2 28.8 %shard_map.178 = (bf16[1536,1024]{1,0:T(8,128)(2,1)}, bf16[1536,512]{1,0:T(8,128)(2,1)}, bf16[1536,512]{1,0:T(8,128)(2,1)}, bf16[1024,512]{1,0:T(8,128)(2,1)}, b...) custom-call(bf16[1536,1024]{1,0:T(8,128)(2,1)} %get-tuple-element.17, ...), custom_call_target="tpu_custom_call", output_to_operand_aliasing={{0}: (23, {}), {1}: (24, {}), {2}: (25, {}), {3}: (26, {}),... | custom-call | flops 1000 | bytes 1000 | tf_op jit(solution)/shard_map/pallas_call | solution.py:434
  425.6 28.8 %shard_map.179 = (bf16[1536,1024]{1,0:T(8,128)(2,1)}, bf16[1536,512]{1,0:T(8,128)(2,1)}, bf16[1536,512]{1,0:T(8,128)(2,1)}, bf16[1024,512]{1,0:T(8,128)(2,1)}, b...) custom-call(bf16[1536,1024]{1,0:T(8,128)(2,1)} %get-tuple-element.17, ...), custom_call_target="tpu_custom_call", output_to_operand_aliasing={{0}: (23, {}), {1}: (24, {}), {2}: (25, {}), {3}: (26, {}),... | custom-call | flops 1000 | bytes 1000 | tf_op jit(solution)/shard_map/pallas_call | solution.py:434
  454.4 5.9 convolution_convert_fusion.4
  470.7 11.8 %shard_map.181 = (bf16[1536,1024]{1,0:T(8,128)(2,1)}, f32[8,1024]{1,0:T(8,128)S(1)}) custom-call(bf16[1536,1024]{1,0:T(8,128)(2,1)} %get-tuple-element.252.refs_0_, bf16[1536,512]{1,0:T(8,128)(2,1)} %get-tuple-element.268.refs_1_, bf16[1536,512]{1,0:T(8,128)(2,1)} %get-tuple-element.258.refs_2_, bf16[1024,1024]{1,0:T(8,128)(2,1)} %shard_map.161.refs_4_.refs_3_, ...), custom_call_target="tpu_custom_call" | custom-call | flops 1000 | bytes 1000 | tf_op jit(solution)/shard_map/pallas_call | solution.py:1022
  487.3 6.5 shard_map.180
  499.9 26.4 %collective-permute-done.29 = bf16[2880,128]{1,0:T(8,128)(2,1)S(1)} collective-permute-done((bf16[2880,128]{1,0:T(8,128)(2,1)S(1)}, bf16[2880,128]{1,0:T(8,128)(2,1)S(1)}, u32[]{:S(2)}, u32[]{:S(2)}) %collective-permute-start.29) | collective-permute-done | bytes 737312 | tf_op jit(solution)/shard_map/ppermute | solution.py:59
  532.0 8.6 %collective-permute-done.31 = bf16[2048,128]{1,0:T(8,128)(2,1)S(1)} collective-permute-done((bf16[2048,128]{1,0:T(8,128)(2,1)S(1)}, bf16[2048,128]{1,0:T(8,128)(2,1)S(1)}, u32[]{:S(2)}, u32[]{:S(2)}) %collective-permute-start.31) | collective-permute-done | bytes 524320 | tf_op jit(solution)/shard_map/ppermute | solution.py:708
  542.3 3.5 all-to-all-start.1
  546.2 11.9 %all-to-all-done.1.who = bf16[4,960,128]{2,1,0:T(8,128)(2,1)S(1)} async-done(((bf16[4,960,128]{2,1,0:T(8,128)(2,1)}), bf16[4,960,128]{2,1,0:T(8,128)(2,1)S(1)}, u32[]{:S(2)}, u32[]{:S(2)}) %all-to-all-start.1) | async-done | bytes 983072 | tf_op jit(solution)/shard_map/all_to_all | solution.py:927
  558.9 3.3 all-to-all-start
  569.5 3.0 shard_map.182.flat
  577.8 4.8 collective-permute-done.33
  588.6 9.6 %collective-permute-done.36 = bf16[1024,128]{1,0:T(8,128)(2,1)S(1)} collective-permute-done((bf16[1024,128]{1,0:T(8,128)(2,1)S(1)}, bf16[1024,128]{1,0:T(8,128)(2,1)S(1)}, u32[]{:S(2)}, u32[]{:S(2)}) %collective-permute-start.36) | collective-permute-done | bytes 262176 | tf_op jit(solution)/shard_map/ppermute | solution.py:59
  598.6 5.9 collective-permute-done.37
  608.7 3.5 collective-permute-start.39
  614.8 4.4 collective-permute-done.39
  619.2 10.4 %collective-permute-done.40 = bf16[1312,128]{1,0:T(8,128)(2,1)S(1)} collective-permute-done((bf16[1312,128]{1,0:T(8,128)(2,1)S(1)}, bf16[1312,128]{1,0:T(8,128)(2,1)S(1)}, u32[]{:S(2)}, u32[]{:S(2)}) %collective-permute-start.40) | collective-permute-done | bytes 335904 | tf_op jit(solution)/shard_map/ppermute | solution.py:964
  634.3 16.3 %shard_map.183 = (f32[3872,128]{1,0:T(8,128)}, f32[3872,128]{1,0:T(8,128)}, f32[3872,128]{1,0:T(8,128)}, bf16[3872,128]{1,0:T(8,128)(2,1)}) custom-call(s32[6]{0:T(128)S(1)} %stack.143.info, bf16[4,1312,128]{2,1,0:T(8,128)(2,1)} %pad_maximum_fusion.10.who, bf16[4,1312,128]{2,1,0:T(8,128)(2,1)} %collective-permute-done.42.other, ...), custom_call_target="tpu_custom_call" | custom-call | flops 1000 | bytes 1000 | tf_op jit(solution)/shard_map/pallas_call | solution.py:904
  650.6 15.7 %collective-permute-done.43 = bf16[384,1024]{1,0:T(8,128)(2,1)} collective-permute-done((bf16[384,1024]{1,0:T(8,128)(2,1)}, bf16[384,1024]{1,0:T(8,128)(2,1)}, u32[]{:S(2)}, u32[]{:S(2)}) %collective-permute-start.43) | collective-permute-done | bytes 786464 | tf_op jit(solution)/shard_map/ppermute | solution.py:59
  679.7 62.5 %all-gather.3.cloned.1.call-done = bf16[30976,128]{1,0:T(8,128)(2,1)} async-done(((bf16[3872,128]{1,0:T(8,128)(2,1)}), bf16[30976,128]{1,0:T(8,128)(2,1)}) %all-gather.3.cloned.1.call-update) | async-done | bytes 7929872 | tf_op jit(solution)/shard_map/all_gather | solution.py:984
  742.2 3.7 slice.445
  748.0 5.7 maximum_bitcast_fusion
  (471 shorter events, 188.4 us)
Async XLA Ops:
  10.9 38.7 %collective-permute-start.1 = (bf16[384,1024]{1,0:T(8,128)(2,1)}, bf16[384,1024]{1,0:T(8,128)(2,1)}, u32[]{:S(2)}, u32[]{:S(2)}) collective-permute-start(bf16[384,1024]{1,0:T(8,128)(2,1)} %get-tuple-element.364), channel_id=1, source_target_pairs={{0,4},{1,5},{2,6},{3,7},{4,0},{5,1},{6,2},{7,3},{8,12},{9,13},{10,... | collective-permute-start | bytes 2359304 | tf_op jit(solution)/shard_map/ppermute | solution.py:59
  14.9 53.3 %collective-permute-start = (bf16[384,1024]{1,0:T(8,128)(2,1)}, bf16[384,1024]{1,0:T(8,128)(2,1)}, u32[]{:S(2)}, u32[]{:S(2)}) collective-permute-start(bf16[384,1024]{1,0:T(8,128)(2,1)} %get-tuple-element.365), channel_id=1, source_target_pairs={{0,1},{1,0},{2,3},{3,2},{4,5},{5,4},{6,7},{7,6},{8,9},{9,8},{10,11... | collective-permute-start | bytes 2359304 | tf_op jit(solution)/shard_map/ppermute | solution.py:59
  15.7 52.2 %collective-permute-start.3 = (bf16[1,256,1024]{2,1,0:T(8,128)(2,1)}, bf16[1,256,1024]{2,1,0:T(8,128)(2,1)S(1)}, u32[]{:S(2)}, u32[]{:S(2)}) collective-permute-start(bf16[1,256,1024]{2,1,0:T(8,128)(2,1)} %constant_dynamic-slice_fusion), channel_id=1, source_target_pairs={{0,2},{1,3},{2,0},{3,1},{4,6},{5,7},{6,4},{7,5},{8,10},{9,11},{10,... | collective-permute-start | bytes 1572872 | tf_op jit(solution)/shard_map/ppermute | solution.py:59
  24.6 46.6 %copy-start.2 = (f32[1536,128]{1,0:T(8,128)}, f32[1536,128]{1,0:T(8,128)S(1)}, u32[]{:S(2)}) copy-start(f32[1536,128]{1,0:T(8,128)S(1)} %pad_maximum_fusion.15.refs_2_.cos_q.cos_o) | copy-start | bytes 2359300
  66.1 3.6 collective-permute-start.2
  67.2 19.9 %collective-permute-start.5 = (bf16[1,256,1024]{2,1,0:T(8,128)(2,1)S(1)}, bf16[1,256,1024]{2,1,0:T(8,128)(2,1)S(1)}, u32[]{:S(2)}, u32[]{:S(2)}) collective-permute-start(bf16[1,256,1024]{2,1,0:T(8,128)(2,1)S(1)} %slice_bitcast_fusion.1), channel_id=1, source_target_pairs={{0,2},{1,3},{2,0},{3,1},{4,6},{5,7},{6,4},{7,5},{8,10},{9,11},{10,... | collective-permute-start | bytes 1572872 | tf_op jit(solution)/shard_map/ppermute | solution.py:59
  68.0 21.2 %collective-permute-start.4 = (bf16[1,256,1024]{2,1,0:T(8,128)(2,1)S(1)}, bf16[1,256,1024]{2,1,0:T(8,128)(2,1)}, u32[]{:S(2)}, u32[]{:S(2)}) collective-permute-start(bf16[1,256,1024]{2,1,0:T(8,128)(2,1)S(1)} %collective-permute-done.3), channel_id=1, source_target_pairs={{0,1},{1,0},{2,3},{3,2},{4,5},{5,4},{6,7},{7,6},{8,9},{9,8},{10,11... | collective-permute-start | bytes 1572872 | tf_op jit(solution)/shard_map/ppermute | solution.py:59
  87.1 17.1 %collective-permute-start.6 = (bf16[1,256,1024]{2,1,0:T(8,128)(2,1)S(1)}, bf16[1,256,1024]{2,1,0:T(8,128)(2,1)}, u32[]{:S(2)}, u32[]{:S(2)}) collective-permute-start(bf16[1,256,1024]{2,1,0:T(8,128)(2,1)S(1)} %collective-permute-done.5), channel_id=1, source_target_pairs={{0,1},{1,0},{2,3},{3,2},{4,5},{5,4},{6,7},{7,6},{8,9},{9,8},{10,11... | collective-permute-start | bytes 1572872 | tf_op jit(solution)/shard_map/ppermute | solution.py:59
  100.8 49.9 %collective-permute-start.7 = (bf16[384,1024]{1,0:T(8,128)(2,1)S(1)}, bf16[384,1024]{1,0:T(8,128)(2,1)}, u32[]{:S(2)}, u32[]{:S(2)}) collective-permute-start(bf16[384,1024]{1,0:T(8,128)(2,1)S(1)} %copy-done.71), channel_id=1, source_target_pairs={{0,4},{1,5},{2,6},{3,7},{4,0},{5,1},{6,2},{7,3},{8,12},{9,13},{10,... | collective-permute-start | bytes 2359304 | tf_op jit(solution)/shard_map/ppermute | solution.py:59
  150.8 22.5 %collective-permute-start.8 = (bf16[384,1024]{1,0:T(8,128)(2,1)}, bf16[384,1024]{1,0:T(8,128)(2,1)}, u32[]{:S(2)}, u32[]{:S(2)}) collective-permute-start(bf16[384,1024]{1,0:T(8,128)(2,1)} %collective-permute-done.7), channel_id=1, source_target_pairs={{0,1},{1,0},{2,3},{3,2},{4,5},{5,4},{6,7},{7,6},{8,9},{9,8},{10,11... | collective-permute-start | bytes 2359304 | tf_op jit(solution)/shard_map/ppermute | solution.py:59
  151.2 26.8 %collective-permute-start.12 = (bf16[384,1024]{1,0:T(8,128)(2,1)S(1)}, bf16[384,1024]{1,0:T(8,128)(2,1)}, u32[]{:S(2)}, u32[]{:S(2)}) collective-permute-start(bf16[384,1024]{1,0:T(8,128)(2,1)S(1)} %copy-done.42), channel_id=1, source_target_pairs={{0,1},{1,0},{2,3},{3,2},{4,5},{5,4},{6,7},{7,6},{8,9},{9,8},{10,11... | collective-permute-start | bytes 2359304 | tf_op jit(solution)/shard_map/ppermute | solution.py:59
  174.7 39.9 %collective-permute-start.10 = (bf16[1536,1024]{1,0:T(8,128)(2,1)S(1)}, bf16[1536,1024]{1,0:T(8,128)(2,1)}, u32[]{:S(2)}, u32[]{:S(2)}) collective-permute-start(bf16[1536,1024]{1,0:T(8,128)(2,1)S(1)} %constant_dynamic-update-slice_fusion.5.o), channel_id=1, source_target_pairs={{0,1},{1,0},{2,3},{3,2},{4,5},{5,4},{6,7},{7,6},{8,9},{9,8},{10,11... | collective-permute-start | bytes 9437192 | tf_op jit(solution)/shard_map/ppermute | solution.py:59
  177.9 5.5 collective-permute-start.11
  181.3 33.2 %collective-permute-start.9 = (bf16[512,1024]{1,0:T(8,128)(2,1)S(1)}, bf16[512,1024]{1,0:T(8,128)(2,1)S(1)}, u32[]{:S(2)}, u32[]{:S(2)}) collective-permute-start(bf16[512,1024]{1,0:T(8,128)(2,1)S(1)} %convolution_convert_fusion.8.part), channel_id=1, source_target_pairs={{0,1},{1,0},{2,3},{3,2},{4,5},{5,4},{6,7},{7,6},{8,9},{9,8},{10,11... | collective-permute-start | bytes 3145736 | tf_op jit(solution)/shard_map/ppermute | solution.py:59
  232.7 32.3 %collective-permute-start.13 = (bf16[1536,1536]{1,0:T(8,128)(2,1)}, bf16[1536,1536]{1,0:T(8,128)(2,1)}, u32[]{:S(2)}, u32[]{:S(2)}) collective-permute-start(bf16[1536,1536]{1,0:T(8,128)(2,1)} %get-tuple-element.190), channel_id=1, source_target_pairs={{0,1},{1,0},{2,3},{3,2},{4,5},{5,4},{6,7},{7,6},{8,9},{9,8},{10,11... | collective-permute-start | bytes 14155784 | tf_op jit(solution)/shard_map/ppermute | solution.py:59
  239.4 18.5 %collective-permute-start.15 = (bf16[1024,1024]{1,0:T(8,128)(2,1)S(1)}, bf16[1024,1024]{1,0:T(8,128)(2,1)S(1)}, u32[]{:S(2)}, u32[]{:S(2)}) collective-permute-start(bf16[1024,1024]{1,0:T(8,128)(2,1)S(1)} %copy-done.50), channel_id=1, source_target_pairs={{0,1},{1,0},{2,3},{3,2},{4,5},{5,4},{6,7},{7,6},{8,9},{9,8},{10,11... | collective-permute-start | bytes 6291464 | tf_op jit(solution)/shard_map/ppermute | solution.py:59
  241.5 23.5 %collective-permute-start.14 = (bf16[768,1024]{1,0:T(8,128)(2,1)S(1)}, bf16[768,1024]{1,0:T(8,128)(2,1)S(1)}, u32[]{:S(2)}, u32[]{:S(2)}) collective-permute-start(bf16[768,1024]{1,0:T(8,128)(2,1)S(1)} %pad_maximum_fusion.6), channel_id=1, source_target_pairs={{0,1},{1,0},{2,3},{3,2},{4,5},{5,4},{6,7},{7,6},{8,9},{9,8},{10,11... | collective-permute-start | bytes 4718600 | tf_op jit(solution)/shard_map/ppermute | solution.py:59
  252.2 5.7 collective-permute-start.16
  261.9 37.2 %collective-permute-start.18 = (bf16[1024,768]{1,0:T(8,128)(2,1)}, bf16[1024,768]{1,0:T(8,128)(2,1)}, u32[]{:S(2)}, u32[]{:S(2)}) collective-permute-start(bf16[1024,768]{1,0:T(8,128)(2,1)} %get-tuple-element.324), channel_id=1, source_target_pairs={{0,16},{8,24},{16,0},{24,8},{1,17},{9,25},{17,1},{25,9},{2,18},{10... | collective-permute-start | bytes 4718600 | tf_op jit(solution)/shard_map/ppermute | solution.py:708
  263.4 36.6 %collective-permute-start.17 = (bf16[1024,768]{1,0:T(8,128)(2,1)}, bf16[1024,768]{1,0:T(8,128)(2,1)}, u32[]{:S(2)}, u32[]{:S(2)}) collective-permute-start(bf16[1024,768]{1,0:T(8,128)(2,1)} %get-tuple-element.326), channel_id=1, source_target_pairs={{0,8},{8,0},{16,24},{24,16},{1,9},{9,1},{17,25},{25,17},{2,10},{10... | collective-permute-start | bytes 4718600 | tf_op jit(solution)/shard_map/ppermute | solution.py:708
  300.1 72.7 %collective-permute-start.19 = (bf16[3072,256]{1,0:T(8,128)(2,1)}, bf16[3072,256]{1,0:T(8,128)(2,1)}, u32[]{:S(2)}, u32[]{:S(2)}) collective-permute-start(bf16[3072,256]{1,0:T(8,128)(2,1)} %get-tuple-element.322), channel_id=1, source_target_pairs={{0,8},{8,0},{16,24},{24,16},{1,9},{9,1},{17,25},{25,17},{2,10},{10... | collective-permute-start | bytes 4718600 | tf_op jit(solution)/shard_map/ppermute | solution.py:708
  304.9 67.9 %collective-permute-start.22 = (bf16[1024,384]{1,0:T(8,128)(2,1)}, bf16[1024,384]{1,0:T(8,128)(2,1)}, u32[]{:S(2)}, u32[]{:S(2)}) collective-permute-start(bf16[1024,384]{1,0:T(8,128)(2,1)} %get-tuple-element.350), channel_id=1, source_target_pairs={{0,8},{8,0},{16,24},{24,16},{1,9},{9,1},{17,25},{25,17},{2,10},{10... | collective-permute-start | bytes 2359304 | tf_op jit(solution)/shard_map/ppermute | solution.py:708
  305.4 67.4 %collective-permute-start.21 = (bf16[2048,256]{1,0:T(8,128)(2,1)}, bf16[2048,256]{1,0:T(8,128)(2,1)}, u32[]{:S(2)}, u32[]{:S(2)}) collective-permute-start(bf16[2048,256]{1,0:T(8,128)(2,1)} %get-tuple-element.344), channel_id=1, source_target_pairs={{0,16},{8,24},{16,0},{24,8},{1,17},{9,25},{17,1},{25,9},{2,18},{10... | collective-permute-start | bytes 3145736 | tf_op jit(solution)/shard_map/ppermute | solution.py:708
  309.2 63.6 %collective-permute-start.20 = (bf16[1024,384]{1,0:T(8,128)(2,1)}, bf16[1024,384]{1,0:T(8,128)(2,1)}, u32[]{:S(2)}, u32[]{:S(2)}) collective-permute-start(bf16[1024,384]{1,0:T(8,128)(2,1)} %get-tuple-element.352), channel_id=1, source_target_pairs={{0,16},{8,24},{16,0},{24,8},{1,17},{9,25},{17,1},{25,9},{2,18},{10... | collective-permute-start | bytes 2359304 | tf_op jit(solution)/shard_map/ppermute | solution.py:708
  374.6 41.5 %collective-permute-start.25 = (bf16[2048,128]{1,0:T(8,128)(2,1)S(1)}, bf16[2048,128]{1,0:T(8,128)(2,1)S(1)}, u32[]{:S(2)}, u32[]{:S(2)}) collective-permute-start(bf16[2048,128]{1,0:T(8,128)(2,1)S(1)} %get-tuple-element.374), channel_id=1, source_target_pairs={{0,8},{8,0},{16,24},{24,16},{1,9},{9,1},{17,25},{25,17},{2,10},{10... | collective-permute-start | bytes 1572872 | tf_op jit(solution)/shard_map/ppermute | solution.py:708
  379.0 37.0 %collective-permute-start.24 = (bf16[3072,128]{1,0:T(8,128)(2,1)S(1)}, bf16[3072,128]{1,0:T(8,128)(2,1)S(1)}, u32[]{:S(2)}, u32[]{:S(2)}) collective-permute-start(bf16[3072,128]{1,0:T(8,128)(2,1)S(1)} %get-tuple-element.348), channel_id=1, source_target_pairs={{0,16},{8,24},{16,0},{24,8},{1,17},{9,25},{17,1},{25,9},{2,18},{10... | collective-permute-start | bytes 2359304 | tf_op jit(solution)/shard_map/ppermute | solution.py:708
  385.6 39.1 %collective-permute-start.23 = (bf16[384,1024]{1,0:T(8,128)(2,1)}, bf16[384,1024]{1,0:T(8,128)(2,1)S(1)}, u32[]{:S(2)}, u32[]{:S(2)}) collective-permute-start(bf16[384,1024]{1,0:T(8,128)(2,1)} %pad_maximum_fusion.17), channel_id=1, source_target_pairs={{0,4},{1,5},{2,6},{3,7},{4,0},{5,1},{6,2},{7,3},{8,12},{9,13},{10,... | collective-permute-start | bytes 2359304 | tf_op jit(solution)/shard_map/ppermute | solution.py:59
  420.0 40.3 %collective-permute-start.26 = (bf16[2,2880,128]{2,1,0:T(8,128)(2,1)S(1)}, bf16[2,2880,128]{2,1,0:T(8,128)(2,1)S(1)}, u32[]{:S(2)}, u32[]{:S(2)}) collective-permute-start(bf16[2,2880,128]{2,1,0:T(8,128)(2,1)S(1)} %get-tuple-element.334), channel_id=1, source_target_pairs={{0,2},{1,3},{2,0},{3,1},{4,6},{5,7},{6,4},{7,5},{8,10},{9,11},{10,... | collective-permute-start | bytes 4423688 | tf_op jit(solution)/shard_map/ppermute | solution.py:59
  493.8 32.5 %collective-permute-start.29 = (bf16[2880,128]{1,0:T(8,128)(2,1)S(1)}, bf16[2880,128]{1,0:T(8,128)(2,1)S(1)}, u32[]{:S(2)}, u32[]{:S(2)}) collective-permute-start(bf16[2880,128]{1,0:T(8,128)(2,1)S(1)} %get-tuple-element.366), channel_id=1, source_target_pairs={{0,4},{1,5},{2,6},{3,7},{4,0},{5,1},{6,2},{7,3},{8,12},{9,13},{10,... | collective-permute-start | bytes 2211848 | tf_op jit(solution)/shard_map/ppermute | solution.py:59
  496.4 29.9 %collective-permute-start.28 = (bf16[2048,256]{1,0:T(8,128)(2,1)S(1)}, bf16[2048,256]{1,0:T(8,128)(2,1)S(1)}, u32[]{:S(2)}, u32[]{:S(2)}) collective-permute-start(bf16[2048,256]{1,0:T(8,128)(2,1)S(1)} %get-tuple-element.340), channel_id=1, source_target_pairs={{0,16},{8,24},{16,0},{24,8},{1,17},{9,25},{17,1},{25,9},{2,18},{10... | collective-permute-start | bytes 3145736 | tf_op jit(solution)/shard_map/ppermute | solution.py:708
  497.7 28.5 %collective-permute-start.27 = (bf16[1024,512]{1,0:T(8,128)(2,1)S(1)}, bf16[1024,512]{1,0:T(8,128)(2,1)S(1)}, u32[]{:S(2)}, u32[]{:S(2)}) collective-permute-start(bf16[1024,512]{1,0:T(8,128)(2,1)S(1)} %get-tuple-element.342), channel_id=1, source_target_pairs={{0,8},{8,0},{16,24},{24,16},{1,9},{9,1},{17,25},{25,17},{2,10},{10... | collective-permute-start | bytes 3145736 | tf_op jit(solution)/shard_map/ppermute | solution.py:708
  499.7 29.4 %collective-permute-start.32 = (bf16[1280,1024]{1,0:T(8,128)(2,1)S(1)}, bf16[1280,1024]{1,0:T(8,128)(2,1)S(1)}, u32[]{:S(2)}, u32[]{:S(2)}) collective-permute-start(bf16[1280,1024]{1,0:T(8,128)(2,1)S(1)} %pad_maximum_fusion.4), channel_id=1, source_target_pairs={{0,1},{1,0},{2,3},{3,2},{4,5},{5,4},{6,7},{7,6},{8,9},{9,8},{10,11... | collective-permute-start | bytes 7864328 | tf_op jit(solution)/shard_map/ppermute | solution.py:59
  526.7 13.9 %collective-permute-start.31 = (bf16[2048,128]{1,0:T(8,128)(2,1)S(1)}, bf16[2048,128]{1,0:T(8,128)(2,1)S(1)}, u32[]{:S(2)}, u32[]{:S(2)}) collective-permute-start(bf16[2048,128]{1,0:T(8,128)(2,1)S(1)} %get-tuple-element.370), channel_id=1, source_target_pairs={{0,8},{8,0},{16,24},{24,16},{1,9},{9,1},{17,25},{25,17},{2,10},{10... | collective-permute-start | bytes 1572872 | tf_op jit(solution)/shard_map/ppermute | solution.py:708
  527.6 13.6 %collective-permute-start.30 = (bf16[1024,256]{1,0:T(8,128)(2,1)S(1)}, bf16[1024,256]{1,0:T(8,128)(2,1)S(1)}, u32[]{:S(2)}, u32[]{:S(2)}) collective-permute-start(bf16[1024,256]{1,0:T(8,128)(2,1)S(1)} %get-tuple-element.372), channel_id=1, source_target_pairs={{0,16},{8,24},{16,0},{24,8},{1,17},{9,25},{17,1},{25,9},{2,18},{10... | collective-permute-start | bytes 1572872 | tf_op jit(solution)/shard_map/ppermute | solution.py:708
  532.0 54.4 %collective-permute-start.38 = (bf16[1,512,1024]{2,1,0:T(8,128)(2,1)}, bf16[1,512,1024]{2,1,0:T(8,128)(2,1)}, u32[]{:S(2)}, u32[]{:S(2)}) collective-permute-start(bf16[1,512,1024]{2,1,0:T(8,128)(2,1)} %fusion.37), channel_id=1, source_target_pairs={{0,2},{1,3},{2,0},{3,1},{4,6},{5,7},{6,4},{7,5},{8,10},{9,11},{10,... | collective-permute-start | bytes 3145736 | tf_op jit(solution)/shard_map/ppermute | solution.py:59
  542.3 15.8 %all-to-all-start.1 = ((bf16[4,960,128]{2,1,0:T(8,128)(2,1)}), bf16[4,960,128]{2,1,0:T(8,128)(2,1)S(1)}, u32[]{:S(2)}, u32[]{:S(2)}) async-start(bf16[4,960,128]{2,1,0:T(8,128)(2,1)} %pad_maximum_fusion.14), calls=%async_computation.1 | async-start | bytes 1966080 | tf_op jit(solution)/shard_map/all_to_all | solution.py:927
  558.9 18.9 %all-to-all-start = ((f32[32,18,128]{2,1,0:T(8,128)}), f32[32,18,128]{2,1,0:T(8,128)}, u32[]{:S(2)}, u32[]{:S(2)}) async-start(f32[32,18,128]{2,1,0:T(8,128)} %broadcast_in_dim.59), calls=%async_computation | async-start | bytes 786432 | tf_op jit(solution)/shard_map/all_to_all | solution.py:922
  562.2 180.0 %all-gather.3.cloned.1.call-start = ((), (), s32[]{:S(2)}) async-start(), calls=%async_computation.2 | async-start | bytes 8921088 | tf_op jit(solution)/shard_map/all_gather | solution.py:984
  562.2 7.2 collective-permute-start.34
  563.6 18.9 %collective-permute-start.33 = (bf16[2,1024,128]{2,1,0:T(8,128)(2,1)}, bf16[2,1024,128]{2,1,0:T(8,128)(2,1)}, u32[]{:S(2)}, u32[]{:S(2)}) collective-permute-start(bf16[2,1024,128]{2,1,0:T(8,128)(2,1)} %get-tuple-element.368), channel_id=1, source_target_pairs={{0,2},{1,3},{2,0},{3,1},{4,6},{5,7},{6,4},{7,5},{8,10},{9,11},{10,... | collective-permute-start | bytes 1572872 | tf_op jit(solution)/shard_map/ppermute | solution.py:59
  573.1 9.4 %collective-permute-start.35 = (f32[16,128]{1,0:T(8,128)S(1)}, f32[16,128]{1,0:T(8,128)S(1)}, u32[]{:S(2)}, u32[]{:S(2)}) collective-permute-start(f32[16,128]{1,0:T(8,128)S(1)} %slice.427), channel_id=1, source_target_pairs={{0,2},{1,3},{2,4},{3,5},{4,6},{5,7},{6,8},{7,9},{8,10},{9,11},{10,... | collective-permute-start | bytes 24584 | tf_op jit(solution)/shard_map/ppermute | solution.py:948
  583.8 14.4 %collective-permute-start.36 = (bf16[1024,128]{1,0:T(8,128)(2,1)S(1)}, bf16[1024,128]{1,0:T(8,128)(2,1)S(1)}, u32[]{:S(2)}, u32[]{:S(2)}) collective-permute-start(bf16[1024,128]{1,0:T(8,128)(2,1)S(1)} %dynamic-slice_bitcast_fusion.11), channel_id=1, source_target_pairs={{0,4},{1,5},{2,6},{3,7},{4,0},{5,1},{6,2},{7,3},{8,12},{9,13},{10,... | collective-permute-start | bytes 786440 | tf_op jit(solution)/shard_map/ppermute | solution.py:59
  598.3 6.2 collective-permute-start.37
  608.7 10.5 %collective-permute-start.39 = (bf16[1312,128]{1,0:T(8,128)(2,1)S(1)}, bf16[1312,128]{1,0:T(8,128)(2,1)S(1)}, u32[]{:S(2)}, u32[]{:S(2)}) collective-permute-start(bf16[1312,128]{1,0:T(8,128)(2,1)S(1)} %pad_maximum_fusion.21), channel_id=1, source_target_pairs={{0,8},{1,9},{8,0},{9,1},{10,2},{11,3},{12,4},{13,5},{14,6},{15,7}} | collective-permute-start | bytes 1007624 | tf_op jit(solution)/shard_map/ppermute | solution.py:964
  612.2 17.5 %collective-permute-start.40 = (bf16[1312,128]{1,0:T(8,128)(2,1)S(1)}, bf16[1312,128]{1,0:T(8,128)(2,1)S(1)}, u32[]{:S(2)}, u32[]{:S(2)}) collective-permute-start(bf16[1312,128]{1,0:T(8,128)(2,1)S(1)} %pad_maximum_fusion.21), channel_id=1, source_target_pairs={{16,0},{17,1},{18,2},{19,3},{20,4},{21,5},{22,6},{23,7},{24,8},{25... | collective-permute-start | bytes 1007624 | tf_op jit(solution)/shard_map/ppermute | solution.py:964
  613.5 16.2 %collective-permute-start.41 = (bf16[1312,128]{1,0:T(8,128)(2,1)S(1)}, bf16[1312,128]{1,0:T(8,128)(2,1)S(1)}, u32[]{:S(2)}, u32[]{:S(2)}) collective-permute-start(bf16[1312,128]{1,0:T(8,128)(2,1)S(1)} %pad_maximum_fusion.21), channel_id=1, source_target_pairs={{16,8},{17,9},{24,0},{25,1},{26,2},{27,3},{28,4},{29,5},{30,6},{31... | collective-permute-start | bytes 1007624 | tf_op jit(solution)/shard_map/ppermute | solution.py:964
  630.9 3.4 collective-permute-start.42
  631.9 34.5 %collective-permute-start.43 = (bf16[384,1024]{1,0:T(8,128)(2,1)}, bf16[384,1024]{1,0:T(8,128)(2,1)}, u32[]{:S(2)}, u32[]{:S(2)}) collective-permute-start(bf16[384,1024]{1,0:T(8,128)(2,1)} %pad_maximum_fusion.18), channel_id=1, source_target_pairs={{0,4},{1,5},{2,6},{3,7},{4,0},{5,1},{6,2},{7,3},{8,12},{9,13},{10,... | collective-permute-start | bytes 2359304 | tf_op jit(solution)/shard_map/ppermute | solution.py:59
  (84 other events, 532.3 us)
Sparse Core Ops, SparseCore 0:
  666.5 75.7 all-gather.2
